TPU v7x, 128 devices: a whole 4x4x4 slice. The times are simulated.
128 devices in a mesh: section: 2 (over core), dp: 16 (over z, y), tensor: 4 (over x).
Axes of the slice: x: 4, y: 4, z: 4, core: 2. Of those that a mesh axis runs over, the one named last changes fastest.
Arguments:
- tokens_in: bfloat16 [2, 8192, 1024], P(None, ('dp', 'tensor')), may hold values from -6 to 6
- cotangent: bfloat16 [2, 8192, 1024], P(None, ('dp', 'tensor')), may hold values from -6 to 6
- seq_lengths: int32 [2, 16], P(None, 'dp'), may hold values from 64 to 512, as said below
- gain_in: float32 [2, 1024], P('section'), may hold values from 0.5 to 1.5
- weight_x: bfloat16 [2, 1024, 2048], P('section', 'dp', 'tensor'), may hold values from -0.1875 to 0.1875
- weight_z: bfloat16 [2, 1024, 2048], P('section', 'dp', 'tensor'), may hold values from -0.1875 to 0.1875
- weight_bc: bfloat16 [2, 1024, 256], P('section', 'dp', 'tensor'), may hold values from -0.1875 to 0.1875
- weight_dt: bfloat16 [2, 1024, 32], P('section', 'dp', 'tensor'), may hold values from -0.1875 to 0.1875
- conv_x: float32 [2, 4, 2048], P('section', None, 'tensor'), may hold values from -0.5 to 0.5
- conv_bc: float32 [2, 4, 256], P('section', None, 'tensor'), may hold values from -0.5 to 0.5
- bias_x: float32 [2, 2048], P('section', 'tensor'), may hold values from -0.5 to 0.5
- bias_bc: float32 [2, 256], P('section', 'tensor'), may hold values from -0.5 to 0.5
- dt_bias: float32 [2, 32], P('section', 'tensor'), may hold values from -6 to -2
- decay_log: float32 [2, 32], P('section', 'tensor'), may hold values from -1 to 1.5
- skip_gain: float32 [2, 32], P('section', 'tensor'), may hold values from 0.5 to 1.5
- gain_out: float32 [2, 2048], P('section', 'tensor'), may hold values from 0.5 to 1.5
- weight_out: bfloat16 [2, 2048, 1024], P('section', 'tensor', 'dp'), may hold values from -0.125 to 0.125
Outputs:
- layer_outputs: bfloat16 [2, 2, 8192, 1024], P('section', None, ('dp', 'tensor'))
- input_grads: float32 [2, 2, 8192, 1024], P('section', None, ('dp', 'tensor'))
- grad_gain_in: float32 [2, 1024], P('section')
- grad_weight_x: float32 [2, 1024, 2048], P('section', 'dp', 'tensor')
- grad_weight_z: float32 [2, 1024, 2048], P('section', 'dp', 'tensor')
- grad_weight_bc: float32 [2, 1024, 256], P('section', 'dp', 'tensor')
- grad_weight_dt: float32 [2, 1024, 32], P('section', 'dp', 'tensor')
- grad_conv_x: float32 [2, 4, 2048], P('section', None, 'tensor')
- grad_conv_bc: float32 [2, 4, 256], P('section', None, 'tensor')
- grad_bias_x: float32 [2, 2048], P('section', 'tensor')
- grad_bias_bc: float32 [2, 256], P('section', 'tensor')
- grad_dt_bias: float32 [2, 32], P('section', 'tensor')
- grad_decay_log: float32 [2, 32], P('section', 'tensor')
- grad_skip_gain: float32 [2, 32], P('section', 'tensor')
- grad_gain_out: float32 [2, 2048], P('section', 'tensor')
- grad_weight_out: float32 [2, 2048, 1024], P('section', 'tensor', 'dp')
Inputs may be any that keep to these rules, and one draw needn't show every extreme that they name: `seq_lengths`: in every data group one micro-batch, drawn from the seed, holds a sequence of exactly 512 tokens; every length is at least 64.
All inputs are finite; a program needn't handle non-finite values.
Results may differ from a plain program's by a relative error of at most 0.018.
Values may be sent and summed in bfloat16 or wider, within the bound.
A program may use at most 128 MiB of HBM per device.

v0:
```python
import jax
import jax.numpy as jnp
from jax import lax
from jax.sharding import PartitionSpec as P

INNER = 2048
SPAN = 256


epsilon = 1e-05
highest = lax.Precision.HIGHEST


def from_behind(value, axis, steps):
    count = lax.axis_size(axis)
    leading, last = (max(0, -steps), min(count, count - steps))
    return lax.ppermute(value, axis, [(source, source + steps) for source in range(leading, last)])


def causal_conv(signal, kernel):
    tap_count = kernel.shape[0]
    padded = jnp.pad(signal, ((tap_count - 1, 0), (0, 0)))
    running = jnp.zeros_like(signal)
    for offset in range(tap_count):
        running = running + kernel[offset][None, :] * padded[offset : offset + signal.shape[0]]
    return running


def conv_part(signal, kernel, offsets):
    return jax.nn.silu(causal_conv(signal, kernel) + offsets[None, :])


def scan_blocks(values, step_sizes, rates, inputs_b, inputs_c):
    length, head_count, head_dim = values.shape
    number = length // SPAN
    states = inputs_b.shape[1]
    grouped = (
        values.reshape(number, SPAN, head_count, head_dim),
        step_sizes.reshape(number, SPAN, head_count),
        inputs_b.reshape(number, SPAN, states),
        inputs_c.reshape(number, SPAN, states),
    )
    positions = jnp.arange(SPAN)
    causal = positions[:, None] >= positions[None, :]

    def block_step(carried, pieces):
        block_x, block_dt, block_b, block_c = pieces
        log_steps = block_dt * rates[None, :]
        totals = jnp.cumsum(log_steps, axis=0)
        across = totals.T
        log_gaps = across[:, :, None] - across[:, None, :]
        decays = jnp.where(causal[None], jnp.exp(jnp.where(causal[None], log_gaps, 0.0)), 0.0)
        intersection = jnp.dot(
            block_c, block_b.T, precision=highest, preferred_element_type=jnp.float32
        )
        mixing = decays * intersection[None] * block_dt.T[:, None, :]
        inside = jnp.einsum("hts,shp->thp", mixing, block_x, precision=highest)
        carried_in = (
            jnp.einsum("tn,hpn->thp", block_c, carried, precision=highest)
            * jnp.exp(totals)[:, :, None]
        )
        final_log = totals[-1]
        weights_tail = jnp.exp(final_log[None, :] - totals) * block_dt
        updated = jnp.exp(final_log)[:, None, None] * carried + jnp.einsum(
            "shp,sn->hpn", weights_tail[:, :, None] * block_x, block_b, precision=highest
        )
        return (updated, inside + carried_in)

    initial = jnp.zeros((head_count, head_dim, states), jnp.float32)
    _, outputs = lax.scan(jax.checkpoint(block_step), initial, grouped)
    return outputs.reshape(length, head_count, head_dim)


def mixer(proj_x, proj_z, proj_dt, both_bc, conv_x, bias_x, dt_bias, decay_log, skip_gain):
    head_count = dt_bias.shape[0]
    channels = proj_x.shape[1]
    head_dim = channels // head_count
    states = both_bc.shape[1] // 2
    signal = conv_part(proj_x, conv_x, bias_x)
    step_sizes = jax.nn.softplus(proj_dt + dt_bias[None, :])
    rates = -jnp.exp(decay_log)
    shaped = signal.reshape(signal.shape[0], head_count, head_dim)
    scanned = scan_blocks(shaped, step_sizes, rates, both_bc[:, :states], both_bc[:, states:])
    output = scanned + skip_gain[None, :, None] * shaped
    gated = output.reshape(signal.shape[0], channels) * jax.nn.silu(proj_z)
    return (gated, jnp.sum(gated * gated, axis=-1))


def body(
    tokens_in,
    cotangent,
    seq_lengths,
    gain_in,
    weight_x,
    weight_z,
    weight_bc,
    weight_dt,
    conv_x,
    conv_bc,
    bias_x,
    bias_bc,
    dt_bias,
    decay_log,
    skip_gain,
    gain_out,
    weight_out,
):
    dp_count = lax.axis_size("dp")
    section_pos = lax.axis_index("section")
    is_first = section_pos == 0
    tensor_pos = lax.axis_index("tensor")
    micro_count, rows_dev, model_width = tokens_in.shape
    lengths = seq_lengths[:, 0]
    norm_in = gain_in[0]
    kernel_x = conv_x[0]
    kernel_bc = conv_bc[0]
    offset_x = bias_x[0]
    offset_bc = bias_bc[0]
    dt_local = dt_bias[0]
    log_local = decay_log[0]
    skip_local = skip_gain[0]
    norm_out = gain_out[0]
    inner_local = weight_x.shape[2]
    bc_local = weight_bc.shape[2]
    heads_local = weight_dt.shape[2]
    joined_cols = 2 * inner_local + bc_local + heads_local
    split_at = (inner_local, 2 * inner_local, 2 * inner_local + bc_local)
    local_rows = tensor_pos * rows_dev + jnp.arange(rows_dev)

    def fetch_weights():
        gathered = (
            lax.all_gather(weight_x[0], "dp", axis=0, tiled=True),
            lax.all_gather(weight_z[0], "dp", axis=0, tiled=True),
            lax.all_gather(weight_bc[0], "dp", axis=0, tiled=True),
            lax.all_gather(weight_dt[0], "dp", axis=0, tiled=True),
            lax.all_gather(weight_out[0], "dp", axis=1, tiled=True),
        )
        joined = jnp.concatenate([gathered[0], gathered[1], gathered[2], gathered[3]], axis=1)
        return (joined, gathered[4])

    received = jnp.zeros((rows_dev, model_width), jnp.float32)
    outputs_low = jnp.zeros((micro_count, rows_dev, model_width), jnp.bfloat16)
    stored_steps = []
    for step_index in range(micro_count + 1):
        position = step_index - section_pos
        active = (position >= 0) & (position < micro_count)
        chosen = jnp.clip(position, 0, micro_count - 1)
        weights_now = fetch_weights()
        fresh = lax.dynamic_index_in_dim(tokens_in, chosen, 0, keepdims=False).astype(jnp.float32)
        stream = jnp.where(is_first, fresh, received)
        length = lax.dynamic_index_in_dim(lengths, chosen, 0, keepdims=False)
        forward_joined = weights_now[0]
        out_weight = weights_now[1]
        row_mask = (local_rows < length).astype(jnp.float32)
        scale_in = lax.rsqrt(jnp.mean(stream * stream, axis=-1, keepdims=True) + epsilon)
        normed = (stream * scale_in * norm_in[None, :]).astype(jnp.bfloat16)
        pieces = lax.all_gather(normed, "tensor", axis=0, tiled=True)
        product = jnp.dot(pieces, forward_joined, preferred_element_type=jnp.float32)
        proj_x, proj_z, proj_bc, proj_dt = jnp.split(product, split_at, axis=1)
        own_bc = conv_part(proj_bc, kernel_bc, offset_bc).astype(jnp.bfloat16)
        both_bc = lax.all_gather(own_bc, "tensor", axis=1, tiled=True)
        gated, squares = mixer(
            proj_x,
            proj_z,
            proj_dt,
            both_bc.astype(jnp.float32),
            kernel_x,
            offset_x,
            dt_local,
            log_local,
            skip_local,
        )
        totals = lax.psum(squares, "tensor")
        factor = lax.rsqrt(totals / INNER + epsilon)
        normed_out = (gated * factor[:, None] * norm_out[None, :]).astype(jnp.bfloat16)
        branch = lax.psum_scatter(
            jnp.dot(normed_out, out_weight, preferred_element_type=jnp.float32),
            "tensor",
            scatter_dimension=0,
            tiled=True,
        )
        result = row_mask[:, None] * (stream + branch)
        result, stored = (result, (stream, pieces, product, both_bc, totals, normed_out))
        result_low = result.astype(jnp.bfloat16)
        outputs_low = jnp.where(
            active, lax.dynamic_update_index_in_dim(outputs_low, result_low, chosen, 0), outputs_low
        )
        stored_steps.append(stored)
        if step_index < micro_count:
            received = from_behind(result_low, "section", 1).astype(jnp.float32)
    shards_big = (
        jnp.zeros((model_width // dp_count, joined_cols), jnp.float32),
        jnp.zeros((inner_local, model_width // dp_count), jnp.float32),
    )
    small_sums = (
        jnp.zeros_like(kernel_x),
        jnp.zeros_like(kernel_bc),
        jnp.zeros_like(offset_x),
        jnp.zeros_like(offset_bc),
        jnp.zeros_like(dt_local),
        jnp.zeros_like(log_local),
        jnp.zeros_like(skip_local),
        jnp.zeros_like(norm_out),
    )
    gain_sums = jnp.zeros_like(norm_in)
    back_grads = jnp.zeros((micro_count, rows_dev, model_width), jnp.float32)
    returned = jnp.zeros((rows_dev, model_width), jnp.float32)
    for step_index in range(micro_count + 1):
        position = step_index - (1 - section_pos)
        active = (position >= 0) & (position < micro_count)
        chosen = jnp.clip(position, 0, micro_count - 1)
        weights_now = fetch_weights()
        low_step = max(step_index - 1, 0)
        high_step = min(step_index + 1, micro_count)
        stored = jax.tree.map(
            lambda earlier, later: jnp.where(is_first, earlier, later),
            stored_steps[low_step],
            stored_steps[high_step],
        )
        fresh = lax.dynamic_index_in_dim(cotangent, chosen, 0, keepdims=False).astype(jnp.float32)
        upstream = jnp.where(is_first, returned, fresh)
        length = lax.dynamic_index_in_dim(lengths, chosen, 0, keepdims=False)
        backward_joined = weights_now[0]
        backward_out_weight = weights_now[1]
        (
            backward_stream,
            backward_whole_rows,
            backward_projected,
            backward_both_bc,
            backward_totals,
            backward_normed_out,
        ) = stored
        backward_row_mask = (local_rows < length).astype(jnp.float32)
        seeded = backward_row_mask[:, None] * upstream
        seeded_low = seeded.astype(jnp.bfloat16)
        take_pieces = lax.all_gather(seeded_low, "tensor", axis=0, tiled=True)
        take_product = jnp.einsum(
            "sd,kd->sk", take_pieces, backward_out_weight, preferred_element_type=jnp.float32
        )
        out_grad = jnp.einsum(
            "sk,sd->kd", backward_normed_out, take_pieces, preferred_element_type=jnp.float32
        )
        back_gated, out_grad = (take_product, out_grad)
        backward_proj_x, backward_proj_z, backward_proj_bc, backward_proj_dt = jnp.split(
            backward_projected, split_at, axis=1
        )
        (backward_gated, backward_squares), pull_mixer = jax.vjp(
            mixer,
            backward_proj_x,
            backward_proj_z,
            backward_proj_dt,
            backward_both_bc.astype(jnp.float32),
            kernel_x,
            offset_x,
            dt_local,
            log_local,
            skip_local,
        )
        backward_factor = lax.rsqrt(backward_totals / INNER + epsilon)
        grad_norm_out = jnp.sum(back_gated * backward_gated * backward_factor[:, None], axis=0)
        weighted = back_gated * norm_out[None, :]
        inner_sums = lax.psum(jnp.sum(weighted * backward_gated, axis=-1), "tensor")
        back_mix = (
            backward_factor[:, None] * weighted
            - backward_gated * (backward_factor**3 / INNER)[:, None] * inner_sums[:, None]
        )
        (
            back_x,
            back_z,
            back_dt,
            back_both,
            grad_kernel_x,
            grad_offset_x,
            backward_grad_dt,
            grad_log,
            grad_skip,
        ) = pull_mixer((back_mix, jnp.zeros_like(backward_squares)))
        own_back = lax.psum_scatter(back_both, "tensor", scatter_dimension=1, tiled=True)
        _, pull_conv = jax.vjp(conv_part, backward_proj_bc, kernel_bc, offset_bc)
        back_bc, grad_kernel_bc, grad_offset_bc = pull_conv(own_back)
        back_proj = jnp.concatenate([back_x, back_z, back_bc, back_dt], axis=1).astype(jnp.bfloat16)
        in_grad = jnp.einsum(
            "sd,sc->dc", backward_whole_rows, back_proj, preferred_element_type=jnp.float32
        )
        back_normed = lax.psum_scatter(
            jnp.einsum(
                "sc,dc->sd", back_proj, backward_joined, preferred_element_type=jnp.float32
            ).astype(jnp.bfloat16),
            "tensor",
            scatter_dimension=0,
            tiled=True,
        ).astype(jnp.float32)
        backward_scale_in = lax.rsqrt(
            jnp.mean(backward_stream * backward_stream, axis=-1, keepdims=True) + epsilon
        )
        grad_norm_in = jnp.sum(back_normed * backward_stream * backward_scale_in, axis=0)
        weighted_in = back_normed * norm_in[None, :]
        back_stream = (
            seeded
            + backward_scale_in * weighted_in
            - backward_stream
            * (backward_scale_in**3 / model_width)
            * jnp.sum(weighted_in * backward_stream, axis=-1, keepdims=True)
        )
        small_grads = (
            grad_kernel_x,
            grad_kernel_bc,
            grad_offset_x,
            grad_offset_bc,
            backward_grad_dt,
            grad_log,
            grad_skip,
            grad_norm_out,
        )
        back_stream, big_grads, small_grads, gain_part = (
            back_stream,
            (in_grad, out_grad),
            small_grads,
            grad_norm_in,
        )
        weight_on = active.astype(jnp.float32)
        big_grads = jax.tree.map(lambda member: member * weight_on, big_grads)
        shards_big = jax.tree.map(
            jnp.add,
            shards_big,
            (
                lax.psum_scatter(
                    big_grads[0].astype(jnp.bfloat16), "dp", scatter_dimension=0, tiled=True
                ).astype(jnp.float32),
                lax.psum_scatter(
                    big_grads[1].astype(jnp.bfloat16), "dp", scatter_dimension=1, tiled=True
                ).astype(jnp.float32),
            ),
        )
        small_sums = jax.tree.map(
            lambda running, member: running + member * weight_on, small_sums, small_grads
        )
        gain_sums = gain_sums + gain_part * weight_on
        back_grads = jnp.where(
            active, lax.dynamic_update_index_in_dim(back_grads, back_stream, chosen, 0), back_grads
        )
        if step_index < micro_count:
            returned = from_behind(back_stream.astype(jnp.bfloat16), "section", -1).astype(
                jnp.float32
            )
    small_total = lax.psum(small_sums, "dp")
    gain_total = lax.psum(gain_sums, ("dp", "tensor"))
    in_shard, out_shard = shards_big
    grad_x, grad_z, grad_bc, grad_dt = jnp.split(in_shard, split_at, axis=1)
    return (
        outputs_low[None],
        back_grads[None],
        gain_total[None],
        grad_x[None],
        grad_z[None],
        grad_bc[None],
        grad_dt[None],
        small_total[0][None],
        small_total[1][None],
        small_total[2][None],
        small_total[3][None],
        small_total[4][None],
        small_total[5][None],
        small_total[6][None],
        small_total[7][None],
        out_shard[None],
    )


def solution(mesh):
    in_specs = (
        P(None, ("dp", "tensor"), None),
        P(None, ("dp", "tensor"), None),
        P(None, "dp"),
        P("section", None),
        P("section", "dp", "tensor"),
        P("section", "dp", "tensor"),
        P("section", "dp", "tensor"),
        P("section", "dp", "tensor"),
        P("section", None, "tensor"),
        P("section", None, "tensor"),
        P("section", "tensor"),
        P("section", "tensor"),
        P("section", "tensor"),
        P("section", "tensor"),
        P("section", "tensor"),
        P("section", "tensor"),
        P("section", "tensor", "dp"),
    )
    out_specs = (
        P("section", None, ("dp", "tensor"), None),
        P("section", None, ("dp", "tensor"), None),
        P("section", None),
        P("section", "dp", "tensor"),
        P("section", "dp", "tensor"),
        P("section", "dp", "tensor"),
        P("section", "dp", "tensor"),
        P("section", None, "tensor"),
        P("section", None, "tensor"),
        P("section", "tensor"),
        P("section", "tensor"),
        P("section", "tensor"),
        P("section", "tensor"),
        P("section", "tensor"),
        P("section", "tensor"),
        P("section", "tensor", "dp"),
    )
    return jax.shard_map(body, mesh=mesh, in_specs=in_specs, out_specs=out_specs, check_vma=False)
```

profile of v0, /device:TPU:1, one launch (start us, length us, event | category | flops | bytes accessed | tf_op | source)
XLA Modules:
  0.0 1659.5 jit_solution(13952687797142092474)
XLA Ops:
  13.1 22.0 %all-gather.3 = bf16[1,1024,8]{2,0,1:T(2,128)(2,1)S(1)} all-gather(bf16[1,64,8]{2,0,1:T(2,128)(2,1)S(1)} %copy.399), channel_id=5, replica_groups=mesh['section'=2,'dp'=16,'tensor'=4] {'dp'}, dimensions={1}, use_global_device_ids=true | all-gather | bytes 17408 | tf_op jit(solution)/shard_map/all_gather | solution.py:135
  55.2 44.2 %all-gather.29.cloned.1.call-done = bf16[1,1024,512]{2,1,0:T(8,128)(2,1)} async-done(((bf16[1,64,512]{2,1,0:T(8,128)(2,1)}), bf16[1,1024,512]{2,1,0:T(8,128)(2,1)}) %all-gather.29.cloned.1.call-update) | async-done | bytes 1048592 | tf_op jit(solution)/shard_map/all_gather | solution.py:133
  103.3 22.1 %all-gather.15.cloned.1.call-done = bf16[512,1024]{1,0:T(8,128)(2,1)} async-done(((bf16[128,1024]{1,0:T(8,128)(2,1)}), bf16[512,1024]{1,0:T(8,128)(2,1)}) %all-gather.15.cloned.1.call-update) | async-done | bytes 1048592 | tf_op jit(solution)/shard_map/all_gather | solution.py:157
  147.1 36.4 %while.174 = (s32[]{:T(128)}, f32[8,64,128]{2,1,0:T(8,128)S(1)}, f32[2,256,8,64]{1,0,3,2:T(2,128)}, f32[2,256,8]{1,2,0:T(8,128)S(1)}, f32[8]{0:T(128)S(1)}, /*in...) while((s32[]{:T(128)}, f32[8,64,128]{2,1,0:T(8,128)S(1)}, ...), condition=%wide.region_4.5_spmd.clone.clone, body=%wide.region_1.4_spmd.clone.clone.sunk | while | flops 909582336 | bytes 7883132 | solution.py:70
  200.6 33.1 %reduce-scatter.16.cloned.1.call-done = f32[128,1024]{1,0:T(8,128)} async-done(((f32[512,1024]{1,0:T(8,128)}), f32[128,1024]{1,0:T(8,128)}) %reduce-scatter.16.cloned.1.call-update) | async-done | bytes 524304 | tf_op jit(solution)/shard_map/reduce_scatter | solution.py:176
  296.7 44.4 %while.175 = (s32[]{:T(128)}, f32[8,64,128]{2,1,0:T(8,128)S(1)}, f32[2,256,8,64]{1,0,3,2:T(2,128)}, f32[2,256,8]{1,2,0:T(8,128)S(1)}, f32[8]{0:T(128)S(1)}, /*in...) while((s32[]{:T(128)}, f32[8,64,128]{2,1,0:T(8,128)S(1)}, ...), condition=%wide.region_12.13_spmd.clone.clone, body=%wide.region_9.12_spmd.clone.clone.sunk | while | flops 909582336 | bytes 7883668 | solution.py:70
  343.3 40.4 %while.177 = (s32[]{:T(128)}, f32[8,64,128]{2,1,0:T(8,128)S(1)}, f32[2,256,8,64]{1,0,3,2:T(2,128)}, f32[2,8,64,128]{3,2,1,0:T(8,128)}, f32[2,256,8]{1,2,0:T(8,12...) while((s32[]{:T(128)}, f32[8,64,128]{2,1,0:T(8,128)S(1)}, ...), condition=%wide.region_28.30_spmd.clone.clone, body=%wide.region_25.29_spmd.clone.clone.sunk | while | flops 909582336 | bytes 8351653 | solution.py:70
  417.9 87.3 %while.171 = (s32[]{:T(128)}, f32[8]{0:T(128)}, f32[8,64,128]{2,1,0:T(8,128)}, f32[2,256,8,64]{1,0,3,2:T(2,128)}, f32[2,256,8]{1,2,0:T(8,128)}, /*index=5*/f32[2...) while((s32[]{:T(128)}, f32[8]{0:T(128)}, ...), condition=%wide.region_45.47_spmd.clone, body=%wide.region_31.46_spmd.clone.sunk | while | flops 2126546944 | bytes 30675960 | solution.py:70
  545.0 26.1 %reduce-scatter.18.cloned.1.call-done = f32[128,1024]{1,0:T(8,128)} async-done(((f32[512,1024]{1,0:T(8,128)}), f32[128,1024]{1,0:T(8,128)}) %reduce-scatter.18.cloned.1.call-update) | async-done | bytes 524304 | tf_op jit(solution)/shard_map/reduce_scatter | solution.py:176
  574.4 21.5 %reduce-scatter.24.cloned.1.call-done = bf16[128,1024]{1,0:T(8,128)(2,1)} async-done(((bf16[512,1024]{1,0:T(8,128)(2,1)}), bf16[128,1024]{1,0:T(8,128)(2,1)}) %reduce-scatter.24.cloned.1.call-update) | async-done | bytes 262160 | tf_op jit(solution)/shard_map/reduce_scatter | solution.py:285
  664.2 44.4 %while.176 = (s32[]{:T(128)}, f32[8,64,128]{2,1,0:T(8,128)S(1)}, f32[2,256,8,64]{1,0,3,2:T(2,128)}, f32[2,256,8]{1,2,0:T(8,128)S(1)}, f32[8]{0:T(128)S(1)}, /*in...) while((s32[]{:T(128)}, f32[8,64,128]{2,1,0:T(8,128)S(1)}, ...), condition=%wide.region_20.21_spmd.clone.clone, body=%wide.region_17.20_spmd.clone.clone.sunk | while | flops 909582336 | bytes 7883668 | solution.py:70
  710.8 40.6 %while.178 = (s32[]{:T(128)}, f32[8,64,128]{2,1,0:T(8,128)S(1)}, f32[2,256,8,64]{1,0,3,2:T(2,128)}, f32[2,8,64,128]{3,2,1,0:T(8,128)}, f32[2,256,8]{1,2,0:T(8,12...) while((s32[]{:T(128)}, f32[8,64,128]{2,1,0:T(8,128)S(1)}, ...), condition=%wide.region_53.55_spmd.clone.clone, body=%wide.region_50.54_spmd.clone.clone.sunk | while | flops 909582336 | bytes 8351653 | solution.py:70
  787.3 87.1 %while.172 = (s32[]{:T(128)}, f32[8]{0:T(128)}, f32[8,64,128]{2,1,0:T(8,128)}, f32[2,256,8,64]{1,0,3,2:T(2,128)}, f32[2,256,8]{1,2,0:T(8,128)}, /*index=5*/f32[2...) while((s32[]{:T(128)}, f32[8]{0:T(128)}, ...), condition=%wide.region_70.72_spmd.clone, body=%wide.region_56.71_spmd.clone.sunk | while | flops 2126546944 | bytes 30675960 | solution.py:70
  886.0 21.1 %reduce-scatter.26.cloned.1.call-done = f32[512,64]{0,1:T(8,128)} async-done(((f32[512,256]{0,1:T(8,128)}), f32[512,64]{0,1:T(8,128)}) %reduce-scatter.26.cloned.1.call-update) | async-done | bytes 131088 | tf_op jit(solution)/shard_map/reduce_scatter | solution.py:278
  914.1 23.7 %reduce-scatter.28.cloned.1.call-done = bf16[128,1024]{1,0:T(8,128)(2,1)} async-done(((bf16[512,1024]{1,0:T(8,128)(2,1)}), bf16[128,1024]{1,0:T(8,128)(2,1)}) %reduce-scatter.28.cloned.1.call-update) | async-done | bytes 262160 | tf_op jit(solution)/shard_map/reduce_scatter | solution.py:285
  953.7 42.6 %while.179 = (s32[]{:T(128)}, f32[8,64,128]{2,1,0:T(8,128)S(1)}, f32[2,256,8,64]{1,0,3,2:T(2,128)}, f32[2,8,64,128]{3,2,1,0:T(8,128)}, f32[2,256,8]{1,2,0:T(8,12...) while((s32[]{:T(128)}, f32[8,64,128]{2,1,0:T(8,128)S(1)}, ...), condition=%wide.region_78.80_spmd.clone.clone, body=%wide.region_75.79_spmd.clone.clone.sunk | while | flops 909582336 | bytes 7303557 | solution.py:70
  1021.2 86.6 %while.173 = (s32[]{:T(128)}, f32[8]{0:T(128)}, f32[8,64,128]{2,1,0:T(8,128)}, f32[2,256,8,64]{1,0,3,2:T(2,128)}, f32[2,256,8]{1,2,0:T(8,128)}, /*index=5*/f32[2...) while((s32[]{:T(128)}, f32[8]{0:T(128)}, ...), condition=%wide.region_95.97_spmd.clone, body=%wide.region_81.96_spmd.clone.sunk | while | flops 2126546944 | bytes 27530148 | solution.py:70
  1162.1 61.0 %all-reduce.69 = (f32[1,4,512]{2,1,0:T(4,128)}, f32[1,4,64]{2,1,0:T(4,128)}, f32[1,512]{1,0:T(1,128)}, f32[1,64]{1,0:T(1,128)}, f32[1,8]{1,0:T(1,128)}, /*index=...) all-reduce(f32[1,4,512]{2,1,0:T(4,128)S(1)} %add_bitcast_fusion.19,, ...), channel_id=1, replica_groups=mesh['section'=2,'dp'=16,'tensor'=4] {'dp'}, use_global_device_ids=true, to_apply=%region_118.120 | all-reduce | flops 3416 | bytes 27328 | tf_op jit(solution)/shard_map/psum | solution.py:346
  1223.1 59.0 %reduce-scatter.42.cloned.1.call-done = bf16[512,64]{0,1:T(8,128)(2,1)} async-done(((bf16[512,1024]{0,1:T(8,128)(2,1)}), bf16[512,64]{0,1:T(8,128)(2,1)}) %reduce-scatter.42.cloned.1.call-update) | async-done | bytes 65552 | tf_op jit(solution)/shard_map/reduce_scatter | solution.py:330
  1282.0 75.5 %reduce-scatter.44.cloned.1.call-done = bf16[512,64]{0,1:T(8,128)(2,1)} async-done(((bf16[512,1024]{0,1:T(8,128)(2,1)}), bf16[512,64]{0,1:T(8,128)(2,1)}) %reduce-scatter.44.cloned.1.call-update) | async-done | bytes 65552 | tf_op jit(solution)/shard_map/reduce_scatter | solution.py:330
  1359.1 23.9 %reduce-scatter.32.cloned.1.call-done = bf16[128,1024]{1,0:T(8,128)(2,1)} async-done(((bf16[512,1024]{1,0:T(8,128)(2,1)}), bf16[128,1024]{1,0:T(8,128)(2,1)}) %reduce-scatter.32.cloned.1.call-update) | async-done | bytes 262160 | tf_op jit(solution)/shard_map/reduce_scatter | solution.py:285
  1384.2 150.3 %psum.111 = f32[1,1024]{1,0:T(1,128)} all-reduce(f32[1,1024]{1,0:T(1,128)S(1)} %bitcast.1403), channel_id=1, replica_groups=mesh['section'=2,'dp'=16,'tensor'=4] {'dp','tensor'}, use_global_device_ids=true, to_apply=%region_102.104 | all-reduce | flops 1024 | bytes 8192 | tf_op jit(solution)/shard_map/psum | solution.py:347
  1538.5 32.8 %reduce-scatter.36.cloned.1.call-done = bf16[64,1096]{1,0:T(8,128)(2,1)} async-done(((bf16[1024,1096]{1,0:T(8,128)(2,1)}), bf16[64,1096]{1,0:T(8,128)(2,1)}) %reduce-scatter.36.cloned.1.call-update) | async-done | bytes 140304 | tf_op jit(solution)/shard_map/reduce_scatter | solution.py:327
  1571.3 77.9 %reduce-scatter.38.cloned.1.call-done = bf16[64,1096]{1,0:T(8,128)(2,1)} async-done(((bf16[1024,1096]{1,0:T(8,128)(2,1)}), bf16[64,1096]{1,0:T(8,128)(2,1)}) %reduce-scatter.38.cloned.1.call-update) | async-done | bytes 140304 | tf_op jit(solution)/shard_map/reduce_scatter | solution.py:327
  (1478 shorter events, 943.1 us)
Async XLA Ops:
  7.2 47.9 %all-gather.27.cloned.1.call-start = ((), (), s32[]{:S(2)}) async-start(), calls=%async_computation.36 | async-start | bytes 1114112 | tf_op jit(solution)/shard_map/all_gather | solution.py:132
  8.0 91.4 %all-gather.29.cloned.1.call-start = ((), (), s32[]{:S(2)}) async-start(), calls=%async_computation.37 | async-start | bytes 1114112 | tf_op jit(solution)/shard_map/all_gather | solution.py:133
  8.7 116.7 %all-gather.15.cloned.1.call-start = ((), (), s32[]{:S(2)}) async-start(), calls=%async_computation.15 | async-start | bytes 1310720 | tf_op jit(solution)/shard_map/all_gather | solution.py:157
  11.7 183.3 %all-gather.31.cloned.1.call-start = ((), (), s32[]{:S(2)}) async-start(), calls=%async_computation.38 | async-start | bytes 1114112 | tf_op jit(solution)/shard_map/all_gather | solution.py:136
  12.3 221.4 %reduce-scatter.16.cloned.1.call-start = ((), (), s32[]{:S(2)}) async-start(), calls=%async_computation.16 | async-start | bytes 2621440 | tf_op jit(solution)/shard_map/reduce_scatter | solution.py:176
  199.2 63.2 %all-gather.17.cloned.1.call-start = ((), (), s32[]{:S(2)}) async-start(), calls=%async_computation.17 | async-start | bytes 1310720 | tf_op jit(solution)/shard_map/all_gather | solution.py:157
  240.0 156.3 %all-gather.21.cloned.1.call-start = ((), (), s32[]{:S(2)}) async-start(), calls=%async_computation.21 | async-start | bytes 1310720 | tf_op jit(solution)/shard_map/all_gather | solution.py:236
  241.6 295.9 %reduce-scatter.22.cloned.1.call-start = ((), (), s32[]{:S(2)}) async-start(), calls=%async_computation.22 | async-start | bytes 655360 | tf_op jit(solution)/shard_map/reduce_scatter | solution.py:278
  508.4 62.7 %reduce-scatter.18.cloned.1.call-start = ((), (), s32[]{:S(2)}) async-start(), calls=%async_computation.18 | async-start | bytes 2621440 | tf_op jit(solution)/shard_map/reduce_scatter | solution.py:176
  512.0 83.9 %reduce-scatter.24.cloned.1.call-start = ((), (), s32[]{:S(2)}) async-start(), calls=%async_computation.23 | async-start | bytes 1310720 | tf_op jit(solution)/shard_map/reduce_scatter | solution.py:285
  544.2 80.1 %all-gather.19.cloned.1.call-start = ((), (), s32[]{:S(2)}) async-start(), calls=%async_computation.19 | async-start | bytes 1310720 | tf_op jit(solution)/shard_map/all_gather | solution.py:157
  600.1 166.0 %all-gather.23.cloned.1.call-start = ((), (), s32[]{:S(2)}) async-start(), calls=%async_computation.24 | async-start | bytes 1310720 | tf_op jit(solution)/shard_map/all_gather | solution.py:236
  606.0 301.1 %reduce-scatter.26.cloned.1.call-start = ((), (), s32[]{:S(2)}) async-start(), calls=%async_computation.25 | async-start | bytes 655360 | tf_op jit(solution)/shard_map/reduce_scatter | solution.py:278
  878.1 59.6 %reduce-scatter.28.cloned.1.call-start = ((), (), s32[]{:S(2)}) async-start(), calls=%async_computation.26 | async-start | bytes 1310720 | tf_op jit(solution)/shard_map/reduce_scatter | solution.py:285
  914.0 84.8 %all-gather.25.cloned.1.call-start = ((), (), s32[]{:S(2)}) async-start(), calls=%async_computation.27 | async-start | bytes 1310720 | tf_op jit(solution)/shard_map/all_gather | solution.py:236
  951.5 178.7 %reduce-scatter.30.cloned.1.call-start = ((), (), s32[]{:S(2)}) async-start(), calls=%async_computation.28 | async-start | bytes 655360 | tf_op jit(solution)/shard_map/reduce_scatter | solution.py:278
  1111.0 112.1 %reduce-scatter.40.cloned.1.call-start = ((), (), s32[]{:S(2)}) async-start(), calls=%async_computation.33 | async-start | bytes 1114112 | tf_op jit(solution)/shard_map/reduce_scatter | solution.py:330
  1112.9 169.2 %reduce-scatter.42.cloned.1.call-start = ((), (), s32[]{:S(2)}) async-start(), calls=%async_computation.34 | async-start | bytes 1114112 | tf_op jit(solution)/shard_map/reduce_scatter | solution.py:330
  1116.2 241.3 %reduce-scatter.44.cloned.1.call-start = ((), (), s32[]{:S(2)}) async-start(), calls=%async_computation.35 | async-start | bytes 1114112 | tf_op jit(solution)/shard_map/reduce_scatter | solution.py:330
  1120.5 262.5 %reduce-scatter.32.cloned.1.call-start = ((), (), s32[]{:S(2)}) async-start(), calls=%async_computation.29 | async-start | bytes 1310720 | tf_op jit(solution)/shard_map/reduce_scatter | solution.py:285
  1136.4 400.2 %reduce-scatter.20.cloned.1.call-start = ((), (), s32[]{:S(2)}) async-start(), calls=%async_computation.20 | async-start | bytes 2621440 | tf_op jit(solution)/shard_map/reduce_scatter | solution.py:176
  1140.0 398.5 %reduce-scatter.34.cloned.1.call-start = ((), (), s32[]{:S(2)}) async-start(), calls=%async_computation.30 | async-start | bytes 2506752 | tf_op jit(solution)/shard_map/reduce_scatter | solution.py:327
  1143.2 428.1 %reduce-scatter.36.cloned.1.call-start = ((), (), s32[]{:S(2)}) async-start(), calls=%async_computation.31 | async-start | bytes 2506752 | tf_op jit(solution)/shard_map/reduce_scatter | solution.py:327
  1148.6 500.5 %reduce-scatter.38.cloned.1.call-start = ((), (), s32[]{:S(2)}) async-start(), calls=%async_computation.32 | async-start | bytes 2506752 | tf_op jit(solution)/shard_map/reduce_scatter | solution.py:327
  (361 other events, 7066.9 us)
Sparse Core Ops, SparseCore 0:
  10.2 44.9 all-gather.26
  57.3 42.0 all-gather.28
  101.6 23.7 all-gather.14
  127.4 42.7 all-gather.30
  199.3 34.3 reduce-scatter.15
  240.1 22.2 all-gather.16
  264.2 24.6 all-gather.20
  508.5 28.8 reduce-scatter.21
  540.0 31.0 reduce-scatter.17
  573.9 21.8 reduce-scatter.23
  600.2 24.0 all-gather.18
  625.9 24.4 all-gather.22
  878.3 28.8 reduce-scatter.25
  914.1 23.5 reduce-scatter.27
  951.6 22.2 all-gather.24
  1111.1 18.9 reduce-scatter.29
  1133.2 73.1 reduce-scatter.39
  1209.7 72.2 reduce-scatter.41
  1285.2 72.2 reduce-scatter.43
  1359.9 23.0 reduce-scatter.31
  1385.4 31.0 reduce-scatter.19
  1420.2 73.1 reduce-scatter.33
  1497.1 74.1 reduce-scatter.35
  1574.8 74.3 reduce-scatter.37
where the time goes:
time: 1680 us; the launch traced here: 1660 us
  waiting for transfers between devices  523 us (31%)
  local copies, waits for them, and re-layouts  377 us (22%)
  blocking collectives  323 us (19%)
  matrix products  221 us (13%)
  other arithmetic  181 us (11%)
  between operations  17.4 us (1%)
    dynamic_update_slice x36, local copies, waits for them, and re-layouts, scan_blocks(): _, outputs = lax.scan(jax.checkpoint(block_step), initial, grouped)  218 us
    psum x1, blocking collectives, body(): gain_total = lax.psum(gain_sums, ('dp', 'tensor'))  150 us
    reduce_scatter x3, waiting for transfers between devices, body(): lax.psum_scatter(big_grads[1].astype(jnp.bfloat16), 'dp', scatter_dimensi...  134 us
    reduce_scatter x3, waiting for transfers between devices, body(): lax.psum_scatter(big_grads[0].astype(jnp.bfloat16), 'dp', scatter_dimensi...  111 us
    dot_general x24, matrix products, block_step(): inside = jnp.einsum('hts,shp->thp', mixing, block_x, precision=highest)  76 us
    reduce_scatter x3, waiting for transfers between devices, body(): lax.psum_scatter(jnp.einsum('sc,dc->sd', back_proj, backward_joined, pref...  69.1 us
    psum x1, blocking collectives, body(): small_total = lax.psum(small_sums, 'dp')  61 us
    all_gather x3, waiting for transfers between devices, body(): pieces = lax.all_gather(normed, 'tensor', axis=0, tiled=True)  60.4 us
  transfers between devices with their start and end apart: 28, of which 19 were waited for; matrix products, arithmetic and copies ran while one was open for 26% of the time, Pallas kernels for 0%

commit v1 on v0

v1 whole, which is shorter than its diff:
```python
import functools

import jax
import jax.numpy as jnp
from jax import lax
from jax.experimental import pallas as pl
from jax.experimental.pallas import tpu as pltpu
from jax.sharding import PartitionSpec as P

F32 = jnp.float32
BF16 = jnp.bfloat16
T = 512
L = 128
NB = T // L
D = 1024
CH = 512
INNER = 2048
NST = 128
EPS = 1e-05
X0, Z0, O0, B0, S0, COLS = 0, 512, 1024, 1536, 1792, 1920
VMEM_LIMIT = 56 * 2**20

NN = (((1,), (0,)), ((), ()))
NT = (((1,), (1,)), ((), ()))
TN = (((0,), (0,)), ((), ()))


def mm(a, b, dims=NN):
    return lax.dot_general(a, b, dims, preferred_element_type=F32)


def mm_exact(a, b):
    return lax.dot_general(a, b, NN, precision=lax.Precision.HIGHEST, preferred_element_type=F32)


def mm_split(a, b):
    hi = a.astype(BF16)
    lo = (a - hi.astype(F32)).astype(BF16)
    return mm(hi, b) + mm(lo, b)


def iota(shape, dim):
    return lax.broadcasted_iota(jnp.int32, shape, dim)


def as_row(column):
    return jnp.broadcast_to(column, (L, 128)).T[0:1, :]


def as_column(row):
    return jnp.broadcast_to(row, (128, L)).T[:, 0:1]


def softplus(v):
    return jnp.maximum(v, 0.0) + jnp.log1p(jnp.exp(-jnp.abs(v)))


def head_spread():
    return (iota((128, CH), 1) // 64 == iota((128, CH), 0)).astype(BF16)


def head_collect():
    return (iota((CH, 128), 0) // 64 == iota((CH, 128), 1)).astype(BF16)


def row_mask(length, start, rows, columns):
    return (iota((rows, columns), 0) + start < length).astype(F32)


def rows_of(block):
    return pl.ds(pl.multiple_of(block * L, L), L)


def fwd_kernel(second, *refs):
    if second:
        (len_ref, u_ref, w_ref, par_ref, cot_ref, p_ref, sq_ref, n_ref, px_ref, cx_ref, pz_ref, pbc_ref, cbc_ref,
         v_ref, y_ref, h_ref, gb_ref, dno_ref, padx, padbc, state, step, cum, g_ref) = refs
    else:
        (u_ref, w_ref, par_ref, p_ref, sq_ref, n_ref, px_ref, cx_ref, pz_ref, pbc_ref, cbc_ref,
         v_ref, y_ref, h_ref, padx, padbc, state, step, cum, g_ref) = refs

    def par(row, start, size):
        return par_ref[0, row : row + 1, start : start + size]

    gain_in = jnp.concatenate([par(6, 0, 512), par(7, 0, 512)], axis=1)

    def norm_rows(i, carry):
        rows = pl.ds(pl.multiple_of(i * 64, 64), 64)
        u = u_ref[rows, :].astype(F32)
        r = lax.rsqrt(jnp.mean(u * u, axis=-1, keepdims=True) + EPS)
        n_ref[rows, :] = (u * r * gain_in).astype(BF16)
        return carry

    lax.fori_loop(0, T // 64, norm_rows, 0)

    def weight(start, size):
        return w_ref[0, :, :, start : start + size].reshape(D, size)

    padx[0:8, :] = jnp.zeros((8, CH), F32)
    padbc[0:8, :] = jnp.zeros((8, 256), F32)
    padbc[8 : 8 + T, :] = mm(n_ref[...], weight(B0, 256))
    v_ref[...] = mm(n_ref[...], weight(S0, 128)) + par(8, 0, 128)
    for j in range(2):
        padx[8 : 8 + T, 256 * j : 256 * j + 256] = mm(n_ref[...], weight(X0 + 256 * j, 256))
    for j in range(2):
        pz_ref[:, 256 * j : 256 * j + 256] = mm(n_ref[...], weight(Z0 + 256 * j, 256))
    px_ref[...] = padx[8 : 8 + T, :]
    pbc_ref[...] = padbc[8 : 8 + T, :]

    for b in range(NB):
        for j in range(4):
            cols = slice(128 * j, 128 * j + 128)
            c = par(4, 128 * j, 128)
            for k in range(4):
                c = c + par(k, 128 * j, 128) * padx[5 + k + b * L : 5 + k + b * L + L, cols]
            cx_ref[b * L : b * L + L, cols] = c
        for j in range(2):
            cols = slice(128 * j, 128 * j + 128)
            c = par(13, 128 * j, 128)
            for k in range(4):
                c = c + par(9 + k, 128 * j, 128) * padbc[5 + k + b * L : 5 + k + b * L + L, cols]
            cbc_ref[b * L : b * L + L, cols] = c

    lower = iota((L, L), 0) >= iota((L, L), 1)
    tri = lower.astype(F32)
    off = jnp.where(lower, 0.0, -1e30)
    spread = head_spread()
    rate = -jnp.exp(par(8, 128, 128))
    skip = mm_exact(jnp.broadcast_to(par(8, 256, 128), (8, 128)), spread.astype(F32))[0:1, :]
    gain_out = par(5, 0, CH)
    first_half = iota((L, 128), 1) < 64
    state[...] = jnp.zeros((NST, CH), F32)

    def block(b, carry):
        rows = rows_of(b)
        v = v_ref[rows, :]
        st = softplus(v)
        cu = mm_exact(tri, st * rate)
        cut = cu.T
        ea = jnp.exp(cu)
        tail = jnp.exp(cu[L - 1 : L, :] - cu)
        st_e = mm_split(st, spread)
        ea_e = mm_split(ea, spread)
        tail_e = mm_split(tail, spread)
        cx = cx_ref[rows, :]
        xs = cx * jax.nn.sigmoid(cx)
        cbc = cbc_ref[rows, :]
        bc = (cbc * jax.nn.sigmoid(cbc)).astype(BF16)
        bb, cc = bc[:, :NST], bc[:, NST:]
        xd = xs * st_e
        h_in = state[...].astype(BF16)
        h_ref[b] = h_in
        gram = mm(cc, bb, NT)
        y = mm(cc, h_in) * ea_e
        state[...] = state[...] * ea_e[L - 1 : L, :] + mm(bb, (xd * tail_e).astype(BF16), TN)
        inside = []
        for pair in range(4):
            xp = xd[:, 128 * pair : 128 * pair + 128]
            parts = []
            mixes = []
            for half in range(2):
                h = 2 * pair + half
                mixes.append((gram * jnp.exp(cu[:, h : h + 1] - cut[h : h + 1, :] + off)).astype(BF16))
                parts.append(jnp.where(first_half == (half == 0), xp, 0.0).astype(BF16))
            inside.append(mm(jnp.concatenate(mixes, axis=1), jnp.concatenate(parts, axis=0)))
        y = y + jnp.concatenate(inside, axis=1)
        y_ref[rows, :] = y
        z = pz_ref[rows, :]
        gated = (y + xs * skip) * (z * jax.nn.sigmoid(z))
        sq_ref[pl.ds(b, 1), :] = as_row(jnp.sum(gated * gated, axis=-1, keepdims=True))
        weighted = gated * gain_out
        g_ref[rows, :] = weighted.astype(BF16)
        if second:
            cot = cot_ref[rows, :].astype(F32) * row_mask(len_ref[0, 0], b * L, L, D)
            gb = cot.astype(BF16)
            gb_ref[rows, :] = gb
            dno = jnp.concatenate([mm(gb, weight(O0, 256)), mm(gb, weight(O0 + 256, 256))], axis=1)
            dno_ref[rows, :] = dno
            sq_ref[pl.ds(4 + b, 1), :] = as_row(jnp.sum(dno * weighted, axis=-1, keepdims=True))
        return carry

    lax.fori_loop(0, NB, block, 0)
    if not second:
        sq_ref[4:8, :] = jnp.zeros((4, 128), F32)
    for j in range(4):
        wo = w_ref[0, 4 * j : 4 * j + 4, :, O0 : O0 + CH].reshape(256, CH)
        p_ref[:, 256 * j : 256 * j + 256] = mm(g_ref[...], wo, NT).astype(BF16)


def bwd_kernel(second, *refs):
    if second:
        (gb_ref, w_ref, par_ref, sq_ref, n_ref, px_ref, cx_ref, pz_ref, pbc_ref, cbc_ref, v_ref, y_ref, h_ref, dno_ref,
         dn_ref, dw_ref, sg_ref, padx, padbc, dcx, dcbc, dproj, no_ref, dstate, ggo, gsk, gdt, gdl) = refs
    else:
        (gb_ref, w_ref, par_ref, sq_ref, n_ref, px_ref, cx_ref, pz_ref, pbc_ref, cbc_ref, v_ref, y_ref, h_ref,
         dn_ref, dw_ref, sg_ref, padx, padbc, dcx, dcbc, dproj, no_ref, dstate, ggo, gsk, gdt, gdl) = refs

    def par(row, start, size):
        return par_ref[0, row : row + 1, start : start + size]

    def weight(start, size):
        return w_ref[0, :, :, start : start + size].reshape(D, size)

    lower = iota((L, L), 0) >= iota((L, L), 1)
    upper_inc = (iota((L, L), 1) >= iota((L, L), 0)).astype(F32)
    strict = (iota((L, L), 1) < iota((L, L), 0)).astype(F32)
    upper_low = upper_inc.astype(BF16)
    strict_low = strict.astype(BF16)
    tri = lower.astype(F32)
    off = jnp.where(lower, 0.0, -1e30)
    spread = head_spread()
    collect = head_collect()
    rate = -jnp.exp(par(8, 128, 128))
    skip = mm_exact(jnp.broadcast_to(par(8, 256, 128), (8, 128)), spread.astype(F32))[0:1, :]
    gain_out = par(5, 0, CH)
    first_half = iota((L, 128), 1) < 64
    lanes = iota((L, 128), 1)
    dstate[...] = jnp.zeros((NST, CH), F32)
    ggo[...] = jnp.zeros((8, CH), F32)
    gsk[...] = jnp.zeros((8, CH), F32)
    gdt[...] = jnp.zeros((8, 128), F32)
    gdl[...] = jnp.zeros((8, 128), F32)

    def fold(a):
        return jnp.sum(a.reshape(a.shape[0] // 8, 8, a.shape[1]), axis=0)

    def block(i, carry):
        b = NB - 1 - i
        rows = rows_of(b)
        v = v_ref[rows, :]
        st = softplus(v)
        cu = mm_exact(tri, st * rate)
        cut = cu.T
        ea = jnp.exp(cu)
        tail = jnp.exp(cu[L - 1 : L, :] - cu)
        st_e = mm_split(st, spread)
        ea_e = mm_split(ea, spread)
        tail_e = mm_split(tail, spread)
        cx = cx_ref[rows, :]
        sx = jax.nn.sigmoid(cx)
        xs = cx * sx
        cbc = cbc_ref[rows, :]
        sbc = jax.nn.sigmoid(cbc)
        bc = (cbc * sbc).astype(BF16)
        bb, cc = bc[:, :NST], bc[:, NST:]
        xd = xs * st_e
        factor = as_column(lax.rsqrt(sq_ref[pl.ds(b, 1), :] / INNER + EPS))
        inner = as_column(sq_ref[pl.ds(4 + b, 1), :])
        gb = gb_ref[rows, :]
        if second:
            dno = dno_ref[rows, :]
        else:
            dno = jnp.concatenate([mm(gb, weight(O0, 256)), mm(gb, weight(O0 + 256, 256))], axis=1)
        out = y_ref[rows, :] + xs * skip
        z = pz_ref[rows, :]
        sz = jax.nn.sigmoid(z)
        silu_z = z * sz
        gated = out * silu_z
        scaled = gated * factor
        no_ref[rows, :] = (scaled * gain_out).astype(BF16)
        ggo[...] += fold(dno * scaled)
        dgated = factor * (dno * gain_out) - gated * (factor * factor * factor * (1.0 / INNER) * inner)
        dy = dgated * silu_z
        dproj[rows, Z0 : Z0 + CH] = (dgated * out * (sz * (1.0 + z - silu_z))).astype(BF16)
        gsk[...] += fold(dy * xs)
        dyb = dy.astype(BF16)
        h_in = h_ref[b]
        h_back = dstate[...]
        hb_low = h_back.astype(BF16)
        gram = mm(cc, bb, NT)
        xdt = (xd * tail_e).astype(BF16)
        dye = (dy * ea_e).astype(BF16)
        y_in = mm(cc, h_in) * ea_e
        dxd_in = mm(bb, hb_low) * tail_e
        dcc = mm(dye, h_in, NT)
        dbb = mm(xdt, hb_low, NT)
        dgram = jnp.zeros((L, L), F32)
        inside = []
        crossing = jnp.zeros((L, 128), F32)
        for pair in range(4):
            sl = slice(128 * pair, 128 * pair + 128)
            xp = xd[:, sl].astype(BF16)
            dyp = dy[:, sl]
            decs, mixes, parts = [], [], []
            for half in range(2):
                h = 2 * pair + half
                dec = jnp.exp(cu[:, h : h + 1] - cut[h : h + 1, :] + off)
                decs.append(dec)
                mixes.append(gram * dec)
                parts.append(jnp.where(first_half == (half == 0), dyp, 0.0).astype(BF16))
            dy2 = jnp.concatenate(parts, axis=0)
            dmix = mm(dy2, xp, NT)
            dm0, dm1 = dmix[:L, :], dmix[L:, :]
            dgram = dgram + dm0 * decs[0] + dm1 * decs[1]
            inside.append(mm(jnp.concatenate([mixes[0].astype(BF16), mixes[1].astype(BF16)], axis=0), dy2, TN))
            both = jnp.concatenate([(mixes[0] * dm0).astype(BF16), (mixes[1] * dm1).astype(BF16)], axis=1)
            cross = mm(upper_low, both)
            c0 = (cross[:, :L] * strict).astype(BF16)
            c1 = (cross[:, L:] * strict).astype(BF16)
            pick = jnp.concatenate(
                [(lanes == 2 * pair).astype(BF16), (lanes == 2 * pair + 1).astype(BF16)], axis=0
            )
            crossing = crossing + mm(jnp.concatenate([c0, c1], axis=1), pick)
        dgl = dgram.astype(BF16)
        dcc = dcc + mm(dgl, bb)
        dbb = dbb + mm(dgl, cc, TN)
        dxd = jnp.concatenate(inside, axis=1) + dxd_in
        kept = mm_split(jnp.broadcast_to(jnp.sum(h_in.astype(F32) * h_back, axis=0, keepdims=True), (8, CH)), collect)
        kept = kept[0:1, :] * ea[L - 1 : L, :]
        p_in = mm_split(dy * y_in, collect)
        q_in = mm_split(xd * dxd_in, collect)
        dls = crossing + mm_split_right(upper_low, p_in) + mm_split_right(strict_low, q_in) + kept
        dstate[...] = h_back * ea_e[L - 1 : L, :] + mm(cc, dye, TN)
        dst = dls * rate + mm_split(dxd * xs, collect)
        dv = jnp.where(lanes < 8, dst * jax.nn.sigmoid(v), 0.0)
        dproj[rows, S0 - 512 : S0 - 384] = dv.astype(BF16)
        gdt[...] += fold(dv)
        gdl[...] += fold(dls * st)
        dxs = dy * skip + dxd * st_e
        dcx[rows, :] = dxs * (sx * (1.0 + cx - xs))
        dcbc[rows, :] = jnp.concatenate([dbb, dcc], axis=1) * (sbc * (1.0 + cbc - cbc * sbc))
        return carry

    lax.fori_loop(0, NB, block, 0)

    dcx[T : T + 8, :] = jnp.zeros((8, CH), F32)
    dcbc[T : T + 8, :] = jnp.zeros((8, 256), F32)
    padx[0:8, :] = jnp.zeros((8, CH), F32)
    padx[8 : 8 + T, :] = px_ref[...]
    padbc[0:8, :] = jnp.zeros((8, 256), F32)
    padbc[8 : 8 + T, :] = pbc_ref[...]
    sg_ref[...] = jnp.zeros((16, CH), F32)

    def conv_back(width, first_row, bias_row, dc, pad, start):
        for j in range(width // 128):
            cols = slice(128 * j, 128 * j + 128)
            bias = jnp.zeros((8, 128), F32)
            taps = [jnp.zeros((8, 128), F32) for _ in range(4)]
            for b in range(NB):
                d = dc[b * L : b * L + L, cols]
                bias = bias + fold(d)
                total = jnp.zeros((L, 128), F32)
                for k in range(4):
                    taps[k] = taps[k] + fold(d * pad[5 + k + b * L : 5 + k + b * L + L, cols])
                    total = total + par(first_row + k, 128 * j, 128) * dc[b * L + 3 - k : b * L + 3 - k + L, cols]
                dproj[b * L : b * L + L, start + 128 * j : start + 128 * j + 128] = total.astype(BF16)
            sg_ref[bias_row : bias_row + 1, cols] = jnp.sum(bias, axis=0, keepdims=True)
            for k in range(4):
                sg_ref[first_row + k : first_row + k + 1, cols] = jnp.sum(taps[k], axis=0, keepdims=True)

    conv_back(CH, 0, 4, dcx, padx, X0)
    conv_back(256, 9, 13, dcbc, padbc, B0 - 512)
    sg_ref[5:6, :] = jnp.sum(ggo[...], axis=0, keepdims=True)
    sg_ref[8:9, 0:128] = jnp.sum(gdt[...], axis=0, keepdims=True)
    sg_ref[8:9, 128:256] = jnp.sum(gdl[...], axis=0, keepdims=True) * rate
    gs = mm_split(jnp.broadcast_to(jnp.sum(gsk[...], axis=0, keepdims=True), (8, CH)), collect)
    sg_ref[8:9, 256:384] = gs[0:1, :]

    for j in range(4):
        nt = n_ref[:, 256 * j : 256 * j + 256].T
        gt = gb_ref[:, 256 * j : 256 * j + 256].T
        wr = slice(4 * j, 4 * j + 4)
        for c in range(4):
            dw_ref[wr, :, 256 * c : 256 * c + 256] = (
                mm(nt, dproj[:, 256 * c : 256 * c + 256]).astype(BF16).reshape(4, 64, 256)
            )
        dw_ref[wr, :, B0:S0] = mm(nt, dproj[:, B0 - 512 : S0 - 512]).astype(BF16).reshape(4, 64, 256)
        dw_ref[wr, :, S0:COLS] = mm(nt, dproj[:, S0 - 512 : COLS - 512]).astype(BF16).reshape(4, 64, 128)
        for c in range(2):
            dw_ref[wr, :, O0 + 256 * c : O0 + 256 * c + 256] = (
                mm(gt, no_ref[:, 256 * c : 256 * c + 256]).astype(BF16).reshape(4, 64, 256)
            )
        d = mm(dproj[:, 0:1024], w_ref[0, wr, :, 0:1024].reshape(256, 1024), NT)
        d = d + mm(dproj[:, 1024:1408], w_ref[0, wr, :, B0:COLS].reshape(256, 384), NT)
        dn_ref[:, 256 * j : 256 * j + 256] = d.astype(BF16)


def mm_split_right(a, b):
    hi = b.astype(BF16)
    lo = (b - hi.astype(F32)).astype(BF16)
    return mm(a, hi) + mm(a, lo)


def sds(shape, dtype):
    return jax.ShapeDtypeStruct(shape, dtype)


VM = pl.BlockSpec(memory_space=pltpu.VMEM)


def saved_shapes():
    return [
        sds((T, D), BF16),
        sds((T, CH), F32),
        sds((T, CH), F32),
        sds((T, CH), F32),
        sds((T, 256), F32),
        sds((T, 256), F32),
        sds((T, 128), F32),
        sds((T, CH), F32),
        sds((NB, NST, CH), BF16),
    ]


def layer_spec(k, shape):
    rest = (0,) * (len(shape) - 1)
    return pl.BlockSpec((1,) + shape[1:], lambda i: (k,) + rest)


def whole(shape):
    zeros = (0,) * len(shape)
    return pl.BlockSpec(shape, lambda i: zeros)


def forward(k, u, weights, params, cot=None, length=None):
    second = k == 1
    ins = [u, weights, params]
    specs = [whole(u.shape), layer_spec(k, weights.shape), layer_spec(k, params.shape)]
    outs = [sds((T, D), BF16), sds((8, 128), F32)] + saved_shapes()
    if second:
        ins = [length] + ins + [cot]
        specs = [pl.BlockSpec(memory_space=pltpu.SMEM)] + specs + [whole(cot.shape)]
        outs += [sds((T, D), BF16), sds((T, CH), F32)]
    return pl.pallas_call(
        functools.partial(fwd_kernel, second),
        grid=(1,),
        out_shape=outs,
        in_specs=specs,
        out_specs=[whole(o.shape) for o in outs],
        scratch_shapes=[
            pltpu.VMEM((T + 8, CH), F32),
            pltpu.VMEM((T + 8, 256), F32),
            pltpu.VMEM((NST, CH), F32),
            pltpu.VMEM((8, 128), F32),
            pltpu.VMEM((8, 128), F32),
            pltpu.VMEM((T, CH), BF16),
        ],
        compiler_params=pltpu.CompilerParams(vmem_limit_bytes=VMEM_LIMIT),
    )(*ins)


def backward(k, gb, weights, params, sums, saved, dno=None):
    second = k == 1
    ins = [gb, weights, params, sums] + list(saved)
    if second:
        ins += [dno]
    specs = [whole(a.shape) for a in ins]
    specs[1] = layer_spec(k, weights.shape)
    specs[2] = layer_spec(k, params.shape)
    outs = [sds((T, D), BF16), sds((16, 64, COLS), BF16), sds((16, CH), F32)]
    return pl.pallas_call(
        functools.partial(bwd_kernel, second),
        grid=(1,),
        out_shape=outs,
        in_specs=specs,
        out_specs=[whole(o.shape) for o in outs],
        scratch_shapes=[
            pltpu.VMEM((T + 8, CH), F32),
            pltpu.VMEM((T + 8, 256), F32),
            pltpu.VMEM((T + 8, CH), F32),
            pltpu.VMEM((T + 8, 256), F32),
            pltpu.VMEM((T, 1408), BF16),
            pltpu.VMEM((T, CH), BF16),
            pltpu.VMEM((NST, CH), F32),
            pltpu.VMEM((8, CH), F32),
            pltpu.VMEM((8, CH), F32),
            pltpu.VMEM((8, 128), F32),
            pltpu.VMEM((8, 128), F32),
        ],
        compiler_params=pltpu.CompilerParams(vmem_limit_bytes=VMEM_LIMIT),
    )(*ins)


MESH = pl.DeviceIdType.MESH
ROWS = 128
HALF = 32


def places():
    group = lax.axis_index("dp")
    return lax.axis_index("section"), group // 4, lax.rem(group, 4), lax.axis_index("tensor")


def x_peer(j):
    return {"tensor": lax.rem(lax.axis_index("tensor") + j, 4)}


def y_peer(j):
    _, z, y, _ = places()
    return {"dp": z * 4 + lax.rem(y + j, 4)}


def z_peer(j):
    _, z, y, _ = places()
    return {"dp": lax.rem(z + j, 4) * 4 + y}


def twin():
    return {"section": 1 - lax.axis_index("section")}


ORDER = (1, 3, 2)


def greet(peers):
    barrier = pltpu.get_barrier_semaphore()
    for peer in peers:
        pl.semaphore_signal(barrier, inc=1, device_id=peer, device_id_type=MESH)
    pl.semaphore_wait(barrier, len(peers))


class Sender:
    def __init__(self, send_sems, recv_sems):
        self.send_sems, self.recv_sems, self.copies, self.done = send_sems, recv_sems, [], []

    def __call__(self, src, dst, peer):
        i = len(self.copies)
        copy = pltpu.make_async_remote_copy(
            src_ref=src,
            dst_ref=dst,
            send_sem=self.send_sems.at[i],
            recv_sem=self.recv_sems.at[i],
            device_id=peer,
            device_id_type=MESH,
        )
        copy.start()
        self.copies.append(copy)
        return copy

    def drain(self, copies):
        for copy in copies:
            copy.wait_send()
            self.done.append(copy)

    def finish(self):
        for copy in self.copies:
            if all(copy is not other for other in self.done):
                copy.wait_send()


def own_rows(t):
    return pl.ds(pl.multiple_of(t * ROWS, ROWS), ROWS)


def gather_kernel(wx, wz, wo, wb, par, tok, cot, wall, tok_all, cot_all, par_all, own, bc_in, par_in, lsem, ss, rs):
    s, z, y, t = places()
    d = z * 4 + y
    greet([x_peer(j) for j in ORDER] + [y_peer(j) for j in ORDER] + [z_peer(j) for j in ORDER] + [twin()])
    send = Sender(ss, rs)
    early = []
    for j in ORDER:
        early.append(send(wb, bc_in.at[j], x_peer(j)))
        early.append(send(par, par_in.at[j], x_peer(j)))
    rows = own_rows(t)
    late = []
    for j in ORDER:
        late.append(send(tok.at[s], tok_all.at[rows], x_peer(j)))
    local = [
        pltpu.make_async_copy(tok.at[s], tok_all.at[rows], lsem.at[0]),
        pltpu.make_async_copy(cot.at[s], cot_all.at[rows], lsem.at[1]),
    ]
    for copy in local:
        copy.start()
    bc_in[0] = wb[...]
    par_in[0] = par[...]
    own[:, X0:Z0] = wx[...]
    own[:, Z0:O0] = wz[...]
    own[:, O0:B0] = wo[...]
    for copy in early:
        copy.wait_recv()

    left = iota((64, 128), 1) < 64
    pieces = [bc_in[lax.rem(t - i + 4, 4)].astype(F32) for i in range(4)]
    for i in range(2):
        pair = jnp.where(left, pieces[2 * i], pltpu.roll(pieces[2 * i + 1], 64, 1))
        own[:, B0 + 128 * i : B0 + 128 * i + 128] = pair.astype(BF16)
    steps = pltpu.roll(wb[...].astype(F32), 64, 1)
    own[:, S0:COLS] = jnp.where(iota((64, 128), 1) < 8, steps, 0.0).astype(BF16)
    kept = par[...]
    lanes = iota((16, 128), 1)
    row = iota((16, 128), 0)
    bc_rows = (row >= 9) & (row < 14)
    small = [par_in[lax.rem(t - i + 4, 4), :, 0:128] for i in range(4)]
    for i in range(2):
        pair = jnp.where(lanes < 64, small[2 * i], pltpu.roll(small[2 * i + 1], 64, 1))
        par_all[s, :, 128 * i : 128 * i + 128] = jnp.where(bc_rows, pair, kept[:, 128 * i : 128 * i + 128])
    par_all[s, :, 256:512] = kept[:, 256:512]

    first = []
    for j in ORDER:
        first.append(send(own.at[pl.ds(0, HALF)], wall.at[s, d, pl.ds(0, HALF)], y_peer(j)))
        first.append(send(own.at[pl.ds(HALF, HALF)], wall.at[s, d, pl.ds(HALF, HALF)], z_peer(j)))
    mine = pltpu.make_async_copy(own, wall.at[s, d], lsem.at[2])
    mine.start()
    across = [send(par_all.at[s], par_all.at[s], twin())]
    for j in ORDER:
        late.append(send(cot.at[s], cot_all.at[rows], x_peer(j)))
    for copy in first:
        copy.wait_recv()
    mine.wait()
    grid = wall.reshape(2, 4, 4, 64, COLS)
    upper = grid.at[s, z, :, pl.ds(0, HALF)]
    lower = grid.at[s, :, y, pl.ds(HALF, HALF)]
    second = []
    for j in ORDER:
        second.append(send(upper, upper, z_peer(j)))
        second.append(send(lower, lower, y_peer(j)))
    across.append(send(upper, upper, twin()))
    across.append(send(lower, lower, twin()))
    for i, j in enumerate(ORDER):
        second[2 * i].wait_recv()
        got = grid.at[s, lax.rem(z - j + 4, 4), :, pl.ds(0, HALF)]
        across.append(send(got, got, twin()))
        second[2 * i + 1].wait_recv()
        got = grid.at[s, :, lax.rem(y - j + 4, 4), pl.ds(HALF, HALF)]
        across.append(send(got, got, twin()))
    for copy in across + late:
        copy.wait_recv()
    for copy in local:
        copy.wait()
    send.finish()


def hidden_kernel(p, sq, tok, lens, hid_all, ptot, sums, p_in, sq_in, ss, rs):
    s, _, _, t = places()
    greet([x_peer(j) for j in ORDER])
    send = Sender(ss, rs)
    inner = []
    for j in ORDER:
        inner.append(send(sq, sq_in.at[j], x_peer(j)))
    for j in ORDER:
        inner.append(send(p.at[own_rows(lax.rem(t + j, 4))], p_in.at[j], x_peer(j)))
    for copy in inner:
        copy.wait_recv()
    rows = own_rows(t)
    sums[...] = sq[...] + sq_in[1] + sq_in[2] + sq_in[3]
    factor = as_column(lax.rsqrt(sums[pl.ds(t, 1), :] / INNER + EPS))
    length = lens[pl.ds(s, 1), :]
    mask = (iota((ROWS, 1), 0) + t * ROWS < length).astype(F32)
    total = p[rows, :].astype(F32) + p_in[1].astype(F32) + p_in[2].astype(F32) + p_in[3].astype(F32)
    ptot[...] = total
    hid_all[rows, :] = (mask * (tok[s].astype(F32) + factor * total)).astype(BF16)
    outer = [send(hid_all.at[rows], hid_all.at[rows], x_peer(j)) for j in ORDER]
    for copy in outer:
        copy.wait_recv()
    send.finish()


def sums_kernel(sq, sums, sq_in, ss, rs):
    greet([x_peer(j) for j in ORDER])
    send = Sender(ss, rs)
    for j in ORDER:
        send(sq, sq_in.at[j], x_peer(j))
    for copy in send.copies:
        copy.wait_recv()
    sums[...] = sq[...] + sq_in[1] + sq_in[2] + sq_in[3]
    send.finish()


def input_grad(total, u, gain, upstream):
    r = lax.rsqrt(jnp.mean(u * u, axis=-1, keepdims=True) + EPS)
    b = total * gain
    back = upstream + r * b - u * (r * r * r * (1.0 / D)) * jnp.sum(b * u, axis=-1, keepdims=True)
    return back, jnp.sum(total * (u * r), axis=0, keepdims=True)


def turn_kernel(
    dn, p, sq, hid, par, cot, lens, ptot, sums0, gb_all, sums, back_rows, fin_rows, ggi, dn_in, p_in, s_in, ss, rs
):
    s, _, _, t = places()
    greet([x_peer(j) for j in ORDER])
    send = Sender(ss, rs)
    inner = [send(dn.at[own_rows(lax.rem(t + j, 4))], dn_in.at[j], x_peer(j)) for j in ORDER]
    outer = [send(p.at[own_rows(lax.rem(t + j, 4))], p_in.at[j], x_peer(j)) for j in ORDER]
    rows = own_rows(t)
    length = lens[pl.ds(s, 1), :]
    mask = (iota((ROWS, 1), 0) + t * ROWS < length).astype(F32)
    u = hid[rows, :].astype(F32)
    gain = jnp.concatenate([par[1, 6:7, :], par[1, 7:8, :]], axis=1)
    for copy in inner:
        copy.wait_recv()
    total = dn[rows, :].astype(F32) + dn_in[1].astype(F32) + dn_in[2].astype(F32) + dn_in[3].astype(F32)
    back, gain_grad = input_grad(total, u, gain, mask * cot[s].astype(F32))
    back_rows[...] = back
    ggi[...] = jnp.broadcast_to(gain_grad, (8, D))
    low = (mask * back.astype(BF16).astype(F32)).astype(BF16)
    gb_all[rows, :] = low
    spread = [send(gb_all.at[rows], gb_all.at[rows], x_peer(j)) for j in ORDER]
    inner_row = as_row(jnp.sum(low.astype(F32) * ptot[...], axis=-1, keepdims=True))
    s_in[0] = jnp.broadcast_to(inner_row, (8, 128))
    spread += [send(s_in.at[0], s_in.at[j], x_peer(j)) for j in ORDER]
    for copy in outer:
        copy.wait_recv()
    factor = as_column(lax.rsqrt(sq[pl.ds(t, 1), :] / INNER + EPS))
    total = p[rows, :].astype(F32) + p_in[1].astype(F32) + p_in[2].astype(F32) + p_in[3].astype(F32)
    fin_rows[...] = (mask * (u + factor * total)).astype(BF16)
    for copy in spread:
        copy.wait_recv()
    sums[0:4, :] = sums0[0:4, :]
    for j in range(4):
        sums[pl.ds(4 + lax.rem(t - j + 4, 4), 1), :] = s_in[j, 0:1, :]
    send.finish()


def reduce_kernel(
    dw0, dw1, dn, sg0, sg1, ggi1, tok, par, gb, back, fin, hid,
    lo, ig, o_gi, o_wx, o_wz, o_bc, o_dt, o_cx, o_cb, o_bx, o_bb, o_db, o_dl, o_sk, o_go, o_wo,
    mine, theirs, up_in, low_in, up_mid, low_mid, up_last, low_last, dn_in, own_grad, pack, pack_in, result, bcs, bcs_in,
    lsem, ss, rs,
):
    s, z, y, t = places()
    greet([x_peer(j) for j in ORDER] + [y_peer(j) for j in ORDER] + [z_peer(j) for j in ORDER] + [twin()])
    send = Sender(ss, rs)
    rows = own_rows(t)

    def switched(first, second, dst):
        i = len(send.copies)
        pair = [
            pltpu.make_async_remote_copy(
                src_ref=src, dst_ref=dst, send_sem=ss.at[i], recv_sem=rs.at[i], device_id=twin(), device_id_type=MESH
            )
            for src in (first, second)
        ]
        pl.when(s == 0)(pair[1].start)
        pl.when(s == 1)(pair[0].start)
        send.copies.append(pair[0])
        return pair[0]

    def kept(first, second, dst, i):
        pair = [pltpu.make_async_copy(src, dst, lsem.at[i]) for src in (first, second)]
        pl.when(s == 0)(pair[0].start)
        pl.when(s == 1)(pair[1].start)
        return pair[0]

    swap = switched(dw0, dw1, theirs)
    load = kept(dw0, dw1, mine, 0)
    inner = [send(dn.at[own_rows(lax.rem(t + j, 4))], dn_in.at[j], x_peer(j)) for j in ORDER]
    others = [switched(hid.at[rows], fin, lo.at[s])]
    keeps = [kept(hid.at[rows], fin, lo.at[s], 1)]

    for copy in inner:
        copy.wait_recv()
    u = tok[s].astype(F32)
    gain = jnp.concatenate([par[0, 6:7, :], par[0, 7:8, :]], axis=1)
    total = dn[rows, :].astype(F32) + dn_in[1].astype(F32) + dn_in[2].astype(F32) + dn_in[3].astype(F32)
    grad, gain_grad = input_grad(total, u, gain, gb[rows, :].astype(F32))
    own_grad[...] = grad
    others.append(switched(own_grad, back, ig.at[s]))
    keeps.append(kept(own_grad, back, ig.at[s], 2))
    for k, (sg, gg) in enumerate(((sg0, gain_grad), (sg1, ggi1[0:1, :]))):
        pack[k] = sg[...]
        pack[k, 6:7, :] = gg[:, 0:CH]
        pack[k, 7:8, :] = gg[:, CH:D]
    small = send(pack.at[1 - s], pack_in.at[0], twin())

    load.wait()
    swap.wait_recv()

    def add_twin(i, carry):
        mine[i] = (mine[i].astype(F32) + theirs[i].astype(F32)).astype(BF16)
        return carry

    lax.fori_loop(0, 16, add_twin, 0)
    grid = mine.reshape(4, 4, 64, COLS)
    first = []
    for j in ORDER:
        first.append(send(grid.at[:, lax.rem(y + j, 4), pl.ds(0, HALF)], up_in.at[j], y_peer(j)))
        first.append(send(grid.at[lax.rem(z + j, 4), :, pl.ds(HALF, HALF)], low_in.at[j], z_peer(j)))
    small.wait_recv()
    result[...] = pack[s] + pack_in[0]
    around = [send(result, pack_in.at[j], y_peer(j)) for j in ORDER]
    for copy in first:
        copy.wait_recv()
    up_own = mine.reshape(4, 4, 64, COLS)

    def add_first(i, carry):
        a = up_own[i, y, 0:HALF, :].astype(F32)
        b = up_own[z, i, HALF:64, :].astype(F32)
        for j in (1, 2, 3):
            a = a + up_in[j, i].astype(F32)
            b = b + low_in[j, i].astype(F32)
        up_mid[i] = a.astype(BF16)
        low_mid[i] = b.astype(BF16)
        return carry

    lax.fori_loop(0, 4, add_first, 0)
    second = []
    for j in ORDER:
        second.append(send(up_mid.at[lax.rem(z + j, 4)], up_last.at[j], z_peer(j)))
        second.append(send(low_mid.at[lax.rem(y + j, 4)], low_last.at[j], y_peer(j)))
    for copy in around:
        copy.wait_recv()
    send.drain(around)
    result[...] = result[...] + pack_in[1] + pack_in[2] + pack_in[3]
    around2 = [send(result, pack_in.at[3 + j], z_peer(j)) for j in ORDER]
    for copy in second:
        copy.wait_recv()
    up = up_mid[z].astype(F32) + up_last[1].astype(F32) + up_last[2].astype(F32) + up_last[3].astype(F32)
    low = low_mid[y].astype(F32) + low_last[1].astype(F32) + low_last[2].astype(F32) + low_last[3].astype(F32)
    for half, part in ((0, up), (HALF, low)):
        for i in range(2):
            bcs[i, half : half + HALF, :] = part[:, B0 + 128 * i : B0 + 128 * i + 128]
    last = [send(bcs.at[lax.rem(t + j, 4) // 2], bcs_in.at[j], x_peer(j)) for j in ORDER]
    for copy in around2:
        copy.wait_recv()
    send.drain(around2)
    result[...] = result[...] + pack_in[4] + pack_in[5] + pack_in[6]
    around3 = [send(result, pack_in.at[6 + j], x_peer(j)) for j in ORDER]
    for half, part in ((0, up), (HALF, low)):
        o_wx[half : half + HALF, :] = part[:, X0:Z0]
        o_wz[half : half + HALF, :] = part[:, Z0:O0]
        o_dt[half : half + HALF, :] = part[:, S0 : S0 + 8]
    out_part = jnp.concatenate([up[:, O0:B0], low[:, O0:B0]], axis=0)
    o_wo[...] = jnp.concatenate([out_part, out_part], axis=0).T[:, 0:64]
    o_cx[...] = result[0:4, :]
    o_bx[...] = result[4:5, :]
    o_go[...] = result[5:6, :]
    o_db[...] = result[8:9, 0:8]
    o_dl[...] = result[8:9, 128:136]
    o_sk[...] = result[8:9, 256:264]
    for copy in last:
        copy.wait_recv()
    block = bcs[t // 2] + bcs_in[1] + bcs_in[2] + bcs_in[3]
    o_bc[...] = jnp.where(lax.rem(t, 2) == 0, block[:, 0:64], block[:, 64:128])
    for copy in around3:
        copy.wait_recv()
    whole_sum = result[...] + pack_in[7] + pack_in[8] + pack_in[9]
    o_gi[...] = jnp.concatenate([whole_sum[6:7, :], whole_sum[7:8, :]], axis=1)
    chosen = whole_sum[8:16, 0:64]
    for i in range(1, 4):
        chosen = jnp.where(t == i, whole_sum[8:16, 64 * i : 64 * i + 64], chosen)
    o_cb[...] = chosen[1:5, :]
    o_bb[...] = chosen[5:6, :]
    for copy in others:
        copy.wait_recv()
    for copy in keeps:
        copy.wait()
    send.finish()


ANY = pl.BlockSpec(memory_space=pl.ANY)


def talk(kernel, number, ins, in_specs, outs, out_specs, scratch, copies, locals_=0):
    sems = ([pltpu.SemaphoreType.DMA((locals_,))] if locals_ else []) + [pltpu.SemaphoreType.DMA((copies,))] * 2
    return pl.pallas_call(
        kernel,
        out_shape=outs,
        in_specs=in_specs,
        out_specs=out_specs,
        scratch_shapes=list(scratch) + sems,
        compiler_params=pltpu.CompilerParams(
            collective_id=number, has_side_effects=True, vmem_limit_bytes=VMEM_LIMIT
        ),
    )(*ins)


def body(
    tokens_in, cotangent, seq_lengths, gain_in, weight_x, weight_z, weight_bc, weight_dt, conv_x, conv_bc,
    bias_x, bias_bc, dt_bias, decay_log, skip_gain, gain_out, weight_out,
):
    def wide(a, left, right):
        return jnp.pad(a, ((0, 0), (left, right)))

    heads = jnp.concatenate(
        [wide(dt_bias, 0, 120), wide(decay_log, 0, 120), wide(skip_gain, 0, 120 + 128)], axis=1
    )
    par = jnp.concatenate(
        [
            conv_x[0],
            bias_x,
            gain_out,
            gain_in.reshape(2, CH),
            heads,
            wide(conv_bc[0], 0, CH - 64),
            wide(bias_bc, 0, CH - 64),
            jnp.zeros((2, CH), F32),
        ],
        axis=0,
    )
    wb = jnp.concatenate([weight_bc[0], weight_dt[0], jnp.zeros((64, 56), BF16)], axis=1)
    wall, tok_all, cot_all, par_all = talk(
        gather_kernel,
        0,
        [weight_x[0], weight_z[0], weight_out[0].T, wb, par, tokens_in, cotangent],
        [VM] * 5 + [ANY] * 2,
        [sds((2, 16, 64, COLS), BF16), sds((T, D), BF16), sds((T, D), BF16), sds((2, 16, CH), F32)],
        [ANY, ANY, ANY, VM],
        [pltpu.VMEM((64, COLS), BF16), pltpu.VMEM((4, 64, 128), BF16), pltpu.VMEM((4, 16, CH), F32)],
        40,
        3,
    )
    p0, sq0, *saved0 = forward(0, tok_all, wall, par_all)
    hid_all, ptot0, sums0 = talk(
        hidden_kernel,
        1,
        [p0, sq0, tokens_in, seq_lengths],
        [VM] * 4,
        [sds((T, D), BF16), sds((ROWS, D), F32), sds((8, 128), F32)],
        [VM] * 3,
        [pltpu.VMEM((4, ROWS, D), BF16), pltpu.VMEM((4, 8, 128), F32)],
        9,
    )
    length = lax.dynamic_slice_in_dim(seq_lengths, lax.axis_index("section"), 1, 0)
    p1, sq1, *saved1, gb1, dno1 = forward(1, hid_all, wall, par_all, cot_all, length)
    sums1 = talk(
        sums_kernel, 2, [sq1], [VM], sds((8, 128), F32), VM, [pltpu.VMEM((4, 8, 128), F32)], 3
    )
    dn1, dw1, sg1 = backward(1, gb1, wall, par_all, sums1, saved1, dno1)
    gb0, sums0b, back, fin, ggi1 = talk(
        turn_kernel,
        3,
        [dn1, p1, sums1, hid_all, par_all, cotangent, seq_lengths, ptot0, sums0],
        [VM] * 9,
        [sds((T, D), BF16), sds((8, 128), F32), sds((ROWS, D), F32), sds((ROWS, D), BF16), sds((8, D), F32)],
        [VM] * 5,
        [pltpu.VMEM((4, ROWS, D), BF16), pltpu.VMEM((4, ROWS, D), BF16), pltpu.VMEM((4, 8, 128), F32)],
        12,
    )
    dn0, dw0, sg0 = backward(0, gb0, wall, par_all, sums0b, saved0)
    outs = [
        sds((2, ROWS, D), BF16),
        sds((2, ROWS, D), F32),
        sds((1, D), F32),
        sds((64, CH), F32),
        sds((64, CH), F32),
        sds((64, 64), F32),
        sds((64, 8), F32),
        sds((4, CH), F32),
        sds((4, 64), F32),
        sds((1, CH), F32),
        sds((1, 64), F32),
        sds((1, 8), F32),
        sds((1, 8), F32),
        sds((1, 8), F32),
        sds((1, CH), F32),
        sds((CH, 64), F32),
    ]
    found = talk(
        reduce_kernel,
        4,
        [dw0, dw1, dn0, sg0, sg1, ggi1, tokens_in, par_all, gb0, back, fin, hid_all],
        [ANY, ANY] + [VM] * 7 + [ANY, ANY, ANY],
        outs,
        [ANY, ANY] + [VM] * 14,
        [
            pltpu.VMEM((16, 64, COLS), BF16),
            pltpu.VMEM((16, 64, COLS), BF16),
            pltpu.VMEM((4, 4, HALF, COLS), BF16),
            pltpu.VMEM((4, 4, HALF, COLS), BF16),
            pltpu.VMEM((4, HALF, COLS), BF16),
            pltpu.VMEM((4, HALF, COLS), BF16),
            pltpu.VMEM((4, HALF, COLS), BF16),
            pltpu.VMEM((4, HALF, COLS), BF16),
            pltpu.VMEM((4, ROWS, D), BF16),
            pltpu.VMEM((ROWS, D), F32),
            pltpu.VMEM((2, 16, CH), F32),
            pltpu.VMEM((10, 16, CH), F32),
            pltpu.VMEM((16, CH), F32),
            pltpu.VMEM((2, 64, 128), F32),
            pltpu.VMEM((4, 64, 128), F32),
        ],
        32,
        3,
    )
    return tuple(
        a if i in (2, 9, 10, 11, 12, 13, 14) else a[None] for i, a in enumerate(found)
    )


def solution(mesh):
    in_specs = (
        P(None, ("dp", "tensor"), None),
        P(None, ("dp", "tensor"), None),
        P(None, "dp"),
        P("section", None),
        P("section", "dp", "tensor"),
        P("section", "dp", "tensor"),
        P("section", "dp", "tensor"),
        P("section", "dp", "tensor"),
        P("section", None, "tensor"),
        P("section", None, "tensor"),
        P("section", "tensor"),
        P("section", "tensor"),
        P("section", "tensor"),
        P("section", "tensor"),
        P("section", "tensor"),
        P("section", "tensor"),
        P("section", "tensor", "dp"),
    )
    out_specs = (
        P("section", None, ("dp", "tensor"), None),
        P("section", None, ("dp", "tensor"), None),
        P("section", None),
        P("section", "dp", "tensor"),
        P("section", "dp", "tensor"),
        P("section", "dp", "tensor"),
        P("section", "dp", "tensor"),
        P("section", None, "tensor"),
        P("section", None, "tensor"),
        P("section", "tensor"),
        P("section", "tensor"),
        P("section", "tensor"),
        P("section", "tensor"),
        P("section", "tensor"),
        P("section", "tensor"),
        P("section", "tensor", "dp"),
    )
    return jax.shard_map(body, mesh=mesh, in_specs=in_specs, out_specs=out_specs, check_vma=False)
```

time: 1680 us -> 280 us (0.17)
  waiting for transfers between devices: 523 us -> 0 us
  local copies, waits for them, and re-layouts: 377 us -> 21.8 us
  blocking collectives: 323 us -> 0 us
  Pallas kernels: 0 us -> 249 us
  matrix products: 221 us -> 0 us
  other arithmetic: 181 us -> 3.44 us
    reduce_scatter x15 -> x0, waiting for transfers between devices: 413 us -> none  [the longest x3 134 us: body(): lax.psum_scatter(big_grads[1].astype(jnp.bfloat16), 'dp', scatter_dimensi...]
    psum x8 -> x0, blocking collectives: 252 us -> none  [the longest x1 150 us: body(): gain_total = lax.psum(gain_sums, ('dp', 'tensor'))]
    pallas_call x0 -> x9, Pallas kernels: none -> 249 us  [the longest x5 177 us: talk(): pl.pallas_call(kernel, out_shape=outs, in_specs=in_specs, out_specs=out_s...]
    dot_general x126 -> x0, matrix products: 221 us -> none  [the longest x24 76 us: block_step(): inside = jnp.einsum('hts,shp->thp', mixing, block_x, precision=highest)]
    dynamic_update_slice x36 -> x0, local copies, waits for them, and re-layouts: 218 us -> none  [scan_blocks(): _, outputs = lax.scan(jax.checkpoint(block_step), initial, grouped)]
    all_gather x9 -> x0, waiting for transfers between devices: 106 us -> none  [the longest x3 60.4 us: body(): pieces = lax.all_gather(normed, 'tensor', axis=0, tiled=True)]
    all_gather x5 -> x0, blocking collectives: 70.9 us -> none  [the longest x3 30.4 us: body(): both_bc = lax.all_gather(own_bc, 'tensor', axis=1, tiled=True)]
    reduce_sum x41 -> x0, other arithmetic: 66.5 us -> none  [the longest x6 18.3 us: causal_conv(): kernel[offset][None, :] * padded[offset:offset + signal.shape[0]]]
  transfers between devices with their start and end apart: 28 -> 0, of which waited for: 19 -> 0; matrix products, arithmetic and copies ran while one was open for 26% -> 0% of each run, Pallas kernels for 0% -> 0%
where the time goes in v1:
time: 280 us; the launch traced here: 275 us
  Pallas kernels  249 us (89%)
  local copies, waits for them, and re-layouts  21.8 us (8%)
  other arithmetic  3.44 us (1%)
    pallas_call x5, Pallas kernels, talk(): pl.pallas_call(kernel, out_shape=outs, in_specs=in_specs, out_specs=out_s...  177 us
    pallas_call x2, Pallas kernels, backward(): pl.pallas_call(functools.partial(bwd_kernel, second), grid=(1,), out_shap...  45.4 us
    pallas_call x2, Pallas kernels, forward(): pl.pallas_call(functools.partial(fwd_kernel, second), grid=(1,), out_shap...  26.9 us
    unnamed x41, local copies, waits for them, and re-layouts  17.9 us

profile of v1, /device:TPU:1, one launch (start us, length us, event | category | flops | bytes accessed | tf_op | source)
XLA Modules:
  0.0 275.3 jit_solution(2607851903426195927)
XLA Ops:
  0.7 0.7 copy.33.lens
  2.0 0.7 pad.23
  2.7 0.7 fusion.1
  3.9 1.3 reduce.3
  5.2 0.7 pad.22
  5.9 2.0 concatenate.11.par
  7.9 0.8 copy.34
  8.6 1.4 maximum_maximum_fusion.wb
  10.1 48.4 %shard_map.288 = (bf16[2,16,64,1920]{3,2,1,0:T(8,128)(2,1)}, bf16[512,1024]{1,0:T(8,128)(2,1)}, bf16[512,1024]{1,0:T(8,128)(2,1)}, f32[2,16,512]{2,1,0:T(8,128)}) custom-call(bf16[64,512]{1,0:T(8,128)(2,1)} %bitcast.23, bf16[64,512]{1,0:T(8,128)(2,1)} %bitcast.24, bf16[64,512]{1,0:T(8,128)(2,1)} %bitcast.25, bf16[64,128]{1,0:T(8,128)(2,1)} %maximum_maximum_fusion.wb, ...), custom_call_target="tpu_custom_call" | custom-call | tf_op jit(solution)/shard_map/pallas_call | solution.py:846
  58.5 12.1 %shard_map.289 = (bf16[512,1024]{1,0:T(8,128)(2,1)}, f32[8,128]{1,0:T(8,128)}, bf16[512,1024]{1,0:T(8,128)(2,1)}, f32[512,512]{1,0:T(8,128)}, f32[512,512]{1,0:T...) custom-call(bf16[512,1024]{1,0:T(8,128)(2,1)} %get-tuple-element.74., ...), custom_call_target="tpu_custom_call" | custom-call | tf_op jit(solution)/shard_map/pallas_call | solution.py:424
  70.5 31.3 %shard_map.290 = (bf16[512,1024]{1,0:T(8,128)(2,1)}, f32[128,1024]{1,0:T(8,128)}, f32[8,128]{1,0:T(8,128)}) custom-call(bf16[512,1024]{1,0:T(8,128)(2,1)} %get-tuple-element.77.p, f32[8,128]{1,0:T(8,128)} %get-tuple-element.78.sq, bf16[2,128,1024]{2,1,0:T(8,128)(2,1)} %tok.5, s32[2,1]{1,0:T(2,128)} %copy-done.3), custom_call_target="tpu_custom_call" | custom-call | tf_op jit(solution)/shard_map/pallas_call | solution.py:846
  101.8 14.8 %shard_map.291 = (bf16[512,1024]{1,0:T(8,128)(2,1)}, f32[8,128]{1,0:T(8,128)}, bf16[512,1024]{1,0:T(8,128)(2,1)}, f32[512,512]{1,0:T(8,128)}, f32[512,512]{1,0:T...) custom-call(s32[1,1]{1,0:T(1,128)} %constant_dynamic-slice_fusion.re, ...), custom_call_target="tpu_custom_call" | custom-call | tf_op jit(solution)/shard_map/pallas_call | solution.py:424
  116.6 5.4 %shard_map.292.refs_3_.sq = f32[8,128]{1,0:T(8,128)} custom-call(f32[8,128]{1,0:T(8,128)} %get-tuple-element.82.sq), custom_call_target="tpu_custom_call" | custom-call | tf_op jit(solution)/shard_map/pallas_call | solution.py:846
  122.0 22.3 %shard_map.293 = (bf16[512,1024]{1,0:T(8,128)(2,1)}, bf16[16,64,1920]{2,1,0:T(8,128)(2,1)}, f32[16,512]{1,0:T(8,128)}) custom-call(bf16[512,1024]{1,0:T(8,128)(2,1)} %get-tuple-element.81.refs_0_, bf16[2,16,64,1920]{3,2,1,0:T(8,128)(2,1)} %get-tuple-element.75.refs_1_.refs_2_, f32[2,16,512]{2,1,0:T(8,128)} %get-tuple-element.76.refs_2_.refs_3_.par, ...), custom_call_target="tpu_custom_call" | custom-call | tf_op jit(solution)/shard_map/pallas_call | solution.py:451
  144.3 38.4 %shard_map.294 = (bf16[512,1024]{1,0:T(8,128)(2,1)}, f32[8,128]{1,0:T(8,128)}, f32[128,1024]{1,0:T(8,128)}, bf16[128,1024]{1,0:T(8,128)(2,1)}, f32[8,1024]{1,0:T(8,128)}) custom-call(bf16[512,1024]{1,0:T(8,128)(2,1)} %get-tuple-element.93.dn, bf16[512,1024]{1,0:T(8,128)(2,1)} %get-tuple-element.94.p, f32[8,128]{1,0:T(8,128)} %shard_map.292.refs_3_.sq, ...), custom_call_target="tpu_custom_call" | custom-call | tf_op jit(solution)/shard_map/pallas_call | solution.py:846
  182.7 23.1 %shard_map.295 = (bf16[512,1024]{1,0:T(8,128)(2,1)}, bf16[16,64,1920]{2,1,0:T(8,128)(2,1)}, f32[16,512]{1,0:T(8,128)}) custom-call(bf16[512,1024]{1,0:T(8,128)(2,1)} %get-tuple-element.97.refs_0_.gb, bf16[2,16,64,1920]{3,2,1,0:T(8,128)(2,1)} %get-tuple-element.75.refs_1_.refs_2_, f32[2,16,512]{2,1,0:T(8,128)} %get-tuple-element.76.refs_2_.refs_3_.par, ...), custom_call_target="tpu_custom_call" | custom-call | tf_op jit(solution)/shard_map/pallas_call | solution.py:451
  205.8 53.5 %shard_map.296 = (bf16[2,128,1024]{2,1,0:T(8,128)(2,1)}, f32[2,128,1024]{2,1,0:T(8,128)}, f32[1,1024]{1,0:T(1,128)}, f32[64,512]{1,0:T(8,128)}, f32[64,512]{1,0:...) custom-call(bf16[16,64,1920]{2,1,0:T(8,128)(2,1)} %get-tuple-element, ...), custom_call_target="tpu_custom_call" | custom-call | tf_op jit(solution)/shard_map/pallas_call | solution.py:846
  259.5 1.4 copy.37
  260.9 1.7 copy.38
  262.6 1.9 copy.53
  264.5 2.3 copy.54
  266.8 1.3 copy.55
  268.1 1.6 copy.56
  269.6 0.7 copy.57
  (37 shorter events, 6.2 us)
Async XLA Ops:
  1.5 69.1 %copy-start.3 = (s32[2,1]{1,0:T(2,128)}, s32[2,1]{1,0:T(2,128)S(1)}, u32[]{:S(2)}) copy-start(s32[2,1]{1,0:T(2,128)S(1)} %copy.33.lens) | copy-start | bytes 28
  259.4 10.3 %copy-start = (f32[64,512]{1,0:T(8,128)S(1)}, f32[64,512]{1,0:T(8,128)}, u32[]{:S(2)}) copy-start(f32[64,512]{1,0:T(8,128)} %get-tuple-element.120) | copy-start | bytes 393220
  259.4 10.9 %copy-start.1 = (f32[64,64]{1,0:T(8,128)S(1)}, f32[64,64]{1,0:T(8,128)}, u32[]{:S(2)}) copy-start(f32[64,64]{1,0:T(8,128)} %get-tuple-element.121) | copy-start | bytes 49156
  259.4 11.5 %copy-start.2 = (f32[4,512]{1,0:T(4,128)S(1)}, f32[4,512]{1,0:T(4,128)}, u32[]{:S(2)}) copy-start(f32[4,512]{1,0:T(4,128)} %get-tuple-element.123) | copy-start | bytes 24580
  259.4 12.1 %copy-start.6 = (f32[4,64]{1,0:T(4,128)S(1)}, f32[4,64]{1,0:T(4,128)}, u32[]{:S(2)}) copy-start(f32[4,64]{1,0:T(4,128)} %get-tuple-element.124) | copy-start | bytes 3076
  259.4 12.7 %copy-start.5 = (f32[1,512]{1,0:T(1,128)S(1)}, f32[1,512]{1,0:T(1,128)}, u32[]{:S(2)}) copy-start(f32[1,512]{1,0:T(1,128)} %get-tuple-element.173) | copy-start | bytes 6148
  259.4 13.3 %copy-start.10 = (f32[1,64]{1,0:T(1,128)S(1)}, f32[1,64]{1,0:T(1,128)}, u32[]{:S(2)}) copy-start(f32[1,64]{1,0:T(1,128)} %get-tuple-element.174) | copy-start | bytes 772
  259.4 13.8 %copy-start.9 = (f32[1,8]{1,0:T(1,128)S(1)}, f32[1,8]{1,0:T(1,128)}, u32[]{:S(2)}) copy-start(f32[1,8]{1,0:T(1,128)} %get-tuple-element.175) | copy-start | bytes 100
  259.4 14.3 %copy-start.8 = (f32[1,8]{1,0:T(1,128)S(1)}, f32[1,8]{1,0:T(1,128)}, u32[]{:S(2)}) copy-start(f32[1,8]{1,0:T(1,128)} %get-tuple-element.176) | copy-start | bytes 100
  259.4 14.8 %copy-start.7 = (f32[1,8]{1,0:T(1,128)S(1)}, f32[1,8]{1,0:T(1,128)}, u32[]{:S(2)}) copy-start(f32[1,8]{1,0:T(1,128)} %get-tuple-element.177) | copy-start | bytes 100
  259.4 15.3 %copy-start.4 = (f32[1,512]{1,0:T(1,128)S(1)}, f32[1,512]{1,0:T(1,128)}, u32[]{:S(2)}) copy-start(f32[1,512]{1,0:T(1,128)} %get-tuple-element.178) | copy-start | bytes 6148

commit v2 on v0

v2 whole, which is shorter than its diff:
```python
import jax
import jax.numpy as jnp
from jax import lax
from jax.experimental import pallas as pl
from jax.experimental.pallas import tpu as pltpu
from jax.sharding import PartitionSpec as P

F32 = jnp.float32
BF16 = jnp.bfloat16
T = 512
L = 128
NB = T // L
D = 1024
CH = 512
INNER = 2048
NST = 128
EPS = 1e-05
X0, Z0, O0, B0, S0, COLS = 0, 512, 1024, 1536, 1792, 1920
VMEM_LIMIT = 60 * 2**20
MESH = pl.DeviceIdType.MESH
ROWS = 128
HALF = 32
ORDER = (1, 3, 2)

NN = (((1,), (0,)), ((), ()))
NT = (((1,), (1,)), ((), ()))
TN = (((0,), (0,)), ((), ()))


def mm(a, b, dims=NN):
    return lax.dot_general(a, b, dims, preferred_element_type=F32)


def mm_exact(a, b):
    return lax.dot_general(a, b, NN, precision=lax.Precision.HIGHEST, preferred_element_type=F32)


def mm_split(a, b):
    hi = a.astype(BF16)
    lo = (a - hi.astype(F32)).astype(BF16)
    return mm(hi, b) + mm(lo, b)


def mm_split_right(a, b):
    hi = b.astype(BF16)
    lo = (b - hi.astype(F32)).astype(BF16)
    return mm(a, hi) + mm(a, lo)


def iota(shape, dim):
    return lax.broadcasted_iota(jnp.int32, shape, dim)


def as_row(column):
    return jnp.broadcast_to(column, (L, 128)).T[0:1, :]


def as_column(row):
    return jnp.broadcast_to(row, (128, L)).T[:, 0:1]


def softplus(v):
    return jnp.maximum(v, 0.0) + jnp.log1p(jnp.exp(-jnp.abs(v)))


def head_spread():
    return (iota((128, CH), 1) // 64 == iota((128, CH), 0)).astype(BF16)


def head_collect():
    return (iota((CH, 128), 0) // 64 == iota((CH, 128), 1)).astype(BF16)


def fold(a):
    return jnp.sum(a.reshape(a.shape[0] // 8, 8, a.shape[1]), axis=0)


def span(start, size):
    return pl.ds(pl.multiple_of(start, size), size)


def places():
    group = lax.axis_index("dp")
    return lax.axis_index("section"), group // 4, lax.rem(group, 4), lax.axis_index("tensor")


def x_peer(j):
    return {"tensor": lax.rem(lax.axis_index("tensor") + j, 4)}


def twin():
    return {"section": 1 - lax.axis_index("section")}


def greet(peers):
    barrier = pltpu.get_barrier_semaphore()
    for peer in peers:
        pl.semaphore_signal(barrier, inc=1, device_id=peer, device_id_type=MESH)
    pl.semaphore_wait(barrier, len(peers))


class Link:
    def __init__(self, send_sems, recv_sems):
        self.send_sems, self.recv_sems = send_sems, recv_sems

    def copy(self, src, dst, at, peer):
        return pltpu.make_async_remote_copy(
            src_ref=src,
            dst_ref=dst,
            send_sem=self.send_sems.at[at],
            recv_sem=self.recv_sems.at[at],
            device_id=peer,
            device_id_type=MESH,
        )

    def start(self, src, dst, at, peer):
        self.copy(src, dst, at, peer).start()

    def arrived(self, like, at):
        self.copy(like, like, at, twin()).wait_recv()

    def sent(self, like, at):
        self.copy(like, like, at, twin()).wait_send()


SCRATCH = dict(
    wall0=((16, 64, COLS), BF16),
    wall1=((16, 64, COLS), BF16),
    dw1=((16, 64, COLS), BF16),
    theirs=((2, 16, HALF, COLS), BF16),
    first_in=((2, 3, 4, HALF, COLS), BF16),
    mid=((2, 4, HALF, COLS), BF16),
    last_in=((2, 4, HALF, COLS), BF16),
    half=((2, HALF, COLS), F32),
    other_half=((HALF, COLS), F32),
    own=((64, COLS), BF16),
    src=((2, HALF, COLS), BF16),
    bc_in=((4, 64, 128), BF16),
    par_own=((16, CH), F32),
    par_in=((4, 16, CH), F32),
    par_all=((2, 16, CH), F32),
    tok=((T, D), BF16),
    hid=((T, D), BF16),
    gb1=((T, D), BF16),
    gb0=((T, D), BF16),
    pa=((T, D), BF16),
    pb=((T, D), BF16),
    pc=((T, D), BF16),
    ra=((NB, 3, HALF, D), BF16),
    rb=((NB, 3, HALF, D), BF16),
    pb_in=((3, ROWS, D), BF16),
    pc_in=((3, ROWS, D), BF16),
    ptot0=((NB, HALF, D), F32),
    sq_tile=((2, NB, 8, 128), F32),
    sq_in=((2, NB, 4, 8, 128), F32),
    sums=((2, NB, 8, 128), F32),
    inner0=((T, 128), F32),
    factors=((ROWS, 128), F32),
    dno=((T, CH), F32),
    blkx=((L + 8, CH), F32),
    blkbc=((L + 8, 256), F32),
    dcx=((L + 8, CH), F32),
    dcbc=((L + 8, 256), F32),
    gate=((T, CH), BF16),
    dproj=((T, 1408), BF16),
    state=((NST, CH), F32),
    ggo=((8, CH), F32),
    gsk=((8, CH), F32),
    gdt=((8, 128), F32),
    gdl=((8, 128), F32),
    tapx=((5, 8, CH), F32),
    tapbc=((5, 8, 256), F32),
    gi1=((8, D), F32),
    pack=((2, 16, CH), F32),
    pack_in=((10, 16, CH), F32),
    bcs=((2, 64, 128), F32),
    bcs_in=((4, 64, 128), F32),
    los=((2, ROWS, D), BF16),
    igs=((2, ROWS, D), F32),
)
SAVED = dict(
    n=((T, D), BF16),
    px=((T + 8, CH), F32),
    cx=((T, CH), F32),
    pz=((T, CH), F32),
    pbc=((T + 8, 256), F32),
    cbc=((T, 256), F32),
    v=((T, 128), F32),
    y=((T, CH), F32),
    h=((NB, NST, CH), BF16),
)
LINKS = dict(
    early=(2, 3),
    toks=(2, 3),
    halves=(1,),
    params=(1,),
    g_first=(2, 3),
    g_second=(2, 4, 3),
    g_twin=(2, 4, 4),
    p0=(NB, 3),
    sq0=(NB, 3),
    hids=(NB, 3),
    sq1=(NB, 3),
    dn1=(NB, 3),
    gbs=(NB, 3),
    in0=(NB, 3),
    p1=(3,),
    dn0=(3,),
    d_twin=(2, 4),
    d_first=(2, 4, 3),
    d_second=(2, 3),
    shard=(1,),
    small=(10,),
    bcx=(3,),
    outs=(2,),
)
INPUTS = (
    "gain_in", "weight_x", "weight_z", "weight_bc", "weight_dt", "conv_x", "conv_bc", "bias_x", "bias_bc", "dt_bias",
    "decay_log", "skip_gain", "gain_out", "weight_out", "lens", "tokens", "cot",
)
OUTPUTS = ("lo", "ig", "shard_out", "small_out")


class Names:
    def __init__(self, **kw):
        self.__dict__.update(kw)


def layer_kernel(*refs):
    names = list(INPUTS) + list(OUTPUTS) + list(SCRATCH)
    names += [f"{n}{k}" for k in range(2) for n in SAVED]
    k_ = Names(**dict(zip(names, refs)))
    rest = refs[len(names) :]
    lsem = rest[0]
    links = Names(**{n: Link(rest[1 + 2 * i], rest[2 + 2 * i]) for i, n in enumerate(LINKS)})
    saved = [Names(**{n: getattr(k_, f"{n}{k}") for n in SAVED}) for k in range(2)]
    walls = (k_.wall0, k_.wall1)
    s, z, y, t = places()
    own_d = z * 4 + y
    a1 = (1 - s) * y + s * z
    a2 = (1 - s) * z + s * y

    def index(first, second):
        return (1 - s) * (4 * second + first) + s * (4 * first + second)

    def first_peer(j):
        return {"dp": index(lax.rem(a1 + j, 4), a2)}

    def second_peer(j):
        return {"dp": index(a1, lax.rem(a2 + j, 4))}

    def x_of(j):
        return lax.rem(t + j, 4)

    my_half = span(HALF * s, HALF)
    twin_half = span(HALF * (1 - s), HALF)

    greet(
        [x_peer(j) for j in ORDER]
        + [first_peer(j) for j in ORDER]
        + [second_peer(j) for j in ORDER]
        + [twin()]
    )

    k_.par_own[...] = jnp.zeros((16, CH), F32)
    k_.par_own[0:4, :] = k_.conv_x[0]
    k_.par_own[4:5, :] = k_.bias_x[...]
    k_.par_own[5:6, :] = k_.gain_out[...]
    k_.par_own[6:7, :] = k_.gain_in[:, 0:CH]
    k_.par_own[7:8, :] = k_.gain_in[:, CH:D]
    k_.par_own[8:9, 0:8] = k_.dt_bias[...]
    k_.par_own[8:9, 128:136] = k_.decay_log[...]
    k_.par_own[8:9, 256:264] = k_.skip_gain[...]
    k_.par_own[9:13, 0:64] = k_.conv_bc[0]
    k_.par_own[13:14, 0:64] = k_.bias_bc[...]
    k_.bc_in[0] = jnp.zeros((64, 128), BF16)
    k_.bc_in[0, :, 0:64] = k_.weight_bc[0]
    for i, j in enumerate(ORDER):
        links.early.start(k_.bc_in.at[0], k_.bc_in.at[j], (0, i), x_peer(j))
        links.early.start(k_.par_own, k_.par_in.at[j], (1, i), x_peer(j))
    rows_t = span(t * ROWS, ROWS)
    for i, j in enumerate(ORDER):
        links.toks.start(k_.tokens.at[s], k_.tok.at[rows_t], (0, i), x_peer(j))
    local_tok = pltpu.make_async_copy(k_.tokens.at[s], k_.tok.at[rows_t], lsem.at[0])
    local_cot = pltpu.make_async_copy(k_.cot.at[s], k_.gb1.at[rows_t], lsem.at[1])
    local_tok.start()
    local_cot.start()
    k_.own[:, X0:Z0] = k_.weight_x[0]
    k_.own[:, Z0:O0] = k_.weight_z[0]
    k_.own[:, O0:B0] = k_.weight_out[0].T
    k_.own[:, S0:COLS] = jnp.zeros((64, 128), BF16)
    k_.own[:, S0 : S0 + 8] = k_.weight_dt[0]
    k_.par_in[0] = k_.par_own[...]
    for i, j in enumerate(ORDER):
        links.early.arrived(k_.bc_in.at[0], (0, i))
        links.early.arrived(k_.par_own, (1, i))
    left = iota((64, 128), 1) < 64
    lanes16 = iota((16, 128), 1)
    row16 = iota((16, 128), 0)
    bc_rows = (row16 >= 9) & (row16 < 14)
    slots = [lax.rem(t - i + 4, 4) for i in range(4)]
    for i in range(2):
        right = pltpu.roll(k_.bc_in[slots[2 * i + 1]].astype(F32), 64, 1)
        k_.own[:, B0 + 128 * i : B0 + 128 * i + 128] = jnp.where(
            left, k_.bc_in[slots[2 * i]].astype(F32), right
        ).astype(BF16)
        right = pltpu.roll(k_.par_in[slots[2 * i + 1], :, 0:128], 64, 1)
        pair = jnp.where(lanes16 < 64, k_.par_in[slots[2 * i], :, 0:128], right)
        cols = slice(128 * i, 128 * i + 128)
        k_.par_all[s, :, cols] = jnp.where(bc_rows, pair, k_.par_own[:, cols])
    k_.par_all[s, :, 256:512] = k_.par_own[:, 256:512]
    links.halves.start(k_.own.at[twin_half], k_.src.at[s], 0, twin())
    links.params.start(k_.par_all.at[s], k_.par_all.at[s], 0, twin())
    k_.src[s] = k_.own[my_half, :]
    links.halves.arrived(k_.src.at[0], 0)

    def gather_first(k):
        for i, j in enumerate(ORDER):
            links.g_first.start(k_.src.at[k], walls[k].at[own_d, my_half], (k, i), first_peer(j))
        walls[k][own_d, my_half, :] = k_.src[k]

    def gather_second(k):
        for r in (0,) + ORDER:
            piece = walls[k].at[index(lax.rem(a1 - r + 4, 4), a2), my_half]
            if r:
                links.g_first.arrived(piece, (k, ORDER.index(r)))
            for i, j in enumerate(ORDER):
                links.g_second.start(piece, piece, (k, r, i), second_peer(j))
            links.g_twin.start(piece, piece, (k, r, 0), twin())

    def gather_twin(k):
        for i, j in enumerate(ORDER):
            for r in (0,) + ORDER:
                piece = walls[k].at[index(lax.rem(a1 - r + 4, 4), lax.rem(a2 - j + 4, 4)), my_half]
                links.g_second.arrived(piece, (k, r, i))
                links.g_twin.start(piece, piece, (k, r, i + 1), twin())

    def gather_done(k):
        for r in range(4):
            for i in range(4):
                links.g_twin.arrived(walls[k].at[0, pl.ds(0, HALF)], (k, r, i))

    def gather_sent(k):
        for r in range(4):
            for i in range(3):
                links.g_second.sent(k_.src.at[0], (k, r, i))
            for i in range(4):
                links.g_twin.sent(k_.src.at[0], (k, r, i))

    gather_first(0)
    links.params.arrived(k_.par_all.at[0], 0)
    for i, j in enumerate(ORDER):
        links.toks.start(k_.cot.at[s], k_.gb1.at[rows_t], (1, i), x_peer(j))
    gather_second(0)

    length = k_.lens[pl.ds(s, 1), :]

    def row_mask(start, rows):
        return (iota((rows, 1), 0) + start < length).astype(F32)

    lower = iota((L, L), 0) >= iota((L, L), 1)
    tri = lower.astype(F32)
    off = jnp.where(lower, 0.0, -1e30)
    first_half = iota((L, 128), 1) < 64
    lanes = iota((L, 128), 1)

    def make_par(k):
        def par(row, start, size):
            return k_.par_all[k, row : row + 1, start : start + size]

        return par

    def weight(k, start, size):
        return walls[k][:, :, start : start + size].reshape(D, size)

    def forward_block(k, b):
        par, keep = make_par(k), saved[k]
        rows = span(b * L, L)
        spread = head_spread()
        rate = -jnp.exp(par(8, 128, 128))
        skip = mm_exact(jnp.broadcast_to(par(8, 256, 128), (8, 128)), spread.astype(F32))[0:1, :]
        n = keep.n[rows, :]
        k_.blkbc[0:8, :] = k_.blkbc[L : L + 8, :]
        k_.blkx[0:8, :] = k_.blkx[L : L + 8, :]
        k_.blkbc[8 : 8 + L, :] = mm(n, weight(k, B0, 256))
        v = mm(n, weight(k, S0, 128)) + par(8, 0, 128)
        keep.v[rows, :] = v
        for j in range(2):
            k_.blkx[8 : 8 + L, 256 * j : 256 * j + 256] = mm(n, weight(k, X0 + 256 * j, 256))
        for j in range(2):
            keep.pz[rows, 256 * j : 256 * j + 256] = mm(n, weight(k, Z0 + 256 * j, 256))
        shifted = pl.ds(pl.multiple_of(b * L + 8, 8), L)
        keep.px[shifted, :] = k_.blkx[8 : 8 + L, :]
        keep.pbc[shifted, :] = k_.blkbc[8 : 8 + L, :]
        for j in range(4):
            cols = slice(128 * j, 128 * j + 128)
            c = par(4, 128 * j, 128)
            for tap in range(4):
                c = c + par(tap, 128 * j, 128) * k_.blkx[5 + tap : 5 + tap + L, cols]
            keep.cx[rows, cols] = c
        for j in range(2):
            cols = slice(128 * j, 128 * j + 128)
            c = par(13, 128 * j, 128)
            for tap in range(4):
                c = c + par(9 + tap, 128 * j, 128) * k_.blkbc[5 + tap : 5 + tap + L, cols]
            keep.cbc[rows, cols] = c
        st = softplus(v)
        cu = mm_exact(tri, st * rate)
        cut = cu.T
        ea = jnp.exp(cu)
        tail = jnp.exp(cu[L - 1 : L, :] - cu)
        st_e = mm_split(st, spread)
        ea_e = mm_split(ea, spread)
        tail_e = mm_split(tail, spread)
        cx = keep.cx[rows, :]
        xs = cx * jax.nn.sigmoid(cx)
        cbc = keep.cbc[rows, :]
        bc = (cbc * jax.nn.sigmoid(cbc)).astype(BF16)
        bb, cc = bc[:, :NST], bc[:, NST:]
        xd = xs * st_e
        h_in = k_.state[...].astype(BF16)
        keep.h[b] = h_in
        gram = mm(cc, bb, NT)
        yy = mm(cc, h_in) * ea_e
        k_.state[...] = k_.state[...] * ea_e[L - 1 : L, :] + mm(bb, (xd * tail_e).astype(BF16), TN)
        inside = []
        for pair in range(4):
            xp = xd[:, 128 * pair : 128 * pair + 128]
            parts, mixes = [], []
            for part in range(2):
                h = 2 * pair + part
                mixes.append((gram * jnp.exp(cu[:, h : h + 1] - cut[h : h + 1, :] + off)).astype(BF16))
                parts.append(jnp.where(first_half == (part == 0), xp, 0.0).astype(BF16))
            inside.append(mm(jnp.concatenate(mixes, axis=1), jnp.concatenate(parts, axis=0)))
        yy = yy + jnp.concatenate(inside, axis=1)
        keep.y[rows, :] = yy
        zz = keep.pz[rows, :]
        gated = (yy + xs * skip) * (zz * jax.nn.sigmoid(zz))
        k_.sq_tile[k, b, 0:1, :] = as_row(jnp.sum(gated * gated, axis=-1, keepdims=True))
        weighted = gated * par(5, 0, CH)
        k_.gate[rows, :] = weighted.astype(BF16)
        if k == 1:
            gb = (k_.gb1[rows, :].astype(F32) * row_mask(b * L, L)).astype(BF16)
            k_.gb1[rows, :] = gb
            dno = jnp.concatenate([mm(gb, weight(k, O0, 256)), mm(gb, weight(k, O0 + 256, 256))], axis=1)
            k_.dno[rows, :] = dno
            k_.sq_tile[k, b, 1:2, :] = as_row(jnp.sum(dno * weighted, axis=-1, keepdims=True))

    def norm_block(k, b, u):
        par = make_par(k)
        gain = jnp.concatenate([par(6, 0, CH), par(7, 0, CH)], axis=1)
        for i in range(4):
            part = span(b * L + 32 * i, 32)
            a = u[part, :].astype(F32)
            r = lax.rsqrt(jnp.mean(a * a, axis=-1, keepdims=True) + EPS)
            saved[k].n[part, :] = (a * r * gain).astype(BF16)

    def reset_forward(k):
        k_.blkx[...] = jnp.zeros((L + 8, CH), F32)
        k_.blkbc[...] = jnp.zeros((L + 8, 256), F32)
        saved[k].px[0:8, :] = jnp.zeros((8, CH), F32)
        saved[k].pbc[0:8, :] = jnp.zeros((8, 256), F32)
        k_.state[...] = jnp.zeros((NST, CH), F32)

    def output_rows(k, rows, dst):
        for j in range(4):
            wo = walls[k][4 * j : 4 * j + 4, :, O0 : O0 + CH].reshape(256, CH)
            dst[rows, 256 * j : 256 * j + 256] = mm(k_.gate[rows, :], wo, NT).astype(BF16)

    def slice_of(b, place):
        return span(b * L + place * HALF, HALF)

    def spread_slices(link, buf, into, b):
        for i, j in enumerate(ORDER):
            link.start(buf.at[slice_of(b, x_of(j))], into.at[b, j - 1], (b, i), x_peer(j))

    def spread_tile(link, k, b):
        for i, j in enumerate(ORDER):
            link.start(k_.sq_tile.at[k, b], k_.sq_in.at[k, b, j], (b, i), x_peer(j))

    def slice_sum(buf, into, b):
        total = buf[slice_of(b, t), :].astype(F32)
        for j in (1, 2, 3):
            total = total + into[b, j - 1].astype(F32)
        return total

    def tile_sum(link, k, b):
        for i, j in enumerate(ORDER):
            link.arrived(k_.sq_in.at[k, b, j], (b, i))
        k_.sums[k, b] = (
            k_.sq_tile[k, b] + k_.sq_in[k, b, 1] + k_.sq_in[k, b, 2] + k_.sq_in[k, b, 3]
        )

    def factor_column(k, b):
        return as_column(lax.rsqrt(k_.sums[k, b, 0:1, :] / INNER + EPS))

    def hidden_block(b):
        tile_sum(links.sq0, 0, b)
        for i, j in enumerate(ORDER):
            links.p0.arrived(k_.ra.at[b, j - 1], (b, i))
        k_.factors[...] = jnp.broadcast_to(factor_column(0, b), (ROWS, 128))
        factor = k_.factors[span(t * HALF, HALF), :][:, 0:1]
        total = slice_sum(k_.pa, k_.ra, b)
        k_.ptot0[b] = total
        rows = slice_of(b, t)
        mask = row_mask(b * L + t * HALF, HALF)
        k_.hid[rows, :] = (mask * (k_.tok[rows, :].astype(F32) + factor * total)).astype(BF16)
        for i, j in enumerate(ORDER):
            links.hids.start(k_.hid.at[rows], k_.hid.at[rows], (b, i), x_peer(j))

    for i, j in enumerate(ORDER):
        links.toks.arrived(k_.tok.at[rows_t], (0, i))
    local_tok.wait()
    for b in range(NB):
        norm_block(0, b, k_.tok)
    reset_forward(0)
    k_.sq_tile[...] = jnp.zeros((2, NB, 8, 128), F32)
    gather_twin(0)
    gather_done(0)
    gather_first(1)

    def first_forward(b, carry):
        pl.when(b == 1)(lambda: gather_second(1))
        pl.when(b >= 2)(lambda: hidden_block(b - 2))
        forward_block(0, b)
        spread_tile(links.sq0, 0, b)
        output_rows(0, span(b * L, L), k_.pa)
        spread_slices(links.p0, k_.pa, k_.ra, b)
        return carry

    lax.fori_loop(0, NB, first_forward, 0)

    gather_twin(1)
    for i, j in enumerate(ORDER):
        links.toks.arrived(k_.gb1.at[rows_t], (1, i))
    local_cot.wait()
    reset_forward(1)
    gather_done(1)

    def second_forward(b, carry):
        pl.when(b < 2)(lambda: hidden_block(b + 2))
        for i, j in enumerate(ORDER):
            links.hids.arrived(k_.hid.at[slice_of(b, 0)], (b, i))
        norm_block(1, b, k_.hid)
        forward_block(1, b)
        spread_tile(links.sq1, 1, b)
        return carry

    lax.fori_loop(0, NB, second_forward, 0)
    output_rows(1, pl.ds(0, T), k_.pb)

    upper_low = (iota((L, L), 1) >= iota((L, L), 0)).astype(BF16)
    strict = (iota((L, L), 1) < iota((L, L), 0)).astype(F32)
    strict_low = strict.astype(BF16)

    def reset_backward():
        k_.state[...] = jnp.zeros((NST, CH), F32)
        k_.ggo[...] = jnp.zeros((8, CH), F32)
        k_.gsk[...] = jnp.zeros((8, CH), F32)
        k_.gdt[...] = jnp.zeros((8, 128), F32)
        k_.gdl[...] = jnp.zeros((8, 128), F32)
        k_.tapx[...] = jnp.zeros((5, 8, CH), F32)
        k_.tapbc[...] = jnp.zeros((5, 8, 256), F32)
        k_.dcx[...] = jnp.zeros((L + 8, CH), F32)
        k_.dcbc[...] = jnp.zeros((L + 8, 256), F32)

    def backward_block(k, b, gb_ref, inner, dn_ref):
        par, keep = make_par(k), saved[k]
        rows = span(b * L, L)
        spread, collect = head_spread(), head_collect()
        rate = -jnp.exp(par(8, 128, 128))
        skip = mm_exact(jnp.broadcast_to(par(8, 256, 128), (8, 128)), spread.astype(F32))[0:1, :]
        gain_out = par(5, 0, CH)
        v = keep.v[rows, :]
        st = softplus(v)
        cu = mm_exact(tri, st * rate)
        cut = cu.T
        ea = jnp.exp(cu)
        tail = jnp.exp(cu[L - 1 : L, :] - cu)
        st_e = mm_split(st, spread)
        ea_e = mm_split(ea, spread)
        tail_e = mm_split(tail, spread)
        cx = keep.cx[rows, :]
        sx = jax.nn.sigmoid(cx)
        xs = cx * sx
        cbc = keep.cbc[rows, :]
        sbc = jax.nn.sigmoid(cbc)
        bc = (cbc * sbc).astype(BF16)
        bb, cc = bc[:, :NST], bc[:, NST:]
        xd = xs * st_e
        factor = factor_column(k, b)
        if k == 1:
            dno = k_.dno[rows, :]
        else:
            gb = gb_ref[rows, :]
            dno = jnp.concatenate([mm(gb, weight(k, O0, 256)), mm(gb, weight(k, O0 + 256, 256))], axis=1)
        out = keep.y[rows, :] + xs * skip
        zz = keep.pz[rows, :]
        sz = jax.nn.sigmoid(zz)
        silu_z = zz * sz
        gated = out * silu_z
        scaled = gated * factor
        k_.gate[rows, :] = (scaled * gain_out).astype(BF16)
        k_.ggo[...] += fold(dno * scaled)
        dgated = factor * (dno * gain_out) - gated * (factor * factor * factor * (1.0 / INNER) * inner)
        dy = dgated * silu_z
        k_.dproj[rows, Z0 : Z0 + CH] = (dgated * out * (sz * (1.0 + zz - silu_z))).astype(BF16)
        k_.gsk[...] += fold(dy * xs)
        h_in = keep.h[b]
        h_back = k_.state[...]
        hb_low = h_back.astype(BF16)
        gram = mm(cc, bb, NT)
        xdt = (xd * tail_e).astype(BF16)
        dye = (dy * ea_e).astype(BF16)
        y_in = mm(cc, h_in) * ea_e
        dxd_in = mm(bb, hb_low) * tail_e
        dcc = mm(dye, h_in, NT)
        dbb = mm(xdt, hb_low, NT)
        dgram = jnp.zeros((L, L), F32)
        inside = []
        crossing = jnp.zeros((L, 128), F32)
        for pair in range(4):
            sl = slice(128 * pair, 128 * pair + 128)
            xp = xd[:, sl].astype(BF16)
            dyp = dy[:, sl]
            decs, mixes, parts = [], [], []
            for part in range(2):
                h = 2 * pair + part
                dec = jnp.exp(cu[:, h : h + 1] - cut[h : h + 1, :] + off)
                decs.append(dec)
                mixes.append(gram * dec)
                parts.append(jnp.where(first_half == (part == 0), dyp, 0.0).astype(BF16))
            dy2 = jnp.concatenate(parts, axis=0)
            dmix = mm(dy2, xp, NT)
            dm0, dm1 = dmix[:L, :], dmix[L:, :]
            dgram = dgram + dm0 * decs[0] + dm1 * decs[1]
            inside.append(mm(jnp.concatenate([mixes[0].astype(BF16), mixes[1].astype(BF16)], axis=0), dy2, TN))
            both = jnp.concatenate([(mixes[0] * dm0).astype(BF16), (mixes[1] * dm1).astype(BF16)], axis=1)
            cross = mm(upper_low, both)
            c0 = (cross[:, :L] * strict).astype(BF16)
            c1 = (cross[:, L:] * strict).astype(BF16)
            pick = jnp.concatenate(
                [(lanes == 2 * pair).astype(BF16), (lanes == 2 * pair + 1).astype(BF16)], axis=0
            )
            crossing = crossing + mm(jnp.concatenate([c0, c1], axis=1), pick)
        dgl = dgram.astype(BF16)
        dcc = dcc + mm(dgl, bb)
        dbb = dbb + mm(dgl, cc, TN)
        dxd = jnp.concatenate(inside, axis=1) + dxd_in
        kept = mm_split(jnp.broadcast_to(jnp.sum(h_in.astype(F32) * h_back, axis=0, keepdims=True), (8, CH)), collect)
        kept = kept[0:1, :] * ea[L - 1 : L, :]
        p_in = mm_split(dy * y_in, collect)
        q_in = mm_split(xd * dxd_in, collect)
        dls = crossing + mm_split_right(upper_low, p_in) + mm_split_right(strict_low, q_in) + kept
        k_.state[...] = h_back * ea_e[L - 1 : L, :] + mm(cc, dye, TN)
        dst = dls * rate + mm_split(dxd * xs, collect)
        dv = jnp.where(lanes < 8, dst * jax.nn.sigmoid(v), 0.0)
        k_.dproj[rows, S0 - 512 : S0 - 384] = dv.astype(BF16)
        k_.gdt[...] += fold(dv)
        k_.gdl[...] += fold(dls * st)
        dxs = dy * skip + dxd * st_e
        k_.dcx[L : L + 8, :] = k_.dcx[0:8, :]
        k_.dcbc[L : L + 8, :] = k_.dcbc[0:8, :]
        k_.dcx[0:L, :] = dxs * (sx * (1.0 + cx - xs))
        k_.dcbc[0:L, :] = jnp.concatenate([dbb, dcc], axis=1) * (sbc * (1.0 + cbc - cbc * sbc))
        window = pl.ds(pl.multiple_of(b * L, 8), L + 8)
        k_.blkx[...] = keep.px[window, :]
        k_.blkbc[...] = keep.pbc[window, :]

        def conv_back(width, first_row, dc, blk, taps, start):
            for j in range(width // 128):
                cols = slice(128 * j, 128 * j + 128)
                d = dc[0:L, cols]
                taps[4, :, cols] += fold(d)
                total = jnp.zeros((L, 128), F32)
                for tap in range(4):
                    taps[tap, :, cols] += fold(d * blk[5 + tap : 5 + tap + L, cols])
                    total = total + par(first_row + tap, 128 * j, 128) * dc[3 - tap : 3 - tap + L, cols]
                k_.dproj[rows, start + 128 * j : start + 128 * j + 128] = total.astype(BF16)

        conv_back(CH, 0, k_.dcx, k_.blkx, k_.tapx, X0)
        conv_back(256, 9, k_.dcbc, k_.blkbc, k_.tapbc, B0 - 512)
        for j in range(4):
            wr = slice(4 * j, 4 * j + 4)
            d = mm(k_.dproj[rows, 0:1024], walls[k][wr, :, 0:1024].reshape(256, 1024), NT)
            d = d + mm(k_.dproj[rows, 1024:1408], walls[k][wr, :, B0:COLS].reshape(256, 384), NT)
            dn_ref[rows, 256 * j : 256 * j + 256] = d.astype(BF16)

    def small_grads(k):
        par = make_par(k)
        rate = -jnp.exp(par(8, 128, 128))
        k_.pack[k] = jnp.zeros((16, CH), F32)
        for tap in range(5):
            k_.pack[k, tap : tap + 1, :] = jnp.sum(k_.tapx[tap], axis=0, keepdims=True)
            k_.pack[k, 9 + tap : 10 + tap, 0:256] = jnp.sum(k_.tapbc[tap], axis=0, keepdims=True)
        k_.pack[k, 5:6, :] = jnp.sum(k_.ggo[...], axis=0, keepdims=True)
        k_.pack[k, 8:9, 0:128] = jnp.sum(k_.gdt[...], axis=0, keepdims=True)
        k_.pack[k, 8:9, 128:256] = jnp.sum(k_.gdl[...], axis=0, keepdims=True) * rate
        gs = mm_split(jnp.broadcast_to(jnp.sum(k_.gsk[...], axis=0, keepdims=True), (8, CH)), head_collect())
        k_.pack[k, 8:9, 256:384] = gs[0:1, :]

    def weight_grads(k, gb_ref, dst):
        for j in range(4):
            nt = saved[k].n[:, 256 * j : 256 * j + 256].T
            gt = gb_ref[:, 256 * j : 256 * j + 256].T
            wr = slice(4 * j, 4 * j + 4)

            def put(start, size, value):
                dst[wr, :, start : start + size] = value.astype(BF16).reshape(4, 64, size)

            for c in range(4):
                put(256 * c, 256, mm(nt, k_.dproj[:, 256 * c : 256 * c + 256]))
            put(B0, 256, mm(nt, k_.dproj[:, B0 - 512 : S0 - 512]))
            put(S0, 128, mm(nt, k_.dproj[:, S0 - 512 : COLS - 512]))
            for c in range(2):
                put(O0 + 256 * c, 256, mm(gt, k_.gate[:, 256 * c : 256 * c + 256]))
            links.d_twin.start(dst.at[wr, twin_half], k_.theirs.at[k, wr], (k, j), twin())

    def input_grad(k, total, u, upstream):
        par = make_par(k)
        gain = jnp.concatenate([par(6, 0, CH), par(7, 0, CH)], axis=1)
        r = lax.rsqrt(jnp.mean(u * u, axis=-1, keepdims=True) + EPS)
        c = total * gain
        back = upstream + r * c - u * (r * r * r * (1.0 / D)) * jnp.sum(c * u, axis=-1, keepdims=True)
        return back, fold(total * (u * r))

    def turn_block(b):
        for i, j in enumerate(ORDER):
            links.dn1.arrived(k_.rb.at[b, j - 1], (b, i))
        rows = slice_of(b, t)
        u = k_.hid[rows, :].astype(F32)
        back, gain_grad = input_grad(1, slice_sum(k_.pc, k_.rb, b), u, k_.gb1[rows, :].astype(F32))
        k_.gi1[...] += gain_grad
        low = (row_mask(b * L + t * HALF, HALF) * back).astype(BF16)
        k_.gb0[rows, :] = low
        inner = jnp.sum(low.astype(F32) * k_.ptot0[b], axis=-1, keepdims=True)
        k_.inner0[rows, :] = jnp.broadcast_to(inner, (HALF, 128))
        for i, j in enumerate(ORDER):
            links.gbs.start(k_.gb0.at[rows], k_.gb0.at[rows], (b, i), x_peer(j))
            links.in0.start(k_.inner0.at[rows], k_.inner0.at[rows], (b, i), x_peer(j))

    def owner_slices(link, buf, into):
        for i, j in enumerate(ORDER):
            link.start(buf.at[span(x_of(j) * ROWS, ROWS)], into.at[j - 1], i, x_peer(j))

    def reduce_first(k, dst):
        for j in range(4):
            links.d_twin.arrived(k_.theirs.at[k, 0:4], (k, j))

        def add(i, carry):
            dst[i, my_half, :] = (dst[i, my_half, :].astype(F32) + k_.theirs[k, i].astype(F32)).astype(BF16)
            return carry

        lax.fori_loop(0, 16, add, 0)
        for i, j in enumerate(ORDER):
            for r in range(4):
                piece = dst.at[index(lax.rem(a1 + j, 4), r), my_half]
                links.d_first.start(piece, k_.first_in.at[k, j - 1, r], (k, r, i), first_peer(j))

    def reduce_second(k, dst):
        for i, j in enumerate(ORDER):
            for r in range(4):
                links.d_first.arrived(k_.first_in.at[k, j - 1, r], (k, r, i))

        def add(r, carry):
            total = dst[index(a1, r), my_half, :].astype(F32)
            for j in (1, 2, 3):
                total = total + k_.first_in[k, j - 1, r].astype(F32)
            k_.mid[k, r] = total.astype(BF16)
            return carry

        lax.fori_loop(0, 4, add, 0)
        for i, j in enumerate(ORDER):
            links.d_second.start(k_.mid.at[k, lax.rem(a2 + j, 4)], k_.last_in.at[k, j], (k, i), second_peer(j))

    def reduce_last(k):
        for i, j in enumerate(ORDER):
            links.d_second.arrived(k_.last_in.at[k, j], (k, i))
        total = k_.mid[k, a2].astype(F32)
        for j in (1, 2, 3):
            total = total + k_.last_in[k, j].astype(F32)
        k_.half[k] = total

    reset_backward()
    k_.gi1[...] = jnp.zeros((8, D), F32)

    def second_backward(i, carry):
        b = NB - 1 - i
        tile_sum(links.sq1, 1, b)
        backward_block(1, b, k_.gb1, as_column(k_.sums[1, b, 1:2, :]), k_.pc)
        spread_slices(links.dn1, k_.pc, k_.rb, b)
        pl.when(i >= 2)(lambda: turn_block(b + 2))
        return carry

    lax.fori_loop(0, NB, second_backward, 0)
    small_grads(1)
    weight_grads(1, k_.gb1, k_.dw1)

    reset_backward()
    for b in range(NB):
        for i in range(3):
            links.p0.sent(k_.ra.at[0, 0], (b, i))

    def first_backward(i, carry):
        b = NB - 1 - i
        pl.when(i < 2)(lambda: turn_block(1 - i))
        pl.when(i == 1)(lambda: reduce_first(1, k_.dw1))
        pl.when(i == 3)(lambda: owner_slices(links.p1, k_.pb, k_.pb_in))
        for q in range(3):
            links.gbs.arrived(k_.gb0.at[slice_of(b, 0)], (b, q))
            links.in0.arrived(k_.inner0.at[slice_of(b, 0)], (b, q))
        inner = k_.inner0[span(b * L, L), :][:, 0:1]
        backward_block(0, b, k_.gb0, inner, k_.pa)
        return carry

    lax.fori_loop(0, NB, first_backward, 0)
    owner_slices(links.dn0, k_.pa, k_.pc_in)
    small_grads(0)
    gather_sent(1)
    weight_grads(0, k_.gb0, k_.wall1)

    reduce_second(1, k_.dw1)
    reduce_first(0, k_.wall1)
    for i, j in enumerate(ORDER):
        links.dn0.arrived(k_.pc_in.at[j - 1], i)
    total = k_.pa[rows_t, :].astype(F32)
    for j in (1, 2, 3):
        total = total + k_.pc_in[j - 1].astype(F32)
    grad, gain_grad = input_grad(0, total, k_.tok[rows_t, :].astype(F32), k_.gb0[rows_t, :].astype(F32))
    k_.igs[0] = grad
    k_.igs[1] = k_.gb0[rows_t, :].astype(F32)
    for k, part in ((0, gain_grad), (1, k_.gi1[...])):
        part = jnp.sum(part, axis=0, keepdims=True)
        k_.pack[k, 6:7, :] = part[:, 0:CH]
        k_.pack[k, 7:8, :] = part[:, CH:D]
    links.small.start(k_.pack.at[1 - s], k_.pack_in.at[0], 0, twin())
    for i, j in enumerate(ORDER):
        links.p1.arrived(k_.pb_in.at[j - 1], i)
    total = k_.pb[rows_t, :].astype(F32)
    for j in (1, 2, 3):
        total = total + k_.pb_in[j - 1].astype(F32)
    mask = row_mask(t * ROWS, ROWS)
    factor = factor_column(1, t)
    k_.los[0] = k_.hid[rows_t, :]
    k_.los[1] = (mask * (k_.hid[rows_t, :].astype(F32) + factor * total)).astype(BF16)
    links.outs.start(k_.los.at[1 - s], k_.lo.at[s], 0, twin())
    links.outs.start(k_.igs.at[1 - s], k_.ig.at[s], 1, twin())
    keep_lo = pltpu.make_async_copy(k_.los.at[s], k_.lo.at[s], lsem.at[2])
    keep_ig = pltpu.make_async_copy(k_.igs.at[s], k_.ig.at[s], lsem.at[3])
    keep_lo.start()
    keep_ig.start()
    reduce_last(1)
    links.small.arrived(k_.pack_in.at[0], 0)
    k_.par_in[0] = k_.pack[s] + k_.pack_in[0]
    for i, j in enumerate(ORDER):
        links.small.start(k_.par_in.at[0], k_.pack_in.at[j], 1 + i, first_peer(j))
    reduce_second(0, k_.wall1)

    def small_step(src, dst, first, peers):
        for i, j in enumerate(ORDER):
            links.small.arrived(k_.pack_in.at[j], first + i)
        k_.par_in[dst] = (
            k_.par_in[src] + k_.pack_in[first] + k_.pack_in[first + 1] + k_.pack_in[first + 2]
        )
        if peers is not None:
            for i, j in enumerate(ORDER):
                links.small.start(k_.par_in.at[dst], k_.pack_in.at[first + 2 + j], first + 3 + i, peers(j))

    small_step(0, 1, 1, second_peer)
    reduce_last(0)
    links.shard.start(k_.half.at[1 - s], k_.other_half, 0, twin())
    small_step(1, 2, 4, x_peer)
    links.shard.arrived(k_.other_half, 0)
    mine, others = k_.half[s], k_.other_half[...]
    k_.shard_out[my_half, :] = mine
    k_.shard_out[twin_half, :] = others
    for i in range(2):
        k_.bcs[i, my_half, :] = mine[:, B0 + 128 * i : B0 + 128 * i + 128]
        k_.bcs[i, twin_half, :] = others[:, B0 + 128 * i : B0 + 128 * i + 128]
    for i, j in enumerate(ORDER):
        links.bcx.start(k_.bcs.at[x_of(j) // 2], k_.bcs_in.at[j], i, x_peer(j))
    for i, j in enumerate(ORDER):
        links.small.arrived(k_.pack_in.at[j], 7 + i)
    over_x = k_.par_in[2] + k_.pack_in[7] + k_.pack_in[8] + k_.pack_in[9]
    row = iota((16, CH), 0)
    shared = (row == 6) | (row == 7) | (row >= 9)
    over_x = jnp.where(shared, over_x, k_.par_in[2])
    k_.small_out[...] = over_x
    chosen = over_x[8:16, 0:64]
    for i in range(1, 4):
        chosen = jnp.where(t == i, over_x[8:16, 64 * i : 64 * i + 64], chosen)
    k_.small_out[9:14, 0:64] = chosen[1:6, :]
    for i, j in enumerate(ORDER):
        links.bcx.arrived(k_.bcs_in.at[j], i)
    block = k_.bcs[t // 2] + k_.bcs_in[1] + k_.bcs_in[2] + k_.bcs_in[3]
    k_.shard_out[:, B0 : B0 + 64] = jnp.where(lax.rem(t, 2) == 0, block[:, 0:64], block[:, 64:128])

    keep_lo.wait()
    keep_ig.wait()
    links.outs.arrived(k_.los.at[0], 0)
    links.outs.arrived(k_.igs.at[0], 1)
    links.outs.sent(k_.los.at[0], 0)
    links.outs.sent(k_.igs.at[0], 1)
    links.halves.sent(k_.src.at[0], 0)
    links.params.sent(k_.par_all.at[0], 0)
    links.shard.sent(k_.other_half, 0)
    for i in range(10):
        links.small.sent(k_.par_in.at[0], i)
    for i in range(3):
        links.early.sent(k_.bc_in.at[0], (0, i))
        links.early.sent(k_.par_own, (1, i))
        links.toks.sent(k_.tok.at[rows_t], (0, i))
        links.toks.sent(k_.tok.at[rows_t], (1, i))
        links.p1.sent(k_.pb_in.at[0], i)
        links.dn0.sent(k_.pc_in.at[0], i)
        links.bcx.sent(k_.bcs.at[0], i)
        for k in range(2):
            links.g_first.sent(k_.src.at[0], (k, i))
            links.d_second.sent(k_.src.at[0], (k, i))
            for r in range(4):
                links.d_first.sent(k_.src.at[0], (k, r, i))
        for b in range(NB):
            links.sq0.sent(k_.sq_tile.at[0, 0], (b, i))
            links.sq1.sent(k_.sq_tile.at[0, 0], (b, i))
            links.hids.sent(k_.ra.at[0, 0], (b, i))
            links.dn1.sent(k_.ra.at[0, 0], (b, i))
            links.gbs.sent(k_.ra.at[0, 0], (b, i))
            links.in0.sent(k_.inner0.at[pl.ds(0, HALF)], (b, i))
    for k in range(2):
        for r in range(4):
            links.d_twin.sent(k_.theirs.at[0, 0:4], (k, r))
    gather_sent(0)


def unpack_kernel(
    shard, small, lo, ig,
    o_lo, o_ig, o_gi, o_wx, o_wz, o_bc, o_dt, o_cx, o_cb, o_bx, o_bb, o_db, o_dl, o_sk, o_go, o_wo,
):
    o_lo[...] = lo[...]
    o_ig[...] = ig[...]
    o_gi[:, 0:CH] = small[6:7, :]
    o_gi[:, CH:D] = small[7:8, :]
    o_wx[...] = shard[:, X0:Z0]
    o_wz[...] = shard[:, Z0:O0]
    o_bc[...] = shard[:, B0 : B0 + 64]
    o_dt[...] = shard[:, S0 : S0 + 8]
    part = shard[:, O0:B0]
    o_wo[...] = jnp.concatenate([part, part], axis=0).T[:, 0:64]
    o_cx[...] = small[0:4, :]
    o_bx[...] = small[4:5, :]
    o_go[...] = small[5:6, :]
    o_db[...] = small[8:9, 0:8]
    o_dl[...] = small[8:9, 128:136]
    o_sk[...] = small[8:9, 256:264]
    o_cb[...] = small[9:13, 0:64]
    o_bb[...] = small[13:14, 0:64]


def sds(shape, dtype):
    return jax.ShapeDtypeStruct(shape, dtype)


VM = pl.BlockSpec(memory_space=pltpu.VMEM)
ANY = pl.BlockSpec(memory_space=pl.ANY)


def body(
    tokens_in, cotangent, seq_lengths, gain_in, weight_x, weight_z, weight_bc, weight_dt, conv_x, conv_bc,
    bias_x, bias_bc, dt_bias, decay_log, skip_gain, gain_out, weight_out,
):
    ins = [
        gain_in, weight_x, weight_z, weight_bc, weight_dt, conv_x, conv_bc, bias_x, bias_bc, dt_bias, decay_log,
        skip_gain, gain_out, weight_out, seq_lengths, tokens_in, cotangent,
    ]
    scratch = [pltpu.VMEM(*a) for a in SCRATCH.values()]
    scratch += [pltpu.VMEM(*a) for _ in range(2) for a in SAVED.values()]
    scratch += [pltpu.SemaphoreType.DMA((4,))]
    for shape in LINKS.values():
        scratch += [pltpu.SemaphoreType.DMA(shape)] * 2
    lo, ig, shard, small = pl.pallas_call(
        layer_kernel,
        out_shape=[
            sds((2, ROWS, D), BF16),
            sds((2, ROWS, D), F32),
            sds((64, COLS), F32),
            sds((16, CH), F32),
        ],
        in_specs=[VM] * 15 + [ANY] * 2,
        out_specs=[ANY, ANY, VM, VM],
        scratch_shapes=scratch,
        compiler_params=pltpu.CompilerParams(collective_id=0, has_side_effects=True, vmem_limit_bytes=VMEM_LIMIT),
    )(*ins)
    shapes = [
        (2, ROWS, D), (2, ROWS, D), (1, D), (64, CH), (64, CH), (64, 64), (64, 8), (4, CH), (4, 64), (1, CH), (1, 64),
        (1, 8), (1, 8), (1, 8), (1, CH), (CH, 64),
    ]
    found = pl.pallas_call(
        unpack_kernel,
        out_shape=[sds(a, BF16 if i == 0 else F32) for i, a in enumerate(shapes)],
        in_specs=[VM] * 4,
        out_specs=[VM] * 16,
        compiler_params=pltpu.CompilerParams(vmem_limit_bytes=VMEM_LIMIT),
    )(shard, small, lo, ig)
    return tuple(a if i in (2, 9, 10, 11, 12, 13, 14) else a[None] for i, a in enumerate(found))


def solution(mesh):
    in_specs = (
        P(None, ("dp", "tensor"), None),
        P(None, ("dp", "tensor"), None),
        P(None, "dp"),
        P("section", None),
        P("section", "dp", "tensor"),
        P("section", "dp", "tensor"),
        P("section", "dp", "tensor"),
        P("section", "dp", "tensor"),
        P("section", None, "tensor"),
        P("section", None, "tensor"),
        P("section", "tensor"),
        P("section", "tensor"),
        P("section", "tensor"),
        P("section", "tensor"),
        P("section", "tensor"),
        P("section", "tensor"),
        P("section", "tensor", "dp"),
    )
    out_specs = (
        P("section", None, ("dp", "tensor"), None),
        P("section", None, ("dp", "tensor"), None),
        P("section", None),
        P("section", "dp", "tensor"),
        P("section", "dp", "tensor"),
        P("section", "dp", "tensor"),
        P("section", "dp", "tensor"),
        P("section", None, "tensor"),
        P("section", None, "tensor"),
        P("section", "tensor"),
        P("section", "tensor"),
        P("section", "tensor"),
        P("section", "tensor"),
        P("section", "tensor"),
        P("section", "tensor"),
        P("section", "tensor", "dp"),
    )
    return jax.shard_map(body, mesh=mesh, in_specs=in_specs, out_specs=out_specs, check_vma=False)
```

time: 1680 us -> 154 us (0.09); the launches traced: 1660 us -> 153 us
  waiting for transfers between devices: 523 us -> 0 us
  local copies, waits for them, and re-layouts: 377 us -> 7.4 us
  blocking collectives: 323 us -> 0 us
  matrix products: 221 us -> 0 us
  other arithmetic: 181 us -> 0 us
  Pallas kernels: 0 us -> 144 us
    reduce_scatter x15 -> x0, waiting for transfers between devices: 413 us -> none  [the longest x3 134 us: body(): lax.psum_scatter(big_grads[1].astype(jnp.bfloat16), 'dp', scatter_dimensi...]
    psum x8 -> x0, blocking collectives: 252 us -> none  [the longest x1 150 us: body(): gain_total = lax.psum(gain_sums, ('dp', 'tensor'))]
    dot_general x126 -> x0, matrix products: 221 us -> none  [the longest x24 76 us: block_step(): inside = jnp.einsum('hts,shp->thp', mixing, block_x, precision=highest)]
    dynamic_update_slice x36 -> x0, local copies, waits for them, and re-layouts: 218 us -> none  [scan_blocks(): _, outputs = lax.scan(jax.checkpoint(block_step), initial, grouped)]
    pallas_call x0 -> x2, Pallas kernels: none -> 144 us  [the longest x1 141 us: body(): pl.pallas_call(layer_kernel, out_shape=[sds((2, ROWS, D), BF16), sds((2,...]
    all_gather x9 -> x0, waiting for transfers between devices: 106 us -> none  [the longest x3 60.4 us: body(): pieces = lax.all_gather(normed, 'tensor', axis=0, tiled=True)]
    all_gather x5 -> x0, blocking collectives: 70.9 us -> none  [the longest x3 30.4 us: body(): both_bc = lax.all_gather(own_bc, 'tensor', axis=1, tiled=True)]
    reduce_sum x41 -> x0, other arithmetic: 66.5 us -> none  [the longest x6 18.3 us: causal_conv(): kernel[offset][None, :] * padded[offset:offset + signal.shape[0]]]
  transfers between devices with their start and end apart: 28 -> 0, of which waited for: 19 -> 0; matrix products, arithmetic and copies ran while one was open for 26% -> 0% of each run, Pallas kernels for 0% -> 0%
where the time goes in v2:
time: 154 us; the launch traced here: 153 us
  Pallas kernels  144 us (94%)
  local copies, waits for them, and re-layouts  7.4 us (5%)
    pallas_call x1, Pallas kernels, body(): pl.pallas_call(layer_kernel, out_shape=[sds((2, ROWS, D), BF16), sds((2,...  141 us
    unnamed x7, local copies, waits for them, and re-layouts  7.4 us

profile of v2, /device:TPU:1, one launch (start us, length us, event | category | flops | bytes accessed | tf_op | source)
XLA Modules:
  0.0 152.5 jit_solution(13961255966941090861)
XLA Ops:
  0.6 1.3 copy.35.refs_14_
  1.9 1.4 copy.33.refs_4_
  3.3 1.6 %copy.34.refs_13_ = bf16[1,512,64]{2,1,0:T(8,128)(2,1)} copy(bf16[1,512,64]{1,2,0:T(8,128)(2,1)} %param.33) | data formatting | bytes 131072 | tf_op args[16]
  4.9 141.5 %shard_map.288 = (bf16[2,128,1024]{2,1,0:T(8,128)(2,1)}, f32[2,128,1024]{2,1,0:T(8,128)}, f32[64,1920]{1,0:T(8,128)}, f32[16,512]{1,0:T(8,128)}) custom-call(f32[1,1024]{1,0:T(1,128)} %refs_0_.1, bf16[1,64,512]{2,1,0:T(8,128)(2,1)} %refs_1_.1, bf16[1,64,512]{2,1,0:T(8,128)(2,1)} %refs_2_.1, bf16[1,64,64]{2,1,0:T(8,128)(2,1)} %refs_3_.1, ...), custom_call_target="tpu_custom_call" | custom-call | tf_op jit(solution)/shard_map/pallas_call | solution.py:980
  146.4 3.0 %shard_map.289 = (bf16[2,128,1024]{2,1,0:T(8,128)(2,1)}, f32[2,128,1024]{2,1,0:T(8,128)}, f32[1,1024]{1,0:T(1,128)}, f32[64,512]{1,0:T(8,128)}, f32[64,512]{1,0:...) custom-call(f32[64,1920]{1,0:T(8,128)} %get-tuple-element.36.shard, ...), custom_call_target="tpu_custom_call" | custom-call | tf_op jit(solution)/shard_map/pallas_call | solution.py:997
  149.4 0.0 copy-start
  149.4 0.7 copy-done
  150.2 0.7 copy.36
  150.8 1.7 %copy.37 = f32[1,512,64]{1,2,0:T(8,128)} copy(f32[1,512,64]{2,1,0:T(8,128)} %bitcast.9) | data formatting | bytes 262144
Async XLA Ops:
  149.4 0.8 copy-start

commit v3 on v2

--- a/solution.py
+++ b/solution.py
@@ -15,7 +15,7 @@
 INNER = 2048
 NST = 128
 EPS = 1e-05
-X0, Z0, O0, B0, S0, COLS = 0, 512, 1024, 1536, 1792, 1920
+B0, S0, X0, Z0, O0, COLS = 0, 256, 384, 896, 1408, 1920
 VMEM_LIMIT = 60 * 2**20
 MESH = pl.DeviceIdType.MESH
 ROWS = 128
@@ -93,10 +93,12 @@
 
 
 def greet(peers):
-    barrier = pltpu.get_barrier_semaphore()
     for peer in peers:
-        pl.semaphore_signal(barrier, inc=1, device_id=peer, device_id_type=MESH)
-    pl.semaphore_wait(barrier, len(peers))
+        pl.semaphore_signal(pltpu.get_barrier_semaphore(), inc=1, device_id=peer, device_id_type=MESH)
+
+
+def greeted(peers):
+    pl.semaphore_wait(pltpu.get_barrier_semaphore(), len(peers))
 
 
 class Link:
@@ -134,10 +136,12 @@
     half=((2, HALF, COLS), F32),
     other_half=((HALF, COLS), F32),
     own=((64, COLS), BF16),
-    src=((2, HALF, COLS), BF16),
     bc_in=((4, 64, 128), BF16),
     par_own=((16, CH), F32),
-    par_in=((4, 16, CH), F32),
+    par_x=((8, 128), F32),
+    par_in=((4, 8, 128), F32),
+    run=((3, 16, CH), F32),
+    square=((128, 128), F32),
     par_all=((2, 16, CH), F32),
     tok=((T, D), BF16),
     hid=((T, D), BF16),
@@ -190,28 +194,27 @@
     h=((NB, NST, CH), BF16),
 )
 LINKS = dict(
-    early=(2, 3),
-    toks=(2, 3),
-    halves=(1,),
+    early=(2,),
+    toks=(2,),
     params=(1,),
-    g_first=(2, 3),
-    g_second=(2, 4, 3),
-    g_twin=(2, 4, 4),
-    p0=(NB, 3),
-    sq0=(NB, 3),
-    hids=(NB, 3),
-    sq1=(NB, 3),
-    dn1=(NB, 3),
-    gbs=(NB, 3),
-    in0=(NB, 3),
-    p1=(3,),
-    dn0=(3,),
-    d_twin=(2, 4),
-    d_first=(2, 4, 3),
-    d_second=(2, 3),
+    g_first=(2, 4),
+    g_second=(2, 3),
+    g_twin=(2,),
+    p0=(NB,),
+    sq0=(NB,),
+    hids=(NB,),
+    sq1=(NB,),
+    dn1=(NB,),
+    gbs=(NB,),
+    in0=(NB,),
+    p1=(1,),
+    dn0=(1,),
+    d_twin=(2,),
+    d_first=(2,),
+    d_second=(2,),
     shard=(1,),
-    small=(10,),
-    bcx=(3,),
+    small=(4,),
+    bcx=(1,),
     outs=(2,),
 )
 INPUTS = (
@@ -255,12 +258,15 @@
     my_half = span(HALF * s, HALF)
     twin_half = span(HALF * (1 - s), HALF)
 
-    greet(
-        [x_peer(j) for j in ORDER]
-        + [first_peer(j) for j in ORDER]
-        + [second_peer(j) for j in ORDER]
-        + [twin()]
-    )
+    def y_peer(j, section):
+        return {"section": section, "dp": z * 4 + lax.rem(y + j, 4)}
+
+    def z_peer(j, section):
+        return {"section": section, "dp": lax.rem(z + j, 4) * 4 + y}
+
+    everyone = [x_peer(j) for j in ORDER] + [twin()]
+    everyone += [peer(j, section) for peer in (y_peer, z_peer) for section in range(2) for j in ORDER]
+    greet(everyone)
 
     k_.par_own[...] = jnp.zeros((16, CH), F32)
     k_.par_own[0:4, :] = k_.conv_x[0]
@@ -271,89 +277,95 @@
     k_.par_own[8:9, 0:8] = k_.dt_bias[...]
     k_.par_own[8:9, 128:136] = k_.decay_log[...]
     k_.par_own[8:9, 256:264] = k_.skip_gain[...]
-    k_.par_own[9:13, 0:64] = k_.conv_bc[0]
-    k_.par_own[13:14, 0:64] = k_.bias_bc[...]
+    k_.par_x[...] = jnp.zeros((8, 128), F32)
+    k_.par_x[0:4, 0:64] = k_.conv_bc[0]
+    k_.par_x[4:5, 0:64] = k_.bias_bc[...]
+    k_.par_in[0] = k_.par_x[...]
     k_.bc_in[0] = jnp.zeros((64, 128), BF16)
     k_.bc_in[0, :, 0:64] = k_.weight_bc[0]
-    for i, j in enumerate(ORDER):
-        links.early.start(k_.bc_in.at[0], k_.bc_in.at[j], (0, i), x_peer(j))
-        links.early.start(k_.par_own, k_.par_in.at[j], (1, i), x_peer(j))
+    k_.own[:, X0:Z0] = k_.weight_x[0]
+    k_.own[:, Z0:O0] = k_.weight_z[0]
+    k_.own[:, O0:COLS] = k_.weight_out[0]
+    k_.square[...] = jnp.zeros((128, 128), F32)
+    k_.square[0:8, 0:64] = k_.weight_dt[0].astype(F32)
+    k_.own[:, S0:X0] = k_.square[...].T[0:64, :].astype(BF16)
     rows_t = span(t * ROWS, ROWS)
-    for i, j in enumerate(ORDER):
-        links.toks.start(k_.tokens.at[s], k_.tok.at[rows_t], (0, i), x_peer(j))
     local_tok = pltpu.make_async_copy(k_.tokens.at[s], k_.tok.at[rows_t], lsem.at[0])
     local_cot = pltpu.make_async_copy(k_.cot.at[s], k_.gb1.at[rows_t], lsem.at[1])
     local_tok.start()
     local_cot.start()
-    k_.own[:, X0:Z0] = k_.weight_x[0]
-    k_.own[:, Z0:O0] = k_.weight_z[0]
-    k_.own[:, O0:B0] = k_.weight_out[0].T
-    k_.own[:, S0:COLS] = jnp.zeros((64, 128), BF16)
-    k_.own[:, S0 : S0 + 8] = k_.weight_dt[0]
-    k_.par_in[0] = k_.par_own[...]
-    for i, j in enumerate(ORDER):
-        links.early.arrived(k_.bc_in.at[0], (0, i))
-        links.early.arrived(k_.par_own, (1, i))
+    greeted(everyone)
+    for j in ORDER:
+        links.early.start(k_.bc_in.at[0], k_.bc_in.at[j], 0, x_peer(j))
+        links.early.start(k_.par_x, k_.par_in.at[j], 1, x_peer(j))
+
+    def shard_to_all(k, start, size):
+        def part(half):
+            rows = pl.ds(half * HALF, HALF)
+            return k_.own.at[rows, pl.ds(start, size)], walls[k].at[own_d, rows, pl.ds(start, size)]
+
+        for half, peer in enumerate((y_peer, z_peer)):
+            for i, j in enumerate(ORDER):
+                links.g_first.start(*part(half), (k, i), peer(j, half))
+        links.g_first.start(*part(1 - k), (k, 3), twin())
+        rows = pl.ds(k * HALF, HALF)
+        walls[k][own_d, rows, pl.ds(start, size)] = k_.own[rows, pl.ds(start, size)]
+
+    pl.when(s == 0)(lambda: shard_to_all(0, X0, COLS - X0))
+    links.early.arrived(k_.bc_in.at[pl.ds(1, 3)], 0)
+    links.early.arrived(k_.par_in.at[pl.ds(1, 3)], 1)
     left = iota((64, 128), 1) < 64
-    lanes16 = iota((16, 128), 1)
-    row16 = iota((16, 128), 0)
-    bc_rows = (row16 >= 9) & (row16 < 14)
+    left8 = iota((8, 128), 1) < 64
     slots = [lax.rem(t - i + 4, 4) for i in range(4)]
     for i in range(2):
+        cols = slice(128 * i, 128 * i + 128)
         right = pltpu.roll(k_.bc_in[slots[2 * i + 1]].astype(F32), 64, 1)
-        k_.own[:, B0 + 128 * i : B0 + 128 * i + 128] = jnp.where(
-            left, k_.bc_in[slots[2 * i]].astype(F32), right
-        ).astype(BF16)
-        right = pltpu.roll(k_.par_in[slots[2 * i + 1], :, 0:128], 64, 1)
-        pair = jnp.where(lanes16 < 64, k_.par_in[slots[2 * i], :, 0:128], right)
-        cols = slice(128 * i, 128 * i + 128)
-        k_.par_all[s, :, cols] = jnp.where(bc_rows, pair, k_.par_own[:, cols])
-    k_.par_all[s, :, 256:512] = k_.par_own[:, 256:512]
-    links.halves.start(k_.own.at[twin_half], k_.src.at[s], 0, twin())
-    links.params.start(k_.par_all.at[s], k_.par_all.at[s], 0, twin())
-    k_.src[s] = k_.own[my_half, :]
-    links.halves.arrived(k_.src.at[0], 0)
+        k_.own[:, cols] = jnp.where(left, k_.bc_in[slots[2 * i]].astype(F32), right).astype(BF16)
+        right = pltpu.roll(k_.par_in[slots[2 * i + 1]], 64, 1)
+        k_.par_own[9:14, cols] = jnp.where(left8, k_.par_in[slots[2 * i]], right)[0:5, :]
+    pl.when(s == 0)(lambda: shard_to_all(0, B0, X0))
+    k_.par_all[s] = k_.par_own[...]
+    links.params.start(k_.par_own, k_.par_all.at[s], 0, twin())
+    for j in ORDER:
+        links.toks.start(k_.tokens.at[s], k_.tok.at[rows_t], 0, x_peer(j))
 
     def gather_first(k):
-        for i, j in enumerate(ORDER):
-            links.g_first.start(k_.src.at[k], walls[k].at[own_d, my_half], (k, i), first_peer(j))
-        walls[k][own_d, my_half, :] = k_.src[k]
+        pl.when(s == k)(lambda: shard_to_all(k, 0, COLS))
 
     def gather_second(k):
         for r in (0,) + ORDER:
             piece = walls[k].at[index(lax.rem(a1 - r + 4, 4), a2), my_half]
             if r:
                 links.g_first.arrived(piece, (k, ORDER.index(r)))
+            else:
+                pl.when(s != k)(lambda: links.g_first.arrived(piece, (k, 3)))
             for i, j in enumerate(ORDER):
-                links.g_second.start(piece, piece, (k, r, i), second_peer(j))
-            links.g_twin.start(piece, piece, (k, r, 0), twin())
-
-    def gather_twin(k):
+                links.g_second.start(piece, piece, (k, i), second_peer(j))
+            links.g_twin.start(piece, piece, k, twin())
+
+    def gather_twin(k, between=None):
         for i, j in enumerate(ORDER):
+            links.g_second.arrived(k_.mid.at[0], (k, i))
             for r in (0,) + ORDER:
                 piece = walls[k].at[index(lax.rem(a1 - r + 4, 4), lax.rem(a2 - j + 4, 4)), my_half]
-                links.g_second.arrived(piece, (k, r, i))
-                links.g_twin.start(piece, piece, (k, r, i + 1), twin())
+                links.g_twin.start(piece, piece, k, twin())
+            if i == 1 and between is not None:
+                between()
 
     def gather_done(k):
-        for r in range(4):
-            for i in range(4):
-                links.g_twin.arrived(walls[k].at[0, pl.ds(0, HALF)], (k, r, i))
+        links.g_twin.arrived(k_.theirs.at[0], k)
 
     def gather_sent(k):
-        for r in range(4):
-            for i in range(3):
-                links.g_second.sent(k_.src.at[0], (k, r, i))
-            for i in range(4):
-                links.g_twin.sent(k_.src.at[0], (k, r, i))
-
-    gather_first(0)
-    links.params.arrived(k_.par_all.at[0], 0)
-    for i, j in enumerate(ORDER):
-        links.toks.start(k_.cot.at[s], k_.gb1.at[rows_t], (1, i), x_peer(j))
+        for i in range(3):
+            links.g_second.sent(k_.mid.at[0], (k, i))
+        links.g_twin.sent(k_.theirs.at[0], k)
+
+    links.params.arrived(k_.par_own, 0)
     gather_second(0)
-
-    length = k_.lens[pl.ds(s, 1), :]
+    for j in ORDER:
+        links.toks.start(k_.cot.at[s], k_.gb1.at[rows_t], 1, x_peer(j))
+
+    length = jnp.where(s == 0, k_.lens[:, 0:1], k_.lens[:, 1:2])
 
     def row_mask(start, rows):
         return (iota((rows, 1), 0) + start < length).astype(F32)
@@ -471,12 +483,12 @@
         return span(b * L + place * HALF, HALF)
 
     def spread_slices(link, buf, into, b):
-        for i, j in enumerate(ORDER):
-            link.start(buf.at[slice_of(b, x_of(j))], into.at[b, j - 1], (b, i), x_peer(j))
+        for j in ORDER:
+            link.start(buf.at[slice_of(b, x_of(j))], into.at[b, j - 1], b, x_peer(j))
 
     def spread_tile(link, k, b):
-        for i, j in enumerate(ORDER):
-            link.start(k_.sq_tile.at[k, b], k_.sq_in.at[k, b, j], (b, i), x_peer(j))
+        for j in ORDER:
+            link.start(k_.sq_tile.at[k, b], k_.sq_in.at[k, b, j], b, x_peer(j))
 
     def slice_sum(buf, into, b):
         total = buf[slice_of(b, t), :].astype(F32)
@@ -485,8 +497,7 @@
         return total
 
     def tile_sum(link, k, b):
-        for i, j in enumerate(ORDER):
-            link.arrived(k_.sq_in.at[k, b, j], (b, i))
+        link.arrived(k_.sq_in.at[k, b, pl.ds(1, 3)], b)
         k_.sums[k, b] = (
             k_.sq_tile[k, b] + k_.sq_in[k, b, 1] + k_.sq_in[k, b, 2] + k_.sq_in[k, b, 3]
         )
@@ -496,8 +507,7 @@
 
     def hidden_block(b):
         tile_sum(links.sq0, 0, b)
-        for i, j in enumerate(ORDER):
-            links.p0.arrived(k_.ra.at[b, j - 1], (b, i))
+        links.p0.arrived(k_.ra.at[b], b)
         k_.factors[...] = jnp.broadcast_to(factor_column(0, b), (ROWS, 128))
         factor = k_.factors[span(t * HALF, HALF), :][:, 0:1]
         total = slice_sum(k_.pa, k_.ra, b)
@@ -505,19 +515,17 @@
         rows = slice_of(b, t)
         mask = row_mask(b * L + t * HALF, HALF)
         k_.hid[rows, :] = (mask * (k_.tok[rows, :].astype(F32) + factor * total)).astype(BF16)
-        for i, j in enumerate(ORDER):
-            links.hids.start(k_.hid.at[rows], k_.hid.at[rows], (b, i), x_peer(j))
-
-    for i, j in enumerate(ORDER):
-        links.toks.arrived(k_.tok.at[rows_t], (0, i))
+        for j in ORDER:
+            links.hids.start(k_.hid.at[rows], k_.hid.at[rows], b, x_peer(j))
+
+    links.toks.arrived(k_.tok.at[pl.ds(0, 3 * ROWS)], 0)
     local_tok.wait()
     for b in range(NB):
         norm_block(0, b, k_.tok)
     reset_forward(0)
     k_.sq_tile[...] = jnp.zeros((2, NB, 8, 128), F32)
-    gather_twin(0)
+    gather_twin(0, lambda: gather_first(1))
     gather_done(0)
-    gather_first(1)
 
     def first_forward(b, carry):
         pl.when(b == 1)(lambda: gather_second(1))
@@ -531,16 +539,14 @@
     lax.fori_loop(0, NB, first_forward, 0)
 
     gather_twin(1)
-    for i, j in enumerate(ORDER):
-        links.toks.arrived(k_.gb1.at[rows_t], (1, i))
+    links.toks.arrived(k_.tok.at[pl.ds(0, 3 * ROWS)], 1)
     local_cot.wait()
     reset_forward(1)
     gather_done(1)
 
     def second_forward(b, carry):
         pl.when(b < 2)(lambda: hidden_block(b + 2))
-        for i, j in enumerate(ORDER):
-            links.hids.arrived(k_.hid.at[slice_of(b, 0)], (b, i))
+        links.hids.arrived(k_.ra.at[b], b)
         norm_block(1, b, k_.hid)
         forward_block(1, b)
         spread_tile(links.sq1, 1, b)
@@ -655,7 +661,7 @@
         k_.state[...] = h_back * ea_e[L - 1 : L, :] + mm(cc, dye, TN)
         dst = dls * rate + mm_split(dxd * xs, collect)
         dv = jnp.where(lanes < 8, dst * jax.nn.sigmoid(v), 0.0)
-        k_.dproj[rows, S0 - 512 : S0 - 384] = dv.astype(BF16)
+        k_.dproj[rows, S0:X0] = dv.astype(BF16)
         k_.gdt[...] += fold(dv)
         k_.gdl[...] += fold(dls * st)
         dxs = dy * skip + dxd * st_e
@@ -679,11 +685,10 @@
                 k_.dproj[rows, start + 128 * j : start + 128 * j + 128] = total.astype(BF16)
 
         conv_back(CH, 0, k_.dcx, k_.blkx, k_.tapx, X0)
-        conv_back(256, 9, k_.dcbc, k_.blkbc, k_.tapbc, B0 - 512)
+        conv_back(256, 9, k_.dcbc, k_.blkbc, k_.tapbc, B0)
         for j in range(4):
             wr = slice(4 * j, 4 * j + 4)
-            d = mm(k_.dproj[rows, 0:1024], walls[k][wr, :, 0:1024].reshape(256, 1024), NT)
-            d = d + mm(k_.dproj[rows, 1024:1408], walls[k][wr, :, B0:COLS].reshape(256, 384), NT)
+            d = mm(k_.dproj[rows, :], walls[k][wr, :, 0:O0].reshape(256, O0), NT)
             dn_ref[rows, 256 * j : 256 * j + 256] = d.astype(BF16)
 
     def small_grads(k):
@@ -708,13 +713,12 @@
             def put(start, size, value):
                 dst[wr, :, start : start + size] = value.astype(BF16).reshape(4, 64, size)
 
-            for c in range(4):
-                put(256 * c, 256, mm(nt, k_.dproj[:, 256 * c : 256 * c + 256]))
-            put(B0, 256, mm(nt, k_.dproj[:, B0 - 512 : S0 - 512]))
-            put(S0, 128, mm(nt, k_.dproj[:, S0 - 512 : COLS - 512]))
+            for c in range(0, O0, 256):
+                size = min(256, O0 - c)
+                put(c, size, mm(nt, k_.dproj[:, c : c + size]))
             for c in range(2):
                 put(O0 + 256 * c, 256, mm(gt, k_.gate[:, 256 * c : 256 * c + 256]))
-            links.d_twin.start(dst.at[wr, twin_half], k_.theirs.at[k, wr], (k, j), twin())
+            links.d_twin.start(dst.at[wr, twin_half], k_.theirs.at[k, wr], k, twin())
 
     def input_grad(k, total, u, upstream):
         par = make_par(k)
@@ -725,8 +729,7 @@
         return back, fold(total * (u * r))
 
     def turn_block(b):
-        for i, j in enumerate(ORDER):
-            links.dn1.arrived(k_.rb.at[b, j - 1], (b, i))
+        links.dn1.arrived(k_.rb.at[b], b)
         rows = slice_of(b, t)
         u = k_.hid[rows, :].astype(F32)
         back, gain_grad = input_grad(1, slice_sum(k_.pc, k_.rb, b), u, k_.gb1[rows, :].astype(F32))
@@ -735,32 +738,29 @@
         k_.gb0[rows, :] = low
         inner = jnp.sum(low.astype(F32) * k_.ptot0[b], axis=-1, keepdims=True)
         k_.inner0[rows, :] = jnp.broadcast_to(inner, (HALF, 128))
-        for i, j in enumerate(ORDER):
-            links.gbs.start(k_.gb0.at[rows], k_.gb0.at[rows], (b, i), x_peer(j))
-            links.in0.start(k_.inner0.at[rows], k_.inner0.at[rows], (b, i), x_peer(j))
+        for j in ORDER:
+            links.gbs.start(k_.gb0.at[rows], k_.gb0.at[rows], b, x_peer(j))
+            links.in0.start(k_.inner0.at[rows], k_.inner0.at[rows], b, x_peer(j))
 
     def owner_slices(link, buf, into):
-        for i, j in enumerate(ORDER):
-            link.start(buf.at[span(x_of(j) * ROWS, ROWS)], into.at[j - 1], i, x_peer(j))
+        for j in ORDER:
+            link.start(buf.at[span(x_of(j) * ROWS, ROWS)], into.at[j - 1], 0, x_peer(j))
 
     def reduce_first(k, dst):
-        for j in range(4):
-            links.d_twin.arrived(k_.theirs.at[k, 0:4], (k, j))
+        links.d_twin.arrived(k_.theirs.at[k], k)
 
         def add(i, carry):
             dst[i, my_half, :] = (dst[i, my_half, :].astype(F32) + k_.theirs[k, i].astype(F32)).astype(BF16)
             return carry
 
         lax.fori_loop(0, 16, add, 0)
-        for i, j in enumerate(ORDER):
+        for j in ORDER:
             for r in range(4):
                 piece = dst.at[index(lax.rem(a1 + j, 4), r), my_half]
-                links.d_first.start(piece, k_.first_in.at[k, j - 1, r], (k, r, i), first_peer(j))
+                links.d_first.start(piece, k_.first_in.at[k, j - 1, r], k, first_peer(j))
 
     def reduce_second(k, dst):
-        for i, j in enumerate(ORDER):
-            for r in range(4):
-                links.d_first.arrived(k_.first_in.at[k, j - 1, r], (k, r, i))
+        links.d_first.arrived(k_.first_in.at[k], k)
 
         def add(r, carry):
             total = dst[index(a1, r), my_half, :].astype(F32)
@@ -770,12 +770,11 @@
             return carry
 
         lax.fori_loop(0, 4, add, 0)
-        for i, j in enumerate(ORDER):
-            links.d_second.start(k_.mid.at[k, lax.rem(a2 + j, 4)], k_.last_in.at[k, j], (k, i), second_peer(j))
+        for j in ORDER:
+            links.d_second.start(k_.mid.at[k, lax.rem(a2 + j, 4)], k_.last_in.at[k, j], k, second_peer(j))
 
     def reduce_last(k):
-        for i, j in enumerate(ORDER):
-            links.d_second.arrived(k_.last_in.at[k, j], (k, i))
+        links.d_second.arrived(k_.last_in.at[k, pl.ds(1, 3)], k)
         total = k_.mid[k, a2].astype(F32)
         for j in (1, 2, 3):
             total = total + k_.last_in[k, j].astype(F32)
@@ -798,17 +797,15 @@
 
     reset_backward()
     for b in range(NB):
-        for i in range(3):
-            links.p0.sent(k_.ra.at[0, 0], (b, i))
+        links.p0.sent(k_.ra.at[b], b)
 
     def first_backward(i, carry):
         b = NB - 1 - i
         pl.when(i < 2)(lambda: turn_block(1 - i))
         pl.when(i == 1)(lambda: reduce_first(1, k_.dw1))
         pl.when(i == 3)(lambda: owner_slices(links.p1, k_.pb, k_.pb_in))
-        for q in range(3):
-            links.gbs.arrived(k_.gb0.at[slice_of(b, 0)], (b, q))
-            links.in0.arrived(k_.inner0.at[slice_of(b, 0)], (b, q))
+        links.gbs.arrived(k_.ra.at[b], b)
+        links.in0.arrived(k_.inner0.at[pl.ds(0, 3 * HALF)], b)
         inner = k_.inner0[span(b * L, L), :][:, 0:1]
         backward_block(0, b, k_.gb0, inner, k_.pa)
         return carry
@@ -821,8 +818,7 @@
 
     reduce_second(1, k_.dw1)
     reduce_first(0, k_.wall1)
-    for i, j in enumerate(ORDER):
-        links.dn0.arrived(k_.pc_in.at[j - 1], i)
+    links.dn0.arrived(k_.pc_in, 0)
     total = k_.pa[rows_t, :].astype(F32)
     for j in (1, 2, 3):
         total = total + k_.pc_in[j - 1].astype(F32)
@@ -834,8 +830,7 @@
         k_.pack[k, 6:7, :] = part[:, 0:CH]
         k_.pack[k, 7:8, :] = part[:, CH:D]
     links.small.start(k_.pack.at[1 - s], k_.pack_in.at[0], 0, twin())
-    for i, j in enumerate(ORDER):
-        links.p1.arrived(k_.pb_in.at[j - 1], i)
+    links.p1.arrived(k_.pb_in, 0)
     total = k_.pb[rows_t, :].astype(F32)
     for j in (1, 2, 3):
         total = total + k_.pb_in[j - 1].astype(F32)
@@ -851,25 +846,24 @@
     keep_ig.start()
     reduce_last(1)
     links.small.arrived(k_.pack_in.at[0], 0)
-    k_.par_in[0] = k_.pack[s] + k_.pack_in[0]
-    for i, j in enumerate(ORDER):
-        links.small.start(k_.par_in.at[0], k_.pack_in.at[j], 1 + i, first_peer(j))
+    k_.run[0] = k_.pack[s] + k_.pack_in[0]
+    for j in ORDER:
+        links.small.start(k_.run.at[0], k_.pack_in.at[j], 1, first_peer(j))
     reduce_second(0, k_.wall1)
 
-    def small_step(src, dst, first, peers):
-        for i, j in enumerate(ORDER):
-            links.small.arrived(k_.pack_in.at[j], first + i)
-        k_.par_in[dst] = (
-            k_.par_in[src] + k_.pack_in[first] + k_.pack_in[first + 1] + k_.pack_in[first + 2]
+    def small_step(stage, peers):
+        first = 3 * stage - 2
+        links.small.arrived(k_.pack_in.at[pl.ds(first, 3)], stage)
+        k_.run[stage] = (
+            k_.run[stage - 1] + k_.pack_in[first] + k_.pack_in[first + 1] + k_.pack_in[first + 2]
         )
-        if peers is not None:
-            for i, j in enumerate(ORDER):
-                links.small.start(k_.par_in.at[dst], k_.pack_in.at[first + 2 + j], first + 3 + i, peers(j))
-
-    small_step(0, 1, 1, second_peer)
+        for j in ORDER:
+            links.small.start(k_.run.at[stage], k_.pack_in.at[first + 2 + j], stage + 1, peers(j))
+
+    small_step(1, second_peer)
     reduce_last(0)
     links.shard.start(k_.half.at[1 - s], k_.other_half, 0, twin())
-    small_step(1, 2, 4, x_peer)
+    small_step(2, x_peer)
     links.shard.arrived(k_.other_half, 0)
     mine, others = k_.half[s], k_.other_half[...]
     k_.shard_out[my_half, :] = mine
@@ -877,21 +871,19 @@
     for i in range(2):
         k_.bcs[i, my_half, :] = mine[:, B0 + 128 * i : B0 + 128 * i + 128]
         k_.bcs[i, twin_half, :] = others[:, B0 + 128 * i : B0 + 128 * i + 128]
-    for i, j in enumerate(ORDER):
-        links.bcx.start(k_.bcs.at[x_of(j) // 2], k_.bcs_in.at[j], i, x_peer(j))
-    for i, j in enumerate(ORDER):
-        links.small.arrived(k_.pack_in.at[j], 7 + i)
-    over_x = k_.par_in[2] + k_.pack_in[7] + k_.pack_in[8] + k_.pack_in[9]
+    for j in ORDER:
+        links.bcx.start(k_.bcs.at[x_of(j) // 2], k_.bcs_in.at[j], 0, x_peer(j))
+    links.small.arrived(k_.pack_in.at[pl.ds(7, 3)], 3)
+    over_x = k_.run[2] + k_.pack_in[7] + k_.pack_in[8] + k_.pack_in[9]
     row = iota((16, CH), 0)
     shared = (row == 6) | (row == 7) | (row >= 9)
-    over_x = jnp.where(shared, over_x, k_.par_in[2])
+    over_x = jnp.where(shared, over_x, k_.run[2])
     k_.small_out[...] = over_x
     chosen = over_x[8:16, 0:64]
     for i in range(1, 4):
         chosen = jnp.where(t == i, over_x[8:16, 64 * i : 64 * i + 64], chosen)
     k_.small_out[9:14, 0:64] = chosen[1:6, :]
-    for i, j in enumerate(ORDER):
-        links.bcx.arrived(k_.bcs_in.at[j], i)
+    links.bcx.arrived(k_.bcs_in.at[pl.ds(1, 3)], 0)
     block = k_.bcs[t // 2] + k_.bcs_in[1] + k_.bcs_in[2] + k_.bcs_in[3]
     k_.shard_out[:, B0 : B0 + 64] = jnp.where(lax.rem(t, 2) == 0, block[:, 0:64], block[:, 64:128])
 
@@ -901,35 +893,37 @@
     links.outs.arrived(k_.igs.at[0], 1)
     links.outs.sent(k_.los.at[0], 0)
     links.outs.sent(k_.igs.at[0], 1)
-    links.halves.sent(k_.src.at[0], 0)
-    links.params.sent(k_.par_all.at[0], 0)
+    links.params.sent(k_.par_own, 0)
     links.shard.sent(k_.other_half, 0)
-    for i in range(10):
-        links.small.sent(k_.par_in.at[0], i)
-    for i in range(3):
-        links.early.sent(k_.bc_in.at[0], (0, i))
-        links.early.sent(k_.par_own, (1, i))
-        links.toks.sent(k_.tok.at[rows_t], (0, i))
-        links.toks.sent(k_.tok.at[rows_t], (1, i))
-        links.p1.sent(k_.pb_in.at[0], i)
-        links.dn0.sent(k_.pc_in.at[0], i)
-        links.bcx.sent(k_.bcs.at[0], i)
-        for k in range(2):
-            links.g_first.sent(k_.src.at[0], (k, i))
-            links.d_second.sent(k_.src.at[0], (k, i))
-            for r in range(4):
-                links.d_first.sent(k_.src.at[0], (k, r, i))
-        for b in range(NB):
-            links.sq0.sent(k_.sq_tile.at[0, 0], (b, i))
-            links.sq1.sent(k_.sq_tile.at[0, 0], (b, i))
-            links.hids.sent(k_.ra.at[0, 0], (b, i))
-            links.dn1.sent(k_.ra.at[0, 0], (b, i))
-            links.gbs.sent(k_.ra.at[0, 0], (b, i))
-            links.in0.sent(k_.inner0.at[pl.ds(0, HALF)], (b, i))
+    links.small.sent(k_.run.at[0], 0)
+    for i in range(1, 4):
+        links.small.sent(k_.run, i)
+    links.early.sent(k_.bc_in.at[pl.ds(1, 3)], 0)
+    links.early.sent(k_.par_in.at[pl.ds(1, 3)], 1)
+    links.toks.sent(k_.tok.at[pl.ds(0, 3 * ROWS)], 0)
+    links.toks.sent(k_.tok.at[pl.ds(0, 3 * ROWS)], 1)
+    links.p1.sent(k_.pb_in, 0)
+    links.dn0.sent(k_.pc_in, 0)
+    links.bcx.sent(k_.bcs_in.at[pl.ds(1, 3)], 0)
+    gather_sent(0)
+
+    def shard_sent(k):
+        for i in range(3):
+            links.g_first.sent(k_.mid.at[0, pl.ds(0, 2)], (k, i))
+        links.g_first.sent(k_.mid.at[0, 0], (k, 3))
+
     for k in range(2):
-        for r in range(4):
-            links.d_twin.sent(k_.theirs.at[0, 0:4], (k, r))
-    gather_sent(0)
+        pl.when(s == k)(lambda: shard_sent(k))
+        links.d_twin.sent(k_.theirs.at[k], k)
+        links.d_first.sent(k_.first_in.at[k], k)
+        links.d_second.sent(k_.last_in.at[k, pl.ds(1, 3)], k)
+    for b in range(NB):
+        links.sq0.sent(k_.sq_in.at[0, b, pl.ds(1, 3)], b)
+        links.sq1.sent(k_.sq_in.at[1, b, pl.ds(1, 3)], b)
+        links.hids.sent(k_.ra.at[b], b)
+        links.dn1.sent(k_.rb.at[b], b)
+        links.gbs.sent(k_.ra.at[b], b)
+        links.in0.sent(k_.inner0.at[pl.ds(0, 3 * HALF)], b)
 
 
 def unpack_kernel(
@@ -943,9 +937,9 @@
     o_wx[...] = shard[:, X0:Z0]
     o_wz[...] = shard[:, Z0:O0]
     o_bc[...] = shard[:, B0 : B0 + 64]
-    o_dt[...] = shard[:, S0 : S0 + 8]
-    part = shard[:, O0:B0]
-    o_wo[...] = jnp.concatenate([part, part], axis=0).T[:, 0:64]
+    steps = shard[:, S0:X0]
+    o_dt[...] = jnp.concatenate([steps, steps], axis=0).T[0:8, 0:64]
+    o_wo[...] = shard[:, O0:COLS]
     o_cx[...] = small[0:4, :]
     o_bx[...] = small[4:5, :]
     o_go[...] = small[5:6, :]
@@ -969,8 +963,8 @@
     bias_x, bias_bc, dt_bias, decay_log, skip_gain, gain_out, weight_out,
 ):
     ins = [
-        gain_in, weight_x, weight_z, weight_bc, weight_dt, conv_x, conv_bc, bias_x, bias_bc, dt_bias, decay_log,
-        skip_gain, gain_out, weight_out, seq_lengths, tokens_in, cotangent,
+        gain_in, weight_x, weight_z, weight_bc, weight_dt.swapaxes(1, 2), conv_x, conv_bc, bias_x, bias_bc, dt_bias,
+        decay_log, skip_gain, gain_out, weight_out.swapaxes(1, 2), seq_lengths.T, tokens_in, cotangent,
     ]
     scratch = [pltpu.VMEM(*a) for a in SCRATCH.values()]
     scratch += [pltpu.VMEM(*a) for _ in range(2) for a in SAVED.values()]
@@ -991,8 +985,8 @@
         compiler_params=pltpu.CompilerParams(collective_id=0, has_side_effects=True, vmem_limit_bytes=VMEM_LIMIT),
     )(*ins)
     shapes = [
-        (2, ROWS, D), (2, ROWS, D), (1, D), (64, CH), (64, CH), (64, 64), (64, 8), (4, CH), (4, 64), (1, CH), (1, 64),
-        (1, 8), (1, 8), (1, 8), (1, CH), (CH, 64),
+        (2, ROWS, D), (2, ROWS, D), (1, D), (64, CH), (64, CH), (64, 64), (8, 64), (4, CH), (4, 64), (1, CH), (1, 64),
+        (1, 8), (1, 8), (1, 8), (1, CH), (64, CH),
     ]
     found = pl.pallas_call(
         unpack_kernel,
@@ -1001,6 +995,9 @@
         out_specs=[VM] * 16,
         compiler_params=pltpu.CompilerParams(vmem_limit_bytes=VMEM_LIMIT),
     )(shard, small, lo, ig)
+    found = list(found)
+    found[6] = found[6].T
+    found[15] = found[15].T
     return tuple(a if i in (2, 9, 10, 11, 12, 13, 14) else a[None] for i, a in enumerate(found))
 
 

time: 154 us -> 141 us (0.916)
  local copies, waits for them, and re-layouts: 7.4 us -> 0 us
  Pallas kernels: 144 us -> 140 us
    unnamed x7 -> x0, local copies, waits for them, and re-layouts: 7.4 us -> none
    pallas_call x1, Pallas kernels: 141 us -> 137 us  [body(): pl.pallas_call(layer_kernel, out_shape=[sds((2, ROWS, D), BF16), sds((2,...]
where the time goes in v3:
time: 141 us
  Pallas kernels  140 us (99%)
    pallas_call x1, Pallas kernels, body(): pl.pallas_call(layer_kernel, out_shape=[sds((2, ROWS, D), BF16), sds((2,...  137 us
    pallas_call x1, Pallas kernels, body(): pl.pallas_call(unpack_kernel, out_shape=[sds(a, BF16 if i == 0 else F32)...  2.95 us

profile of v3, /device:TPU:1, one launch (start us, length us, event | category | flops | bytes accessed | tf_op | source)
XLA Modules:
  0.0 140.5 jit_solution(7184924611960728895)
XLA Ops:
  0.7 136.8 %shard_map.288 = (bf16[2,128,1024]{2,1,0:T(8,128)(2,1)}, f32[2,128,1024]{2,1,0:T(8,128)}, f32[64,1920]{1,0:T(8,128)}, f32[16,512]{1,0:T(8,128)}) custom-call(f32[1,1024]{1,0:T(1,128)} %refs_0_.1, bf16[1,64,512]{2,1,0:T(8,128)(2,1)} %refs_1_.1, bf16[1,64,512]{2,1,0:T(8,128)(2,1)} %refs_2_.1, bf16[1,64,64]{2,1,0:T(8,128)(2,1)} %refs_3_.1, ...), custom_call_target="tpu_custom_call" | custom-call | tf_op jit(solution)/shard_map/pallas_call | solution.py:974
  137.5 2.9 %shard_map.289 = (bf16[2,128,1024]{2,1,0:T(8,128)(2,1)}, f32[2,128,1024]{2,1,0:T(8,128)}, f32[1,1024]{1,0:T(1,128)}, f32[64,512]{1,0:T(8,128)}, f32[64,512]{1,0:...) custom-call(f32[64,1920]{1,0:T(8,128)} %get-tuple-element.36.shard, ...), custom_call_target="tpu_custom_call" | custom-call | tf_op jit(solution)/shard_map/pallas_call | solution.py:991

commit v4 on v3

--- a/solution.py
+++ b/solution.py
@@ -152,13 +152,13 @@
     pc=((T, D), BF16),
     ra=((NB, 3, HALF, D), BF16),
     rb=((NB, 3, HALF, D), BF16),
-    pb_in=((3, ROWS, D), BF16),
-    pc_in=((3, ROWS, D), BF16),
+    p1_in=((3, ROWS, D), BF16),
+    dn0_in=((3, ROWS, D), BF16),
     ptot0=((NB, HALF, D), F32),
     sq_tile=((2, NB, 8, 128), F32),
     sq_in=((2, NB, 4, 8, 128), F32),
     sums=((2, NB, 8, 128), F32),
-    inner0=((T, 128), F32),
+    inner_in=((NB, 4, 8, 128), F32),
     factors=((ROWS, 128), F32),
     dno=((T, CH), F32),
     blkx=((L + 8, CH), F32),
@@ -174,11 +174,10 @@
     gdl=((8, 128), F32),
     tapx=((5, 8, CH), F32),
     tapbc=((5, 8, 256), F32),
-    gi1=((8, D), F32),
+    gi=((2, 8, D), F32),
     pack=((2, 16, CH), F32),
     pack_in=((10, 16, CH), F32),
-    bcs=((2, 64, 128), F32),
-    bcs_in=((4, 64, 128), F32),
+    bc_last=((2, 4, 4, HALF, 128), BF16),
     los=((2, ROWS, D), BF16),
     igs=((2, ROWS, D), F32),
 )
@@ -195,11 +194,12 @@
 )
 LINKS = dict(
     early=(2,),
-    toks=(2,),
+    rows1=(2, 2),
+    rows2=(2,),
     params=(1,),
-    g_first=(2, 4),
-    g_second=(2, 3),
-    g_twin=(2,),
+    g_first=(4, 4),
+    g_second=(4, 3),
+    g_twin=(4,),
     p0=(NB,),
     sq0=(NB,),
     hids=(NB,),
@@ -209,14 +209,16 @@
     in0=(NB,),
     p1=(1,),
     dn0=(1,),
-    d_twin=(2,),
-    d_first=(2,),
-    d_second=(2,),
+    d_twin=(2, 2),
+    d_first=(2, 2),
+    d_second=(2, 2),
     shard=(1,),
     small=(4,),
-    bcx=(1,),
+    bcx=(2,),
     outs=(2,),
 )
+GROUPS = ((0, X0, O0 - X0), (0, B0, X0), (0, O0, COLS - O0), (1, 0, COLS))
+PARTS = (((Z0, COLS - Z0), (0, Z0)), ((0, COLS),))
 INPUTS = (
     "gain_in", "weight_x", "weight_z", "weight_bc", "weight_dt", "conv_x", "conv_bc", "bias_x", "bias_bc", "dt_bias",
     "decay_log", "skip_gain", "gain_out", "weight_out", "lens", "tokens", "cot",
@@ -266,6 +268,7 @@
 
     everyone = [x_peer(j) for j in ORDER] + [twin()]
     everyone += [peer(j, section) for peer in (y_peer, z_peer) for section in range(2) for j in ORDER]
+    everyone += [{"dp": index(a1, lax.rem(a2 + j, 4)), "tensor": x_of(i)} for j in ORDER for i in ORDER]
     greet(everyone)
 
     k_.par_own[...] = jnp.zeros((16, CH), F32)
@@ -299,19 +302,69 @@
         links.early.start(k_.bc_in.at[0], k_.bc_in.at[j], 0, x_peer(j))
         links.early.start(k_.par_x, k_.par_in.at[j], 1, x_peer(j))
 
-    def shard_to_all(k, start, size):
+    def shard_to_all(group):
+        k, start, size = GROUPS[group]
+        cols = pl.ds(start, size)
+
         def part(half):
             rows = pl.ds(half * HALF, HALF)
-            return k_.own.at[rows, pl.ds(start, size)], walls[k].at[own_d, rows, pl.ds(start, size)]
+            return k_.own.at[rows, cols], walls[k].at[own_d, rows, cols]
 
         for half, peer in enumerate((y_peer, z_peer)):
             for i, j in enumerate(ORDER):
-                links.g_first.start(*part(half), (k, i), peer(j, half))
-        links.g_first.start(*part(1 - k), (k, 3), twin())
+                links.g_first.start(*part(half), (group, i), peer(j, half))
+        links.g_first.start(*part(1 - k), (group, 3), twin())
         rows = pl.ds(k * HALF, HALF)
-        walls[k][own_d, rows, pl.ds(start, size)] = k_.own[rows, pl.ds(start, size)]
-
-    pl.when(s == 0)(lambda: shard_to_all(0, X0, COLS - X0))
+        walls[k][own_d, rows, cols] = k_.own[rows, cols]
+
+    def gather_first(group):
+        pl.when(s == GROUPS[group][0])(lambda: shard_to_all(group))
+
+    def gather_second(group):
+        k, start, size = GROUPS[group]
+        for r in (0,) + ORDER:
+            piece = walls[k].at[index(lax.rem(a1 - r + 4, 4), a2), my_half, pl.ds(start, size)]
+            if r:
+                links.g_first.arrived(piece, (group, ORDER.index(r)))
+            else:
+                pl.when(s != k)(lambda: links.g_first.arrived(piece, (group, 3)))
+            for i, j in enumerate(ORDER):
+                links.g_second.start(piece, piece, (group, i), second_peer(j))
+            links.g_twin.start(piece, piece, group, twin())
+
+    def gather_twin(group):
+        k, start, size = GROUPS[group]
+        for i, j in enumerate(ORDER):
+            links.g_second.arrived(k_.mid.at[0, :, :, pl.ds(start, size)], (group, i))
+            for r in (0,) + ORDER:
+                place = index(lax.rem(a1 - r + 4, 4), lax.rem(a2 - j + 4, 4))
+                piece = walls[k].at[place, my_half, pl.ds(start, size)]
+                links.g_twin.start(piece, piece, group, twin())
+
+    def gather_done(group):
+        links.g_twin.arrived(k_.theirs.at[0, :, :, pl.ds(*GROUPS[group][1:])], group)
+
+    def gather_sent(group):
+        cols = pl.ds(*GROUPS[group][1:])
+        for i in range(3):
+            links.g_second.sent(k_.mid.at[0, :, :, cols], (group, i))
+        links.g_twin.sent(k_.theirs.at[0, :, :, cols], group)
+
+    def rows_first(a, src, dst):
+        links.rows1.start(src.at[s], dst.at[rows_t], (a, 0), x_peer(1))
+        links.rows1.start(src.at[s], dst.at[rows_t], (a, 1), x_peer(3))
+
+    def rows_second(a, dst):
+        links.rows1.arrived(dst.at[rows_t], (a, 0))
+        upper = dst.at[span(x_of(3) * ROWS, ROWS // 2)]
+        links.rows2.start(upper, upper, a, x_peer(1))
+        links.rows1.arrived(dst.at[rows_t], (a, 1))
+        lower_rows = dst.at[span(x_of(1) * ROWS + ROWS // 2, ROWS // 2)]
+        links.rows2.start(lower_rows, lower_rows, a, x_peer(3))
+
+    gather_first(0)
+    rows_first(0, k_.tokens, k_.tok)
+    gather_second(0)
     links.early.arrived(k_.bc_in.at[pl.ds(1, 3)], 0)
     links.early.arrived(k_.par_in.at[pl.ds(1, 3)], 1)
     left = iota((64, 128), 1) < 64
@@ -323,47 +376,14 @@
         k_.own[:, cols] = jnp.where(left, k_.bc_in[slots[2 * i]].astype(F32), right).astype(BF16)
         right = pltpu.roll(k_.par_in[slots[2 * i + 1]], 64, 1)
         k_.par_own[9:14, cols] = jnp.where(left8, k_.par_in[slots[2 * i]], right)[0:5, :]
-    pl.when(s == 0)(lambda: shard_to_all(0, B0, X0))
+    gather_first(1)
+    gather_first(2)
     k_.par_all[s] = k_.par_own[...]
     links.params.start(k_.par_own, k_.par_all.at[s], 0, twin())
-    for j in ORDER:
-        links.toks.start(k_.tokens.at[s], k_.tok.at[rows_t], 0, x_peer(j))
-
-    def gather_first(k):
-        pl.when(s == k)(lambda: shard_to_all(k, 0, COLS))
-
-    def gather_second(k):
-        for r in (0,) + ORDER:
-            piece = walls[k].at[index(lax.rem(a1 - r + 4, 4), a2), my_half]
-            if r:
-                links.g_first.arrived(piece, (k, ORDER.index(r)))
-            else:
-                pl.when(s != k)(lambda: links.g_first.arrived(piece, (k, 3)))
-            for i, j in enumerate(ORDER):
-                links.g_second.start(piece, piece, (k, i), second_peer(j))
-            links.g_twin.start(piece, piece, k, twin())
-
-    def gather_twin(k, between=None):
-        for i, j in enumerate(ORDER):
-            links.g_second.arrived(k_.mid.at[0], (k, i))
-            for r in (0,) + ORDER:
-                piece = walls[k].at[index(lax.rem(a1 - r + 4, 4), lax.rem(a2 - j + 4, 4)), my_half]
-                links.g_twin.start(piece, piece, k, twin())
-            if i == 1 and between is not None:
-                between()
-
-    def gather_done(k):
-        links.g_twin.arrived(k_.theirs.at[0], k)
-
-    def gather_sent(k):
-        for i in range(3):
-            links.g_second.sent(k_.mid.at[0], (k, i))
-        links.g_twin.sent(k_.theirs.at[0], k)
-
+    rows_second(0, k_.tok)
+    gather_second(1)
+    gather_second(2)
     links.params.arrived(k_.par_own, 0)
-    gather_second(0)
-    for j in ORDER:
-        links.toks.start(k_.cot.at[s], k_.gb1.at[rows_t], 1, x_peer(j))
 
     length = jnp.where(s == 0, k_.lens[:, 0:1], k_.lens[:, 1:2])
 
@@ -385,12 +405,9 @@
     def weight(k, start, size):
         return walls[k][:, :, start : start + size].reshape(D, size)
 
-    def forward_block(k, b):
+    def project_block(k, b):
         par, keep = make_par(k), saved[k]
         rows = span(b * L, L)
-        spread = head_spread()
-        rate = -jnp.exp(par(8, 128, 128))
-        skip = mm_exact(jnp.broadcast_to(par(8, 256, 128), (8, 128)), spread.astype(F32))[0:1, :]
         n = keep.n[rows, :]
         k_.blkbc[0:8, :] = k_.blkbc[L : L + 8, :]
         k_.blkx[0:8, :] = k_.blkx[L : L + 8, :]
@@ -416,7 +433,14 @@
             for tap in range(4):
                 c = c + par(9 + tap, 128 * j, 128) * k_.blkbc[5 + tap : 5 + tap + L, cols]
             keep.cbc[rows, cols] = c
-        st = softplus(v)
+
+    def forward_block(k, b):
+        par, keep = make_par(k), saved[k]
+        rows = span(b * L, L)
+        spread = head_spread()
+        rate = -jnp.exp(par(8, 128, 128))
+        skip = mm_exact(jnp.broadcast_to(par(8, 256, 128), (8, 128)), spread.astype(F32))[0:1, :]
+        st = softplus(keep.v[rows, :])
         cu = mm_exact(tri, st * rate)
         cut = cu.T
         ea = jnp.exp(cu)
@@ -486,15 +510,21 @@
         for j in ORDER:
             link.start(buf.at[slice_of(b, x_of(j))], into.at[b, j - 1], b, x_peer(j))
 
-    def spread_tile(link, k, b):
-        for j in ORDER:
-            link.start(k_.sq_tile.at[k, b], k_.sq_in.at[k, b, j], b, x_peer(j))
-
-    def slice_sum(buf, into, b):
+    def slice_sum(link, buf, into, b):
+        link.arrived(into.at[b], b)
         total = buf[slice_of(b, t), :].astype(F32)
         for j in (1, 2, 3):
             total = total + into[b, j - 1].astype(F32)
         return total
+
+    def share_slice(link, buf, b):
+        rows = buf.at[slice_of(b, t)]
+        for j in ORDER:
+            link.start(rows, rows, b, x_peer(j))
+
+    def spread_tile(link, k, b):
+        for j in ORDER:
+            link.start(k_.sq_tile.at[k, b], k_.sq_in.at[k, b, j], b, x_peer(j))
 
     def tile_sum(link, k, b):
         link.arrived(k_.sq_in.at[k, b, pl.ds(1, 3)], b)
@@ -507,47 +537,55 @@
 
     def hidden_block(b):
         tile_sum(links.sq0, 0, b)
-        links.p0.arrived(k_.ra.at[b], b)
         k_.factors[...] = jnp.broadcast_to(factor_column(0, b), (ROWS, 128))
         factor = k_.factors[span(t * HALF, HALF), :][:, 0:1]
-        total = slice_sum(k_.pa, k_.ra, b)
+        total = slice_sum(links.p0, k_.pa, k_.ra, b)
         k_.ptot0[b] = total
         rows = slice_of(b, t)
         mask = row_mask(b * L + t * HALF, HALF)
         k_.hid[rows, :] = (mask * (k_.tok[rows, :].astype(F32) + factor * total)).astype(BF16)
-        for j in ORDER:
-            links.hids.start(k_.hid.at[rows], k_.hid.at[rows], b, x_peer(j))
-
-    links.toks.arrived(k_.tok.at[pl.ds(0, 3 * ROWS)], 0)
+        share_slice(links.hids, k_.hid, b)
+
+    links.rows2.arrived(k_.tok.at[pl.ds(0, ROWS)], 0)
     local_tok.wait()
+    rows_first(1, k_.cot, k_.gb1)
     for b in range(NB):
         norm_block(0, b, k_.tok)
     reset_forward(0)
     k_.sq_tile[...] = jnp.zeros((2, NB, 8, 128), F32)
-    gather_twin(0, lambda: gather_first(1))
+    gather_first(3)
+    gather_twin(0)
+    gather_twin(1)
     gather_done(0)
+    gather_done(1)
 
     def first_forward(b, carry):
-        pl.when(b == 1)(lambda: gather_second(1))
+        project_block(0, b)
+        pl.when(b == 0)(lambda: gather_second(3))
+        pl.when(b == 0)(lambda: rows_second(1, k_.gb1))
         pl.when(b >= 2)(lambda: hidden_block(b - 2))
+        pl.when(b == 3)(lambda: gather_twin(3))
         forward_block(0, b)
+        pl.when(b == 0)(lambda: gather_twin(2))
         spread_tile(links.sq0, 0, b)
+        pl.when(b == 0)(lambda: gather_done(2))
         output_rows(0, span(b * L, L), k_.pa)
         spread_slices(links.p0, k_.pa, k_.ra, b)
         return carry
 
     lax.fori_loop(0, NB, first_forward, 0)
 
-    gather_twin(1)
-    links.toks.arrived(k_.tok.at[pl.ds(0, 3 * ROWS)], 1)
+    links.rows2.arrived(k_.tok.at[pl.ds(0, ROWS)], 1)
+    links.rows2.sent(k_.tok.at[pl.ds(0, ROWS)], 1)
     local_cot.wait()
     reset_forward(1)
-    gather_done(1)
+    gather_done(3)
 
     def second_forward(b, carry):
         pl.when(b < 2)(lambda: hidden_block(b + 2))
         links.hids.arrived(k_.ra.at[b], b)
         norm_block(1, b, k_.hid)
+        project_block(1, b)
         forward_block(1, b)
         spread_tile(links.sq1, 1, b)
         return carry
@@ -570,13 +608,45 @@
         k_.dcx[...] = jnp.zeros((L + 8, CH), F32)
         k_.dcbc[...] = jnp.zeros((L + 8, 256), F32)
 
-    def backward_block(k, b, gb_ref, inner, dn_ref):
+    def gate_back(k, b, inner, xs, skip):
+        par, keep = make_par(k), saved[k]
+        rows = span(b * L, L)
+        gain_out = par(5, 0, CH)
+        factor = factor_column(k, b)
+        if k == 1:
+            dno = k_.dno[rows, :]
+        else:
+            gb = k_.gb0[rows, :]
+            dno = jnp.concatenate([mm(gb, weight(k, O0, 256)), mm(gb, weight(k, O0 + 256, 256))], axis=1)
+        out = keep.y[rows, :] + xs * skip
+        zz = keep.pz[rows, :]
+        sz = jax.nn.sigmoid(zz)
+        silu_z = zz * sz
+        gated = out * silu_z
+        scaled = gated * factor
+        k_.gate[rows, :] = (scaled * gain_out).astype(BF16)
+        k_.ggo[...] += fold(dno * scaled)
+        dgated = factor * (dno * gain_out) - gated * (factor * factor * factor * (1.0 / INNER) * inner)
+        dy = dgated * silu_z
+        k_.dproj[rows, Z0 : Z0 + CH] = (dgated * out * (sz * (1.0 + zz - silu_z))).astype(BF16)
+        k_.gsk[...] += fold(dy * xs)
+        return dy
+
+    def skip_row(k):
+        skip = jnp.broadcast_to(make_par(k)(8, 256, 128), (8, 128))
+        return mm_exact(skip, head_spread().astype(F32))[0:1, :]
+
+    def gate_block(k, b, inner):
+        rows = span(b * L, L)
+        cx = saved[k].cx[rows, :]
+        k_.dno[rows, :] = gate_back(k, b, inner, cx * jax.nn.sigmoid(cx), skip_row(k))
+
+    def backward_block(k, b, inner, dn_ref, between):
         par, keep = make_par(k), saved[k]
         rows = span(b * L, L)
         spread, collect = head_spread(), head_collect()
         rate = -jnp.exp(par(8, 128, 128))
-        skip = mm_exact(jnp.broadcast_to(par(8, 256, 128), (8, 128)), spread.astype(F32))[0:1, :]
-        gain_out = par(5, 0, CH)
+        skip = skip_row(k)
         v = keep.v[rows, :]
         st = softplus(v)
         cu = mm_exact(tri, st * rate)
@@ -594,24 +664,7 @@
         bc = (cbc * sbc).astype(BF16)
         bb, cc = bc[:, :NST], bc[:, NST:]
         xd = xs * st_e
-        factor = factor_column(k, b)
-        if k == 1:
-            dno = k_.dno[rows, :]
-        else:
-            gb = gb_ref[rows, :]
-            dno = jnp.concatenate([mm(gb, weight(k, O0, 256)), mm(gb, weight(k, O0 + 256, 256))], axis=1)
-        out = keep.y[rows, :] + xs * skip
-        zz = keep.pz[rows, :]
-        sz = jax.nn.sigmoid(zz)
-        silu_z = zz * sz
-        gated = out * silu_z
-        scaled = gated * factor
-        k_.gate[rows, :] = (scaled * gain_out).astype(BF16)
-        k_.ggo[...] += fold(dno * scaled)
-        dgated = factor * (dno * gain_out) - gated * (factor * factor * factor * (1.0 / INNER) * inner)
-        dy = dgated * silu_z
-        k_.dproj[rows, Z0 : Z0 + CH] = (dgated * out * (sz * (1.0 + zz - silu_z))).astype(BF16)
-        k_.gsk[...] += fold(dy * xs)
+        dy = k_.dno[rows, :] if inner is None else gate_back(k, b, inner, xs, skip)
         h_in = keep.h[b]
         h_back = k_.state[...]
         hb_low = h_back.astype(BF16)
@@ -665,6 +718,7 @@
         k_.gdt[...] += fold(dv)
         k_.gdl[...] += fold(dls * st)
         dxs = dy * skip + dxd * st_e
+        between()
         k_.dcx[L : L + 8, :] = k_.dcx[0:8, :]
         k_.dcbc[L : L + 8, :] = k_.dcbc[0:8, :]
         k_.dcx[0:L, :] = dxs * (sx * (1.0 + cx - xs))
@@ -689,7 +743,9 @@
         for j in range(4):
             wr = slice(4 * j, 4 * j + 4)
             d = mm(k_.dproj[rows, :], walls[k][wr, :, 0:O0].reshape(256, O0), NT)
-            dn_ref[rows, 256 * j : 256 * j + 256] = d.astype(BF16)
+            cols = slice(256 * j, 256 * j + 256)
+            dn_ref[rows, cols] = d.astype(BF16)
+            k_.gi[k, :, cols] += fold(d * keep.n[rows, cols].astype(F32))
 
     def small_grads(k):
         par = make_par(k)
@@ -703,22 +759,28 @@
         k_.pack[k, 8:9, 128:256] = jnp.sum(k_.gdl[...], axis=0, keepdims=True) * rate
         gs = mm_split(jnp.broadcast_to(jnp.sum(k_.gsk[...], axis=0, keepdims=True), (8, CH)), head_collect())
         k_.pack[k, 8:9, 256:384] = gs[0:1, :]
-
-    def weight_grads(k, gb_ref, dst):
+        gi = jnp.sum(k_.gi[k], axis=0, keepdims=True)
+        k_.pack[k, 6:7, :] = gi[:, 0:CH] / par(6, 0, CH)
+        k_.pack[k, 7:8, :] = gi[:, CH:D] / par(7, 0, CH)
+
+    def weight_grads(k, part, gb_ref, dst):
+        start, size = PARTS[k][part]
         for j in range(4):
             nt = saved[k].n[:, 256 * j : 256 * j + 256].T
-            gt = gb_ref[:, 256 * j : 256 * j + 256].T
             wr = slice(4 * j, 4 * j + 4)
 
-            def put(start, size, value):
-                dst[wr, :, start : start + size] = value.astype(BF16).reshape(4, 64, size)
-
-            for c in range(0, O0, 256):
-                size = min(256, O0 - c)
-                put(c, size, mm(nt, k_.dproj[:, c : c + size]))
-            for c in range(2):
-                put(O0 + 256 * c, 256, mm(gt, k_.gate[:, 256 * c : 256 * c + 256]))
-            links.d_twin.start(dst.at[wr, twin_half], k_.theirs.at[k, wr], k, twin())
+            def put(c, value):
+                width = value.shape[1]
+                dst[wr, :, c : c + width] = value.astype(BF16).reshape(4, 64, width)
+
+            for c in range(start, min(start + size, O0), 256):
+                put(c, mm(nt, k_.dproj[:, c : min(c + 256, start + size, O0)]))
+            if start + size > O0:
+                gt = gb_ref[:, 256 * j : 256 * j + 256].T
+                for c in range(2):
+                    put(O0 + 256 * c, mm(gt, k_.gate[:, 256 * c : 256 * c + 256]))
+            cols = pl.ds(start, size)
+            links.d_twin.start(dst.at[wr, twin_half, cols], k_.theirs.at[k, wr, :, cols], (k, part), twin())
 
     def input_grad(k, total, u, upstream):
         par = make_par(k)
@@ -726,130 +788,170 @@
         r = lax.rsqrt(jnp.mean(u * u, axis=-1, keepdims=True) + EPS)
         c = total * gain
         back = upstream + r * c - u * (r * r * r * (1.0 / D)) * jnp.sum(c * u, axis=-1, keepdims=True)
-        return back, fold(total * (u * r))
+        return back
 
     def turn_block(b):
-        links.dn1.arrived(k_.rb.at[b], b)
         rows = slice_of(b, t)
         u = k_.hid[rows, :].astype(F32)
-        back, gain_grad = input_grad(1, slice_sum(k_.pc, k_.rb, b), u, k_.gb1[rows, :].astype(F32))
-        k_.gi1[...] += gain_grad
+        total = slice_sum(links.dn1, k_.pc, k_.rb, b)
+        back = input_grad(1, total, u, k_.gb1[rows, :].astype(F32))
         low = (row_mask(b * L + t * HALF, HALF) * back).astype(BF16)
         k_.gb0[rows, :] = low
+        share_slice(links.gbs, k_.gb0, b)
         inner = jnp.sum(low.astype(F32) * k_.ptot0[b], axis=-1, keepdims=True)
-        k_.inner0[rows, :] = jnp.broadcast_to(inner, (HALF, 128))
+        inner = jnp.broadcast_to(inner, (HALF, 128)).T[0:8, :]
+        k_.inner_in[b, t] = jnp.concatenate([inner, jnp.zeros((8, 128 - HALF), F32)], axis=1)
         for j in ORDER:
-            links.gbs.start(k_.gb0.at[rows], k_.gb0.at[rows], b, x_peer(j))
-            links.in0.start(k_.inner0.at[rows], k_.inner0.at[rows], b, x_peer(j))
-
-    def owner_slices(link, buf, into):
-        for j in ORDER:
-            link.start(buf.at[span(x_of(j) * ROWS, ROWS)], into.at[j - 1], 0, x_peer(j))
-
-    def reduce_first(k, dst):
-        links.d_twin.arrived(k_.theirs.at[k], k)
+            links.in0.start(k_.inner_in.at[b, t], k_.inner_in.at[b, t], b, x_peer(j))
+
+    def to_owner(b):
+        j = lax.rem(b - t + 4, 4)
+
+        def go():
+            links.dn0.start(k_.pa.at[span(b * L, L)], k_.dn0_in.at[j - 1], 0, {"tensor": b})
+
+        pl.when(j != 0)(go)
+
+    def reduce_first(k, part, dst):
+        cols = pl.ds(*PARTS[k][part])
+        links.d_twin.arrived(k_.theirs.at[k, :, :, cols], (k, part))
 
         def add(i, carry):
-            dst[i, my_half, :] = (dst[i, my_half, :].astype(F32) + k_.theirs[k, i].astype(F32)).astype(BF16)
+            dst[i, my_half, cols] = (
+                dst[i, my_half, cols].astype(F32) + k_.theirs[k, i, :, cols].astype(F32)
+            ).astype(BF16)
             return carry
 
         lax.fori_loop(0, 16, add, 0)
         for j in ORDER:
             for r in range(4):
-                piece = dst.at[index(lax.rem(a1 + j, 4), r), my_half]
-                links.d_first.start(piece, k_.first_in.at[k, j - 1, r], k, first_peer(j))
-
-    def reduce_second(k, dst):
-        links.d_first.arrived(k_.first_in.at[k], k)
+                piece = dst.at[index(lax.rem(a1 + j, 4), r), my_half, cols]
+                links.d_first.start(piece, k_.first_in.at[k, j - 1, r, :, cols], (k, part), first_peer(j))
+
+    def bc_direct(k):
+        for j in (0,) + ORDER:
+            for i in (0,) + ORDER:
+                place = lax.rem(a2 + j, 4)
+                block = k_.mid.at[k, place, :, span((x_of(i) // 2) * 128, 128)]
+                if (j, i) == (0, 0):
+                    k_.bc_last[k, 0, 0] = k_.mid[k, place, :, span((t // 2) * 128, 128)]
+                else:
+                    peer = {"dp": index(a1, place), "tensor": x_of(i)}
+                    links.bcx.start(block, k_.bc_last.at[k, j, i], k, peer)
+
+    def bc_sum(k):
+        links.bcx.arrived(k_.first_in.at[0, 0, 0, :, pl.ds(0, 15 * 128)], k)
+        total = jnp.zeros((HALF, 128), F32)
+        for j in range(4):
+            for i in range(4):
+                total = total + k_.bc_last[k, j, i].astype(F32)
+        k_.half[k, :, B0 : B0 + 64] = jnp.where(lax.rem(t, 2) == 0, total[:, 0:64], total[:, 64:128])
+
+    def reduce_second(k, part, dst):
+        cols = pl.ds(*PARTS[k][part])
+        links.d_first.arrived(k_.first_in.at[k, :, :, :, cols], (k, part))
 
         def add(r, carry):
-            total = dst[index(a1, r), my_half, :].astype(F32)
+            total = dst[index(a1, r), my_half, cols].astype(F32)
             for j in (1, 2, 3):
-                total = total + k_.first_in[k, j - 1, r].astype(F32)
-            k_.mid[k, r] = total.astype(BF16)
+                total = total + k_.first_in[k, j - 1, r, :, cols].astype(F32)
+            k_.mid[k, r, :, cols] = total.astype(BF16)
             return carry
 
         lax.fori_loop(0, 4, add, 0)
         for j in ORDER:
-            links.d_second.start(k_.mid.at[k, lax.rem(a2 + j, 4)], k_.last_in.at[k, j], k, second_peer(j))
-
-    def reduce_last(k):
-        links.d_second.arrived(k_.last_in.at[k, pl.ds(1, 3)], k)
-        total = k_.mid[k, a2].astype(F32)
+            piece = k_.mid.at[k, lax.rem(a2 + j, 4), :, cols]
+            links.d_second.start(piece, k_.last_in.at[k, j, :, cols], (k, part), second_peer(j))
+        if PARTS[k][part][0] == 0:
+            bc_direct(k)
+
+    def reduce_last(k, part):
+        cols = pl.ds(*PARTS[k][part])
+        links.d_second.arrived(k_.last_in.at[k, pl.ds(1, 3), :, cols], (k, part))
+        total = k_.mid[k, a2, :, cols].astype(F32)
         for j in (1, 2, 3):
-            total = total + k_.last_in[k, j].astype(F32)
-        k_.half[k] = total
+            total = total + k_.last_in[k, j, :, cols].astype(F32)
+        k_.half[k, :, cols] = total
+        if PARTS[k][part][0] == 0:
+            bc_sum(k)
 
     reset_backward()
-    k_.gi1[...] = jnp.zeros((8, D), F32)
+    k_.gi[...] = jnp.zeros((2, 8, D), F32)
+    for b in range(NB):
+        tile_sum(links.sq1, 1, b)
 
     def second_backward(i, carry):
         b = NB - 1 - i
-        tile_sum(links.sq1, 1, b)
-        backward_block(1, b, k_.gb1, as_column(k_.sums[1, b, 1:2, :]), k_.pc)
+        inner = as_column(k_.sums[1, b, 1:2, :])
+        backward_block(1, b, inner, k_.pc, lambda: pl.when(i >= 2)(lambda: turn_block(b + 2)))
         spread_slices(links.dn1, k_.pc, k_.rb, b)
-        pl.when(i >= 2)(lambda: turn_block(b + 2))
         return carry
 
     lax.fori_loop(0, NB, second_backward, 0)
     small_grads(1)
-    weight_grads(1, k_.gb1, k_.dw1)
+    weight_grads(1, 0, k_.gb1, k_.dw1)
+    turn_block(1)
 
     reset_backward()
     for b in range(NB):
         links.p0.sent(k_.ra.at[b], b)
+    gather_sent(3)
+
+    def first_inner(b):
+        links.gbs.arrived(k_.ra.at[b], b)
+        links.in0.arrived(k_.inner_in.at[b, pl.ds(1, 3)], b)
+        row = k_.inner_in[b, 0, 0:1, :]
+        for place in range(1, 4):
+            row = row + pltpu.roll(k_.inner_in[b, place], HALF * place, 1)[0:1, :]
+        return as_column(row)
 
     def first_backward(i, carry):
         b = NB - 1 - i
-        pl.when(i < 2)(lambda: turn_block(1 - i))
-        pl.when(i == 1)(lambda: reduce_first(1, k_.dw1))
-        pl.when(i == 3)(lambda: owner_slices(links.p1, k_.pb, k_.pb_in))
-        links.gbs.arrived(k_.ra.at[b], b)
-        links.in0.arrived(k_.inner0.at[pl.ds(0, 3 * HALF)], b)
-        inner = k_.inner0[span(b * L, L), :][:, 0:1]
-        backward_block(0, b, k_.gb0, inner, k_.pa)
+
+        def between():
+            def at0():
+                reduce_first(1, 0, k_.dw1)
+                turn_block(0)
+
+            def at1():
+                for j in ORDER:
+                    links.p1.start(k_.pb.at[span(x_of(j) * ROWS, ROWS)], k_.p1_in.at[j - 1], 0, x_peer(j))
+
+            pl.when(i == 0)(at0)
+            pl.when(i == 1)(at1)
+
+        backward_block(0, b, first_inner(b), k_.pa, between)
         return carry
 
-    lax.fori_loop(0, NB, first_backward, 0)
-    owner_slices(links.dn0, k_.pa, k_.pc_in)
+    lax.fori_loop(0, 2, first_backward, 0)
+    gate_block(0, 1, first_inner(1))
+    gate_block(0, 0, first_inner(0))
+    to_owner(3)
+    to_owner(2)
+    weight_grads(0, 0, k_.gb0, k_.wall1)
+
+    def last_backward(i, carry):
+        b = 1 - i
+
+        def between():
+            pl.when(i == 0)(lambda: reduce_first(0, 0, k_.wall1))
+            pl.when(i == 1)(lambda: reduce_second(1, 0, k_.dw1))
+
+        backward_block(0, b, None, k_.pa, between)
+        to_owner(b)
+        return carry
+
+    lax.fori_loop(0, 2, last_backward, 0)
     small_grads(0)
-    gather_sent(1)
-    weight_grads(0, k_.gb0, k_.wall1)
-
-    reduce_second(1, k_.dw1)
-    reduce_first(0, k_.wall1)
-    links.dn0.arrived(k_.pc_in, 0)
-    total = k_.pa[rows_t, :].astype(F32)
-    for j in (1, 2, 3):
-        total = total + k_.pc_in[j - 1].astype(F32)
-    grad, gain_grad = input_grad(0, total, k_.tok[rows_t, :].astype(F32), k_.gb0[rows_t, :].astype(F32))
-    k_.igs[0] = grad
-    k_.igs[1] = k_.gb0[rows_t, :].astype(F32)
-    for k, part in ((0, gain_grad), (1, k_.gi1[...])):
-        part = jnp.sum(part, axis=0, keepdims=True)
-        k_.pack[k, 6:7, :] = part[:, 0:CH]
-        k_.pack[k, 7:8, :] = part[:, CH:D]
     links.small.start(k_.pack.at[1 - s], k_.pack_in.at[0], 0, twin())
-    links.p1.arrived(k_.pb_in, 0)
-    total = k_.pb[rows_t, :].astype(F32)
-    for j in (1, 2, 3):
-        total = total + k_.pb_in[j - 1].astype(F32)
-    mask = row_mask(t * ROWS, ROWS)
-    factor = factor_column(1, t)
-    k_.los[0] = k_.hid[rows_t, :]
-    k_.los[1] = (mask * (k_.hid[rows_t, :].astype(F32) + factor * total)).astype(BF16)
-    links.outs.start(k_.los.at[1 - s], k_.lo.at[s], 0, twin())
-    links.outs.start(k_.igs.at[1 - s], k_.ig.at[s], 1, twin())
-    keep_lo = pltpu.make_async_copy(k_.los.at[s], k_.lo.at[s], lsem.at[2])
-    keep_ig = pltpu.make_async_copy(k_.igs.at[s], k_.ig.at[s], lsem.at[3])
-    keep_lo.start()
-    keep_ig.start()
-    reduce_last(1)
+    weight_grads(0, 1, k_.gb0, k_.wall1)
+
     links.small.arrived(k_.pack_in.at[0], 0)
     k_.run[0] = k_.pack[s] + k_.pack_in[0]
     for j in ORDER:
         links.small.start(k_.run.at[0], k_.pack_in.at[j], 1, first_peer(j))
-    reduce_second(0, k_.wall1)
+    reduce_first(0, 1, k_.wall1)
+    reduce_second(0, 0, k_.wall1)
 
     def small_step(stage, peers):
         first = 3 * stage - 2
@@ -861,18 +963,36 @@
             links.small.start(k_.run.at[stage], k_.pack_in.at[first + 2 + j], stage + 1, peers(j))
 
     small_step(1, second_peer)
-    reduce_last(0)
+    reduce_second(0, 1, k_.wall1)
+    small_step(2, x_peer)
+    reduce_last(1, 0)
+    reduce_last(0, 0)
+    links.p1.arrived(k_.p1_in, 0)
+    total = k_.pb[rows_t, :].astype(F32)
+    for j in range(3):
+        total = total + k_.p1_in[j].astype(F32)
+    mask = row_mask(t * ROWS, ROWS)
+    factor = factor_column(1, t)
+    k_.los[0] = k_.hid[rows_t, :]
+    k_.los[1] = (mask * (k_.hid[rows_t, :].astype(F32) + factor * total)).astype(BF16)
+    links.outs.start(k_.los.at[1 - s], k_.lo.at[s], 0, twin())
+    keep_lo = pltpu.make_async_copy(k_.los.at[s], k_.lo.at[s], lsem.at[2])
+    keep_lo.start()
+    links.dn0.arrived(k_.dn0_in, 0)
+    total = k_.pa[rows_t, :].astype(F32)
+    for j in range(3):
+        total = total + k_.dn0_in[j].astype(F32)
+    k_.igs[0] = input_grad(0, total, k_.tok[rows_t, :].astype(F32), k_.gb0[rows_t, :].astype(F32))
+    k_.igs[1] = k_.gb0[rows_t, :].astype(F32)
+    links.outs.start(k_.igs.at[1 - s], k_.ig.at[s], 1, twin())
+    keep_ig = pltpu.make_async_copy(k_.igs.at[s], k_.ig.at[s], lsem.at[3])
+    keep_ig.start()
+    reduce_last(0, 1)
     links.shard.start(k_.half.at[1 - s], k_.other_half, 0, twin())
-    small_step(2, x_peer)
     links.shard.arrived(k_.other_half, 0)
     mine, others = k_.half[s], k_.other_half[...]
     k_.shard_out[my_half, :] = mine
     k_.shard_out[twin_half, :] = others
-    for i in range(2):
-        k_.bcs[i, my_half, :] = mine[:, B0 + 128 * i : B0 + 128 * i + 128]
-        k_.bcs[i, twin_half, :] = others[:, B0 + 128 * i : B0 + 128 * i + 128]
-    for j in ORDER:
-        links.bcx.start(k_.bcs.at[x_of(j) // 2], k_.bcs_in.at[j], 0, x_peer(j))
     links.small.arrived(k_.pack_in.at[pl.ds(7, 3)], 3)
     over_x = k_.run[2] + k_.pack_in[7] + k_.pack_in[8] + k_.pack_in[9]
     row = iota((16, CH), 0)
@@ -883,9 +1003,6 @@
     for i in range(1, 4):
         chosen = jnp.where(t == i, over_x[8:16, 64 * i : 64 * i + 64], chosen)
     k_.small_out[9:14, 0:64] = chosen[1:6, :]
-    links.bcx.arrived(k_.bcs_in.at[pl.ds(1, 3)], 0)
-    block = k_.bcs[t // 2] + k_.bcs_in[1] + k_.bcs_in[2] + k_.bcs_in[3]
-    k_.shard_out[:, B0 : B0 + 64] = jnp.where(lax.rem(t, 2) == 0, block[:, 0:64], block[:, 64:128])
 
     keep_lo.wait()
     keep_ig.wait()
@@ -900,30 +1017,37 @@
         links.small.sent(k_.run, i)
     links.early.sent(k_.bc_in.at[pl.ds(1, 3)], 0)
     links.early.sent(k_.par_in.at[pl.ds(1, 3)], 1)
-    links.toks.sent(k_.tok.at[pl.ds(0, 3 * ROWS)], 0)
-    links.toks.sent(k_.tok.at[pl.ds(0, 3 * ROWS)], 1)
-    links.p1.sent(k_.pb_in, 0)
-    links.dn0.sent(k_.pc_in, 0)
-    links.bcx.sent(k_.bcs_in.at[pl.ds(1, 3)], 0)
-    gather_sent(0)
-
-    def shard_sent(k):
+    for a in range(2):
+        links.rows1.sent(k_.tok.at[rows_t], (a, 0))
+        links.rows1.sent(k_.tok.at[rows_t], (a, 1))
+    links.rows2.sent(k_.tok.at[pl.ds(0, ROWS)], 0)
+    links.p1.sent(k_.p1_in, 0)
+    links.dn0.sent(k_.dn0_in, 0)
+    for k in range(2):
+        links.bcx.sent(k_.first_in.at[0, 0, 0, :, pl.ds(0, 15 * 128)], k)
+    for group in range(3):
+        gather_sent(group)
+
+    def shard_sent(group):
+        cols = pl.ds(*GROUPS[group][1:])
         for i in range(3):
-            links.g_first.sent(k_.mid.at[0, pl.ds(0, 2)], (k, i))
-        links.g_first.sent(k_.mid.at[0, 0], (k, 3))
-
+            links.g_first.sent(k_.mid.at[0, pl.ds(0, 2), :, cols], (group, i))
+        links.g_first.sent(k_.mid.at[0, 0, :, cols], (group, 3))
+
+    for group in range(4):
+        pl.when(s == GROUPS[group][0])(lambda: shard_sent(group))
     for k in range(2):
-        pl.when(s == k)(lambda: shard_sent(k))
-        links.d_twin.sent(k_.theirs.at[k], k)
-        links.d_first.sent(k_.first_in.at[k], k)
-        links.d_second.sent(k_.last_in.at[k, pl.ds(1, 3)], k)
+        for part in range(len(PARTS[k])):
+            cols = pl.ds(*PARTS[k][part])
+            links.d_twin.sent(k_.theirs.at[k, :, :, cols], (k, part))
+            links.d_first.sent(k_.first_in.at[k, :, :, :, cols], (k, part))
+            links.d_second.sent(k_.last_in.at[k, pl.ds(1, 3), :, cols], (k, part))
     for b in range(NB):
         links.sq0.sent(k_.sq_in.at[0, b, pl.ds(1, 3)], b)
         links.sq1.sent(k_.sq_in.at[1, b, pl.ds(1, 3)], b)
-        links.hids.sent(k_.ra.at[b], b)
-        links.dn1.sent(k_.rb.at[b], b)
-        links.gbs.sent(k_.ra.at[b], b)
-        links.in0.sent(k_.inner0.at[pl.ds(0, 3 * HALF)], b)
+        links.in0.sent(k_.inner_in.at[b, pl.ds(1, 3)], b)
+        for link in (links.hids, links.gbs, links.dn1):
+            link.sent(k_.ra.at[b], b)
 
 
 def unpack_kernel(

time: 141 us -> 136 us (0.965)
  Pallas kernels: 140 us -> 135 us
    pallas_call x1, Pallas kernels: 137 us -> 132 us  [body(): pl.pallas_call(layer_kernel, out_shape=[sds((2, ROWS, D), BF16), sds((2,...]
where the time goes in v4:
time: 136 us
  Pallas kernels  135 us (99%)
    pallas_call x1, Pallas kernels, body(): pl.pallas_call(layer_kernel, out_shape=[sds((2, ROWS, D), BF16), sds((2,...  132 us
    pallas_call x1, Pallas kernels, body(): pl.pallas_call(unpack_kernel, out_shape=[sds(a, BF16 if i == 0 else F32)...  2.95 us

profile of v4, /device:TPU:1, one launch (start us, length us, event | category | flops | bytes accessed | tf_op | source)
XLA Modules:
  0.0 135.9 jit_solution(14850423918842037702)
XLA Ops:
  0.7 132.2 %shard_map.288 = (bf16[2,128,1024]{2,1,0:T(8,128)(2,1)}, f32[2,128,1024]{2,1,0:T(8,128)}, f32[64,1920]{1,0:T(8,128)}, f32[16,512]{1,0:T(8,128)}) custom-call(f32[1,1024]{1,0:T(1,128)} %refs_0_.1, bf16[1,64,512]{2,1,0:T(8,128)(2,1)} %refs_1_.1, bf16[1,64,512]{2,1,0:T(8,128)(2,1)} %refs_2_.1, bf16[1,64,64]{2,1,0:T(8,128)(2,1)} %refs_3_.1, ...), custom_call_target="tpu_custom_call" | custom-call | tf_op jit(solution)/shard_map/pallas_call | solution.py:1098
  132.8 2.9 %shard_map.289 = (bf16[2,128,1024]{2,1,0:T(8,128)(2,1)}, f32[2,128,1024]{2,1,0:T(8,128)}, f32[1,1024]{1,0:T(1,128)}, f32[64,512]{1,0:T(8,128)}, f32[64,512]{1,0:...) custom-call(f32[64,1920]{1,0:T(8,128)} %get-tuple-element.36.shard, ...), custom_call_target="tpu_custom_call" | custom-call | tf_op jit(solution)/shard_map/pallas_call | solution.py:1115

commit v5 on v4

--- a/solution.py
+++ b/solution.py
@@ -561,8 +561,6 @@
 
     def first_forward(b, carry):
         project_block(0, b)
-        pl.when(b == 0)(lambda: gather_second(3))
-        pl.when(b == 0)(lambda: rows_second(1, k_.gb1))
         pl.when(b >= 2)(lambda: hidden_block(b - 2))
         pl.when(b == 3)(lambda: gather_twin(3))
         forward_block(0, b)
@@ -571,6 +569,8 @@
         pl.when(b == 0)(lambda: gather_done(2))
         output_rows(0, span(b * L, L), k_.pa)
         spread_slices(links.p0, k_.pa, k_.ra, b)
+        pl.when(b == 0)(lambda: gather_second(3))
+        pl.when(b == 0)(lambda: rows_second(1, k_.gb1))
         return carry
 
     lax.fori_loop(0, NB, first_forward, 0)
@@ -742,7 +742,16 @@
         conv_back(256, 9, k_.dcbc, k_.blkbc, k_.tapbc, B0)
         for j in range(4):
             wr = slice(4 * j, 4 * j + 4)
-            d = mm(k_.dproj[rows, :], walls[k][wr, :, 0:O0].reshape(256, O0), NT)
+            if k == 1:
+                d = mm(k_.dproj[rows, 0:D], k_.dw1[:, :, 256 * j : 256 * j + 256].reshape(D, 256))
+                rest = k_.dproj[rows, D:O0]
+                if j < 3:
+                    d = d + mm(rest, k_.dw1[0:6, :, D + 256 * j : D + 256 * j + 256].reshape(O0 - D, 256))
+                else:
+                    tail_cols = (k_.dw1[0:6, :, COLS - 128 : COLS], k_.dw1[6:12, :, D : D + 128])
+                    d = d + jnp.concatenate([mm(rest, a.reshape(O0 - D, 128)) for a in tail_cols], axis=1)
+            else:
+                d = mm(k_.dproj[rows, :], walls[k][wr, :, 0:O0].reshape(256, O0), NT)
             cols = slice(256 * j, 256 * j + 256)
             dn_ref[rows, cols] = d.astype(BF16)
             k_.gi[k, :, cols] += fold(d * keep.n[rows, cols].astype(F32))
@@ -877,6 +886,16 @@
 
     reset_backward()
     k_.gi[...] = jnp.zeros((2, 8, D), F32)
+    for c in range(0, O0, 256):
+        size = min(256, O0 - c)
+        turned = weight(1, c, size).T
+        n = size // 64
+        if c < D:
+            k_.dw1[c // 64 : c // 64 + n, :, 0:D] = turned.reshape(n, 64, D)
+        else:
+            r = (c - D) // 64
+            k_.dw1[r : r + n, :, D:COLS] = turned[:, 0 : COLS - D].reshape(n, 64, COLS - D)
+            k_.dw1[6 + r : 6 + r + n, :, D : D + 128] = turned[:, COLS - D : D].reshape(n, 64, 128)
     for b in range(NB):
         tile_sum(links.sq1, 1, b)
 
@@ -911,7 +930,6 @@
         def between():
             def at0():
                 reduce_first(1, 0, k_.dw1)
-                turn_block(0)
 
             def at1():
                 for j in ORDER:
@@ -921,6 +939,7 @@
             pl.when(i == 1)(at1)
 
         backward_block(0, b, first_inner(b), k_.pa, between)
+        pl.when(i == 0)(lambda: turn_block(0))
         return carry
 
     lax.fori_loop(0, 2, first_backward, 0)

time: 136 us -> 135 us (level)
  no operation moved by 1% of the time
where the time goes in v5:
time: 135 us
  Pallas kernels  134 us (99%)
    pallas_call x1, Pallas kernels, body(): pl.pallas_call(layer_kernel, out_shape=[sds((2, ROWS, D), BF16), sds((2,...  131 us
    pallas_call x1, Pallas kernels, body(): pl.pallas_call(unpack_kernel, out_shape=[sds(a, BF16 if i == 0 else F32)...  2.95 us

profile of v5, /device:TPU:1, one launch (start us, length us, event | category | flops | bytes accessed | tf_op | source)
XLA Modules:
  0.0 134.7 jit_solution(16704995163938430760)
XLA Ops:
  0.7 131.0 %shard_map.288 = (bf16[2,128,1024]{2,1,0:T(8,128)(2,1)}, f32[2,128,1024]{2,1,0:T(8,128)}, f32[64,1920]{1,0:T(8,128)}, f32[16,512]{1,0:T(8,128)}) custom-call(f32[1,1024]{1,0:T(1,128)} %refs_0_.1, bf16[1,64,512]{2,1,0:T(8,128)(2,1)} %refs_1_.1, bf16[1,64,512]{2,1,0:T(8,128)(2,1)} %refs_2_.1, bf16[1,64,64]{2,1,0:T(8,128)(2,1)} %refs_3_.1, ...), custom_call_target="tpu_custom_call" | custom-call | tf_op jit(solution)/shard_map/pallas_call | solution.py:1117
  131.7 2.9 %shard_map.289 = (bf16[2,128,1024]{2,1,0:T(8,128)(2,1)}, f32[2,128,1024]{2,1,0:T(8,128)}, f32[1,1024]{1,0:T(1,128)}, f32[64,512]{1,0:T(8,128)}, f32[64,512]{1,0:...) custom-call(f32[64,1920]{1,0:T(8,128)} %get-tuple-element.36.shard, ...), custom_call_target="tpu_custom_call" | custom-call | tf_op jit(solution)/shard_map/pallas_call | solution.py:1134

commit v6 on v5

--- a/solution.py
+++ b/solution.py
@@ -561,8 +561,6 @@
 
     def first_forward(b, carry):
         project_block(0, b)
-        pl.when(b >= 2)(lambda: hidden_block(b - 2))
-        pl.when(b == 3)(lambda: gather_twin(3))
         forward_block(0, b)
         pl.when(b == 0)(lambda: gather_twin(2))
         spread_tile(links.sq0, 0, b)
@@ -571,6 +569,8 @@
         spread_slices(links.p0, k_.pa, k_.ra, b)
         pl.when(b == 0)(lambda: gather_second(3))
         pl.when(b == 0)(lambda: rows_second(1, k_.gb1))
+        pl.when(b >= 2)(lambda: hidden_block(b - 2))
+        pl.when(b == 3)(lambda: gather_twin(3))
         return carry
 
     lax.fori_loop(0, NB, first_forward, 0)

time: 135 us -> 134 us (level)
  no operation moved by 1% of the time
where the time goes in v6:
time: 134 us
  Pallas kernels  133 us (99%)
    pallas_call x1, Pallas kernels, body(): pl.pallas_call(layer_kernel, out_shape=[sds((2, ROWS, D), BF16), sds((2,...  130 us
    pallas_call x1, Pallas kernels, body(): pl.pallas_call(unpack_kernel, out_shape=[sds(a, BF16 if i == 0 else F32)...  2.95 us

profile of v6, /device:TPU:1, one launch (start us, length us, event | category | flops | bytes accessed | tf_op | source)
XLA Modules:
  0.0 133.7 jit_solution(3124762748654812408)
XLA Ops:
  0.7 129.9 %shard_map.288 = (bf16[2,128,1024]{2,1,0:T(8,128)(2,1)}, f32[2,128,1024]{2,1,0:T(8,128)}, f32[64,1920]{1,0:T(8,128)}, f32[16,512]{1,0:T(8,128)}) custom-call(f32[1,1024]{1,0:T(1,128)} %refs_0_.1, bf16[1,64,512]{2,1,0:T(8,128)(2,1)} %refs_1_.1, bf16[1,64,512]{2,1,0:T(8,128)(2,1)} %refs_2_.1, bf16[1,64,64]{2,1,0:T(8,128)(2,1)} %refs_3_.1, ...), custom_call_target="tpu_custom_call" | custom-call | tf_op jit(solution)/shard_map/pallas_call | solution.py:1117
  130.6 2.9 %shard_map.289 = (bf16[2,128,1024]{2,1,0:T(8,128)(2,1)}, f32[2,128,1024]{2,1,0:T(8,128)}, f32[1,1024]{1,0:T(1,128)}, f32[64,512]{1,0:T(8,128)}, f32[64,512]{1,0:...) custom-call(f32[64,1920]{1,0:T(8,128)} %get-tuple-element.36.shard, ...), custom_call_target="tpu_custom_call" | custom-call | tf_op jit(solution)/shard_map/pallas_call | solution.py:1134
